TPU v7x, 32 devices: a whole 2x2x4 slice. The times are simulated.
32 devices in a mesh: dp: 2 (over x), context: 16 (over z, y, core).
Axes of the slice: x: 2, y: 2, z: 4, core: 2. Of those that a mesh axis runs over, the one named last changes fastest.
Arguments:
- queries: bfloat16 [2, 2048, 2048], P('dp', 'context'), may hold values from -6 to 6
- key_rows: bfloat16 [2, 2048, 2048], P('dp', 'context'), may hold values from -6 to 6
- value_rows: bfloat16 [2, 2048, 2048], P('dp', 'context'), may hold values from -6 to 6
- out_grad: bfloat16 [2, 2048, 2048], P('dp', 'context'), may hold values from -6 to 6
- feature_maps: bfloat16 [16, 128, 128], replicated, may hold values from -0.5 to 0.5
Outputs:
- query_grad: bfloat16 [2, 2048, 2048], P('dp', 'context')
- key_grad: bfloat16 [2, 2048, 2048], P('dp', 'context')
- value_grad: bfloat16 [2, 2048, 2048], P('dp', 'context')
- maps_grad: float32 [2048, 128], P(('dp', 'context'))
All inputs are finite; a program needn't handle non-finite values.
Results may differ from a plain program's by a relative error of at most 0.0085.
Values sent between devices are 32-bit elements; how exact they have to be, the bound alone decides.
No kernel may reach another device: no remote copies, remote signals or barrier semaphores. Data moves between devices by JAX's collectives and lax.ppermute only.
A program may use at most 64 MiB of HBM per device.

v0:
```python
import functools
import math

import jax
import jax.numpy as jnp
from jax import lax
from jax.experimental import pallas as pl
from jax.experimental.pallas import tpu as pltpu
from jax.sharding import PartitionSpec as P

F32 = jnp.float32
BF16 = jnp.bfloat16
VMEM_LIMIT = 57 * 1024 * 1024
MIDDLE_LIMIT = 51 * 1024 * 1024
STATES_LIMIT = 53 * 1024 * 1024
SMALL_LIMIT = 16 * 1024 * 1024
LIGHT = 0.01


class Plan:
    def __init__(self, heads, width, tokens, ranks, copies):
        self.heads, self.width, self.tokens = heads, width, tokens
        self.ranks, self.copies = ranks, copies
        self.groups = ranks // 4
        per_copy = heads // copies if heads % copies == 0 else 0
        self.chunks = 2 if per_copy and per_copy % 2 == 0 and self.groups % 2 == 0 else 1
        self.in_chunk = heads // self.chunks
        self.quarter = self.in_chunk // 4
        self.run = per_copy // self.chunks if self.chunks > 1 else self.in_chunk
        self.stride = per_copy if self.chunks > 1 else 0
        self.height = heads * width // (copies * ranks)
        self.factor = 1.0 / math.sqrt(width * tokens * ranks)
        self.norm = 1.0 / math.sqrt(copies * tokens * ranks)

    def head(self, chunk, place):
        return (place // self.run) * self.stride + chunk * self.run + place % self.run


def device_place():
    index = lax.axis_index("context")
    return index % 2, (index // 2) % 2, index // 4


def dot(left, right, left_dim=1, right_dim=0):
    return lax.dot_general(
        left, right, (((left_dim,), (right_dim,)), ((), ())), preferred_element_type=F32
    )


def call(body, operands, shapes, flops, scratch, copies, aliases=None, near=(), near_out=(), limit=VMEM_LIMIT, weight=1.0):
    moved = sum(x.size * x.dtype.itemsize for x in list(operands) + list(shapes))

    def specs(count, in_vmem):
        return [
            pl.BlockSpec(memory_space=pltpu.VMEM if n in in_vmem else pltpu.HBM)
            for n in range(count)
        ]

    return pl.pallas_call(
        body,
        out_shape=shapes,
        in_specs=specs(len(operands), near),
        out_specs=specs(len(shapes), near_out),
        scratch_shapes=list(scratch) + [pltpu.SemaphoreType.DMA((copies,))],
        input_output_aliases=aliases or {},
        compiler_params=pltpu.CompilerParams(vmem_limit_bytes=limit),
        cost_estimate=pl.CostEstimate(
            flops=int(flops * weight), bytes_accessed=int(moved * weight), transcendentals=0
        ),
    )(*operands)


class Copies:
    def __init__(self, sems):
        self.sems, self.used = sems, 0

    def start(self, source, target):
        copy = pltpu.make_async_copy(source, target, self.sems.at[self.used])
        self.used += 1
        copy.start()
        return copy


def wait(copies):
    for copy in copies:
        copy.wait()


def matmuls(plan, count):
    return 2 * count * plan.tokens * plan.width * plan.width


def load_chunk(plan, copies, chunk, offset, row_refs, maps_ref, row_bufs, maps_buf):
    width, started = plan.width, []
    for first in range(0, plan.in_chunk, plan.run):
        head = plan.head(chunk, first)
        source, target = pl.ds(head, plan.run), pl.ds(offset + first, plan.run)
        started.append(copies.start(maps_ref.at[source], maps_buf.at[target]))
        source = pl.ds(head * width, plan.run * width)
        target = pl.ds((offset + first) * width, plan.run * width)
        for ref, buf in zip(row_refs, row_bufs):
            started.append(copies.start(ref.at[:, source], buf.at[:, target]))
    return started


def chunk_copies(plan):
    return 5 * (plan.in_chunk // plan.run)


def row_scratch(plan, count):
    rows = [pltpu.VMEM((plan.tokens, count * plan.width), BF16)] * 4
    return rows + [pltpu.VMEM((count, plan.width, plan.width), BF16)]


def head_of(buf, place, width):
    return buf[:, place * width : (place + 1) * width]


def quarter_of(plan, place):
    core, chip, _ = device_place()
    low = place // plan.quarter
    core_turn = 1 - core if low % 2 else core
    chip_turn = 1 - chip if low // 2 else chip
    return core_turn, chip_turn, place % plan.quarter


def states_kernel(plan, chunk, *refs):
    row_refs, maps_ref, sent_ref, kept_ref, given_ref = refs[:4], refs[4], refs[5], refs[6], refs[7]
    row_bufs, maps_buf, sems = refs[8:12], refs[12], refs[13]
    copies, width = Copies(sems), plan.width
    started = load_chunk(plan, copies, chunk, 0, row_refs, maps_ref, row_bufs, maps_buf)
    q_buf, k_buf, v_buf, g_buf = row_bufs
    size = 5 * max(1, 4 // plan.run)
    for first in range(0, plan.in_chunk, 4):
        places = range(first, first + 4)
        wait(started[:size])
        started = started[size:]
        feats_key = [dot(head_of(k_buf, n, width), maps_buf[n]).astype(BF16) for n in places]
        feats_query = [dot(head_of(q_buf, n, width), maps_buf[n]).astype(BF16) for n in places]
        key_states = [
            dot(feat, head_of(v_buf, n, width), 0, 0) for feat, n in zip(feats_key, places)
        ]
        query_states = [
            dot(feat, head_of(g_buf, n, width), 0, 0) for feat, n in zip(feats_query, places)
        ]
        for place, key_state, query_state in zip(places, key_states, query_states):
            core_turn, chip_turn, i = quarter_of(plan, place)

            @pl.when(core_turn == 1)
            def _():
                sent_ref[chip_turn, 0, i] = key_state
                sent_ref[chip_turn, 1, i] = query_state

            @pl.when(core_turn == 0)
            def _():
                kept_ref[chip_turn, 0, i] = key_state
                kept_ref[chip_turn, 1, i] = query_state
    given_ref[...] = kept_ref[1]


def block_states(plan, chunk, rows, maps):
    shape = (2, 2, plan.quarter, plan.width, plan.width)
    state = jax.ShapeDtypeStruct(shape, F32)
    return call(
        functools.partial(states_kernel, plan, chunk),
        (*rows, maps),
        [state, state, jax.ShapeDtypeStruct(shape[1:], F32)],
        matmuls(plan, 4 * plan.in_chunk),
        row_scratch(plan, plan.in_chunk),
        chunk_copies(plan),
        near_out=(0, 1, 2),
        limit=STATES_LIMIT,
    )


def causal_mask(tokens):
    row = lax.broadcasted_iota(jnp.int32, (tokens, tokens), 0)
    column = lax.broadcasted_iota(jnp.int32, (tokens, tokens), 1)
    return row >= column


def inner_kernel(plan, *refs):
    row_refs, maps_ref = refs[:4], refs[4]
    out_refs = refs[5 : 5 + 2 * plan.chunks]
    row_bufs, maps_buf = refs[-8:-4], refs[-4]
    base_buf, pair_buf, sems = refs[-3:]
    copies, width = Copies(sems), plan.width
    started = [
        load_chunk(plan, copies, chunk, chunk * plan.in_chunk, row_refs, maps_ref, row_bufs, maps_buf)
        for chunk in range(plan.chunks)
    ]
    causal = causal_mask(plan.tokens)
    written = []
    for chunk in range(plan.chunks):
        wait(started[chunk])
        for first in range(0, plan.in_chunk, 4):
            places = range(first, first + 4)
            at = [chunk * plan.in_chunk + place for place in places]
            queries, keys, values, grads = [
                [head_of(buf, n, width) for n in at] for buf in row_bufs
            ]
            scores = [
                jnp.where(causal, dot(grad, value, 1, 1), 0.0).astype(BF16)
                for grad, value in zip(grads, values)
            ]
            feats_query = [dot(x, maps_buf[n]).astype(BF16) for x, n in zip(queries, at)]
            feats_key = [dot(x, maps_buf[n]).astype(BF16) for x, n in zip(keys, at)]
            grads_a = [dot(s, feat).astype(BF16) for s, feat in zip(scores, feats_key)]
            grads_b = [dot(s, feat, 0, 0).astype(BF16) for s, feat in zip(scores, feats_query)]
            for n, place in enumerate(places):
                pair_buf[chunk, 0, place] = dot(queries[n], grads[n], 0, 0).astype(BF16)
                pair_buf[chunk, 1, place] = dot(keys[n], values[n], 0, 0).astype(BF16)
                base_buf[chunk, place] = dot(queries[n], grads_a[n], 0, 0) + dot(
                    keys[n], grads_b[n], 0, 0
                )
        written.append(copies.start(base_buf.at[chunk], out_refs[2 * chunk]))
        written.append(copies.start(pair_buf.at[chunk], out_refs[2 * chunk + 1]))
    wait(written)


def inner(plan, rows, maps):
    square = (plan.in_chunk, plan.width, plan.width)
    outs = call(
        functools.partial(inner_kernel, plan),
        (*rows, maps),
        [jax.ShapeDtypeStruct(square, F32), jax.ShapeDtypeStruct((2,) + square, BF16)]
        * plan.chunks,
        matmuls(plan, 9 * plan.heads),
        row_scratch(plan, plan.heads)
        + [
            pltpu.VMEM((plan.chunks,) + square, F32),
            pltpu.VMEM((plan.chunks, 2) + square, BF16),
        ],
        plan.chunks * (chunk_copies(plan) + 2),
    )
    return [outs[2 * chunk : 2 * chunk + 2] for chunk in range(plan.chunks)]


def finish_states(plan, state_refs, extra_buf, state_buf):
    core, _, _ = device_place()
    for core_turn in range(2):
        for chip_turn in range(2):
            for side in range(2):
                state = state_refs[2 * core_turn + chip_turn][side]
                if core_turn == 0:
                    wanted = core == 1 - side
                    state = state + jnp.where(wanted, extra_buf[chip_turn, side], 0.0)
                state_buf[core_turn, chip_turn, side] = state.astype(BF16)


def state_scratch(plan):
    shape = (2, 2, plan.quarter, plan.width, plan.width)
    return [pltpu.VMEM(shape, F32), pltpu.VMEM((2,) + shape, BF16)]


def term_kernel(plan, *refs):
    state_refs, extra_ref, base_ref, pair_ref = refs[:4], refs[4], refs[5], refs[6]
    out_refs = refs[7:-5]
    extra_buf, state_buf, base_buf, pair_buf, sems = refs[-5:]
    copies = Copies(sems)
    core, _, _ = device_place()
    extra_copy = copies.start(extra_ref, extra_buf)
    others = [copies.start(pair_ref, pair_buf), copies.start(base_ref, base_buf)]
    extra_copy.wait()
    finish_states(plan, state_refs, extra_buf, state_buf)
    wait(others)
    half = plan.width // 2
    for first in range(0, plan.in_chunk, 4):
        places = range(first, first + 4)
        where = [quarter_of(plan, place) for place in places]
        products = [
            dot(pair_buf[side, place], state_buf[c, y, side, i], 1, 1)
            for place, (c, y, i) in zip(places, where)
            for side in range(2)
        ]
        for n, place in enumerate(places):
            term = plan.factor * (base_buf[place] + products[2 * n] + products[2 * n + 1])
            if len(out_refs) == 1:
                out_refs[0][place] = term
            else:
                out_refs[0][place] = jnp.where(core == 0, term[half:], term[:half])
                out_refs[1][place] = jnp.where(core == 0, term[:half], term[half:])


def maps_term(plan, states, extra, base, pair):
    width = plan.width
    square = (plan.in_chunk, width, width)
    in_halves = 2 * plan.height == width and plan.height % 8 == 0
    shapes = [(plan.in_chunk, width // 2, width)] * 2 if in_halves else [square]
    outs = call(
        functools.partial(term_kernel, plan),
        (*states, extra, base, pair),
        [jax.ShapeDtypeStruct(shape, F32) for shape in shapes],
        matmuls(plan, 2 * plan.in_chunk),
        state_scratch(plan) + [pltpu.VMEM(square, F32), pltpu.VMEM((2,) + square, BF16)],
        3,
        near=range(4),
        near_out=range(2),
        limit=SMALL_LIMIT,
        weight=LIGHT,
    )
    if in_halves:
        return outs
    core, _, _ = device_place()
    parts = outs[0].reshape(-1, 2, plan.height, width)
    return [
        lax.dynamic_index_in_dim(parts, turn, 1, keepdims=False) for turn in (1 - core, core)
    ]


def rows_kernel(plan, chunk, *refs):
    state_refs, extra_ref, row_refs, maps_ref = refs[:4], refs[4], refs[5:9], refs[9]
    refs = refs[10 + (3 if chunk else 0) :]
    out_refs, row_bufs, maps_buf = refs[:3], refs[3:7], refs[7]
    extra_buf, state_buf, out_bufs, sems = refs[8], refs[9], refs[10:13], refs[13]
    copies, width = Copies(sems), plan.width
    extra_copy = copies.start(extra_ref, extra_buf)
    started = load_chunk(plan, copies, chunk, 0, row_refs, maps_ref, row_bufs, maps_buf)
    causal = causal_mask(plan.tokens)
    extra_copy.wait()
    finish_states(plan, state_refs, extra_buf, state_buf)
    written = []
    size = 5 * max(1, 4 // plan.run)
    for first in range(0, plan.in_chunk, 4):
        places = range(first, first + 4)
        wait(started[:size])
        started = started[size:]
        queries, keys, values, grads = [
            [head_of(buf, place, width) for place in places] for buf in row_bufs
        ]
        where = [quarter_of(plan, place) for place in places]
        prefixes = [state_buf[c, y, 0, i] for c, y, i in where]
        suffixes = [state_buf[c, y, 1, i] for c, y, i in where]
        matrices = [maps_buf[place] for place in places]
        scores_gv = [
            jnp.where(causal, dot(grad, value, 1, 1), 0.0).astype(BF16)
            for grad, value in zip(grads, values)
        ]
        feats_query = [dot(x, matrix).astype(BF16) for x, matrix in zip(queries, matrices)]
        feats_key = [dot(x, matrix).astype(BF16) for x, matrix in zip(keys, matrices)]
        scores_ab = [
            jnp.where(causal, dot(left, right, 1, 1), 0.0).astype(BF16)
            for left, right in zip(feats_query, feats_key)
        ]
        grads_a = [
            (plan.factor * (dot(score, feat) + dot(grad, prefix, 1, 1))).astype(BF16)
            for score, feat, grad, prefix in zip(scores_gv, feats_key, grads, prefixes)
        ]
        grads_b = [
            (plan.factor * (dot(score, feat, 0, 0) + dot(value, suffix, 1, 1))).astype(BF16)
            for score, feat, value, suffix in zip(scores_gv, feats_query, values, suffixes)
        ]
        for n, place in enumerate(places):
            at = slice(place * width, (place + 1) * width)
            out_bufs[0][:, at] = dot(grads_a[n], matrices[n], 1, 1).astype(BF16)
            out_bufs[1][:, at] = dot(grads_b[n], matrices[n], 1, 1).astype(BF16)
            value_grad = dot(scores_ab[n], grads[n], 0, 0) + dot(feats_key[n], suffixes[n])
            out_bufs[2][:, at] = (plan.factor * value_grad).astype(BF16)
        for part in range(first, first + 4, min(4, plan.run)):
            count = min(4, plan.run)
            source = pl.ds(part * width, count * width)
            target = pl.ds(plan.head(chunk, part) * width, count * width)
            for buf, ref in zip(out_bufs, out_refs):
                written.append(copies.start(buf.at[:, source], ref.at[:, target]))
    wait(written)


def output_rows(plan, chunk, rows, maps, states, extra, done):
    shape = jax.ShapeDtypeStruct((plan.tokens, plan.heads * plan.width), BF16)
    narrow = [pltpu.VMEM((plan.tokens, plan.in_chunk * plan.width), BF16)] * 3
    return call(
        functools.partial(rows_kernel, plan, chunk),
        (*states, extra, *rows, maps, *done),
        [shape] * 3,
        matmuls(plan, 12 * plan.in_chunk),
        row_scratch(plan, plan.in_chunk) + state_scratch(plan) + narrow,
        chunk_copies(plan) + 3 * plan.in_chunk + 1,
        {10: 0, 11: 1, 12: 2} if done else None,
        near=range(4),
        limit=MIDDLE_LIMIT,
        weight=LIGHT,
    )


def swap_core(plan, state):
    return lax.ppermute(state, "context", [(i, i ^ 1) for i in range(plan.ranks)])


def swap_chip(plan, state):
    return lax.ppermute(state, "context", [(i, i ^ 2) for i in range(plan.ranks)])


def chain_swap(plan, state, hop):
    mirror = plan.groups - 1 - hop
    steps = [(i, i ^ 1) for i in range(plan.ranks)]
    for low in range(4):
        for left in (hop, mirror - 1):
            a, b = 4 * left + low, 4 * left + 4 + low
            steps[a], steps[b] = (a, b), (b, a)
    return lax.ppermute(state, "context", steps)


def chain_split(plan, state, hop):
    mirror = plan.groups - 1 - hop
    up = [(4 * hop + low, 4 * hop + 4 + low) for low in range(4)]
    down = [(4 * mirror + low, 4 * mirror - 4 + low) for low in range(4)]
    return lax.ppermute(state[0], "context", up), lax.ppermute(state[1], "context", down)


def plane_sums(plan, halves):
    _, chip, _ = device_place()
    replica = lax.axis_index("dp")
    ranks, copies, width = plan.ranks, plan.copies, plan.width
    totals = [half.reshape(copies, -1, 2, plan.height, width) for half in halves]

    def plane_part(target_replica, target_chip):
        parts = []
        for total in totals:
            some = lax.dynamic_index_in_dim(total, target_replica, 0, keepdims=False)
            parts.append(lax.dynamic_index_in_dim(some, target_chip, 1, keepdims=False))
        return jnp.concatenate(parts, axis=0)

    plane = plane_part(replica, chip)
    for turn in range(copies):
        for flip in range(2):
            if turn == 0 and flip == 0:
                continue
            steps = [
                (r * ranks + i, ((r + turn) % copies) * ranks + (i ^ (2 * flip)))
                for r in range(copies)
                for i in range(ranks)
            ]
            sent = plane_part((replica + turn) % copies, (chip + flip) % 2)
            plane = plane + lax.ppermute(sent, ("dp", "context"), steps)
    return plane


def group_sum(plan, plane):
    _, _, group = device_place()
    result = lax.dynamic_index_in_dim(plane, group, 0, keepdims=False)
    for turn in range(1, plan.groups):
        steps = [(i, (i + 4 * turn) % plan.ranks) for i in range(plan.ranks)]
        sent = lax.dynamic_index_in_dim(plane, (group + turn) % plan.groups, 0, keepdims=False)
        result = result + lax.ppermute(sent, "context", steps)
    return result


def select_group(plan, got):
    _, _, group = device_place()
    prefix = suffix = jnp.zeros_like(got[0])
    for hop, state in enumerate(got):
        prefix = jnp.where(group == hop + 1, state, prefix)
        suffix = jnp.where(group == plan.groups - 2 - hop, state, suffix)
    return jnp.stack([prefix, suffix])


def scan_alone(plan, group_state):
    before = jnp.zeros_like(group_state)
    for hop in range(plan.groups - 1):
        if plan.groups % 2:
            up, down = chain_split(plan, before + group_state, hop)
            before = before + jnp.stack([up, down])
    return before


def per_device(queries, key_rows, value_rows, out_grad, maps):
    tokens = queries.shape[1]
    heads, width, _ = maps.shape
    plan = Plan(heads, width, tokens, lax.axis_size("context"), lax.axis_size("dp"))
    rows = [x.reshape(tokens, heads * width) for x in (queries, key_rows, value_rows, out_grad)]
    core, chip, group = device_place()
    side = jnp.arange(2).reshape(2, 1, 1, 1)
    chunks, hops, tie = range(plan.chunks), plan.groups - 1, lax.optimization_barrier

    kept, from_core, total, from_chip, group_state = [], [], [], [], []
    for chunk in chunks:
        sent, kept_here, given = block_states(plan, chunk, rows, maps)
        kept.append(kept_here)
        from_core.append(swap_core(plan, sent))
        given = given + from_core[chunk][1]
        if chunk == plan.chunks - 1:
            terms = inner(plan, rows, maps)
        if chunk:
            given, terms = tie((given, terms))
        total.append(kept_here[0] + from_core[chunk][0])
        from_chip.append(swap_chip(plan, given))
        group_state.append(total[chunk] + from_chip[chunk])

    def for_other_chip(chunk, before):
        return before + jnp.where(side == chip, total[chunk], 0.0)

    before, got, down = [None] * plan.chunks, [[] for _ in chunks], [None] * plan.chunks
    if plan.groups % 2:
        for chunk in chunks:
            before[chunk] = scan_alone(plan, group_state[chunk])
            down[chunk] = swap_chip(plan, for_other_chip(chunk, before[chunk]))
    else:
        for stage in range(hops + plan.chunks - 1):
            for chunk in chunks:
                hop = stage - chunk
                if not 0 <= hop < hops:
                    continue
                send = jnp.where(group == hop, group_state[chunk][0], group_state[chunk][1])
                if hop:
                    send = send + got[chunk][-1]
                if chunk and hop < hops - 1:
                    send, got[0][hop] = tie((send, got[0][hop]))
                if chunk and hop == hops - 1:
                    before[0] = select_group(plan, got[0])
                    mate = for_other_chip(0, before[0])
                    send, mate = tie((send, mate))
                    down[0] = swap_chip(plan, mate)
                got[chunk].append(chain_swap(plan, send, hop))
        last = plan.chunks - 1
        if last:
            got[last][-1], down[0] = tie((got[last][-1], down[0]))
        before[last] = select_group(plan, got[last])
        down[last] = swap_chip(plan, for_other_chip(last, before[last]))

    halves, done = [], ()
    for chunk in chunks:
        states = [before[chunk] + jnp.where(side != chip, from_chip[chunk], 0.0), down[chunk]]
        for turn in range(2):
            if turn and done:
                states[1], states[2], done = tie((states[1], states[2], done))
            mine = jnp.where(side == core, kept[chunk][turn], 0.0)
            states.append(swap_core(plan, states[turn] + mine))
        if halves:
            states[3], halves = tie((states[3], halves))
        for_mate, own = maps_term(plan, states, from_core[chunk], *terms[chunk])
        halves.append(own + swap_core(plan, for_mate))
        done = output_rows(plan, chunk, rows, maps, states, from_core[chunk], done)
    plane = plane_sums(plan, halves)
    plane, done = tie((plane, done))
    query_grad, key_grad, value_grad = done
    maps_grad = group_sum(plan, plane) * plan.norm
    return (query_grad[None], key_grad[None], value_grad[None], maps_grad)


def solution(mesh):
    in_specs = (
        P("dp", "context", None),
        P("dp", "context", None),
        P("dp", "context", None),
        P("dp", "context", None),
        P(),
    )
    out_specs = (
        P("dp", "context", None),
        P("dp", "context", None),
        P("dp", "context", None),
        P(("dp", "context"), None),
    )
    return jax.shard_map(
        per_device, mesh=mesh, in_specs=in_specs, out_specs=out_specs, check_vma=False
    )
```

profile of v0, /device:TPU:0, one launch (start us, length us, event | category | flops | bytes accessed | tf_op | source)
XLA Modules:
  0.0 75.7 jit_solution(10633144896547579624)
XLA Ops:
  0.6 3.0 %shard_map.86 = (f32[2,2,2,128,128]{4,3,2,1,0:T(8,128)S(1)}, f32[2,2,2,128,128]{4,3,2,1,0:T(8,128)}, f32[2,2,128,128]{3,2,1,0:T(8,128)S(1)}) custom-call(bf16[128,2048]{1,0:T(8,128)(2,1)} %bitcast.109, bf16[128,2048]{1,0:T(8,128)(2,1)} %bitcast.114, bf16[128,2048]{1,0:T(8,128)(2,1)} %bitcast.119, bf16[128,2048]{1,0:T(8,128)(2,1)} %bitcast.124, ...), custom_call_target="tpu_custom_call" | custom-call | flops 134217728 | bytes 3932160 | tf_op jit(solution)/shard_map/pallas_call | solution.py:59
  4.1 3.0 %shard_map.84 = (f32[2,2,2,128,128]{4,3,2,1,0:T(8,128)S(1)}, f32[2,2,2,128,128]{4,3,2,1,0:T(8,128)}, f32[2,2,128,128]{3,2,1,0:T(8,128)S(1)}) custom-call(bf16[128,2048]{1,0:T(8,128)(2,1)} %bitcast.110, bf16[128,2048]{1,0:T(8,128)(2,1)} %bitcast.115, bf16[128,2048]{1,0:T(8,128)(2,1)} %bitcast.120, bf16[128,2048]{1,0:T(8,128)(2,1)} %bitcast.125, ...), custom_call_target="tpu_custom_call" | custom-call | flops 134217728 | bytes 3932160 | tf_op jit(solution)/shard_map/pallas_call | solution.py:59
  7.3 3.0 %collective-permute-start.3 = (f32[2,2,128,128]{3,2,1,0:T(8,128)S(1)}, f32[2,2,128,128]{3,2,1,0:T(8,128)S(1)}, u32[]{:S(2)}, u32[]{:S(2)}) collective-permute-start(f32[2,2,128,128]{3,2,1,0:T(8,128)S(1)} %fusion), channel_id=1, source_target_pairs={{0,2},{1,3},{2,0},{3,1},{4,6},{5,7},{6,4},{7,5},{8,10},{9,11},{10,... | collective-permute-start | bytes 786440 | tf_op jit(solution)/shard_map/ppermute | solution.py:390
  10.3 5.1 %shard_map.85 = (f32[8,128,128]{2,1,0:T(8,128)}, bf16[2,8,128,128]{3,2,1,0:T(8,128)(2,1)}, f32[8,128,128]{2,1,0:T(8,128)}, bf16[2,8,128,128]{3,2,1,0:T(8,128)(2,1)}) custom-call(bf16[128,2048]{1,0:T(8,128)(2,1)} %bitcast.111, bf16[128,2048]{1,0:T(8,128)(2,1)} %bitcast.116, bf16[128,2048]{1,0:T(8,128)(2,1)} %bitcast.121, bf16[128,2048]{1,0:T(8,128)(2,1)} %bitcast.126, ...), custom_call_target="tpu_custom_call" | custom-call | flops 603979776 | bytes 4718592 | tf_op jit(solution)/shard_map/pallas_call | solution.py:59
  15.6 1.3 %collective-permute-done.3 = f32[2,2,128,128]{3,2,1,0:T(8,128)S(1)} collective-permute-done((f32[2,2,128,128]{3,2,1,0:T(8,128)S(1)}, f32[2,2,128,128]{3,2,1,0:T(8,128)S(1)}, u32[]{:S(2)}, u32[]{:S(2)}) %collective-permute-start.3) | collective-permute-done | bytes 262176 | tf_op jit(solution)/shard_map/ppermute | solution.py:390
  16.9 1.9 %collective-permute-start.4 = (f32[2,128,128]{2,1,0:T(8,128)S(1)}, f32[2,128,128]{2,1,0:T(8,128)S(1)}, u32[]{:S(2)}, u32[]{:S(2)}) collective-permute-start(f32[2,128,128]{2,1,0:T(8,128)S(1)} %select_bitcast_fusion.4), channel_id=1, source_target_pairs={{0,4},{1,5},{2,6},{3,7},{4,0},{5,1},{6,2},{7,3},{8,12},{9,13},{10,... | collective-permute-start | bytes 393224 | tf_op jit(solution)/shard_map/ppermute | solution.py:400
  18.8 4.8 %collective-permute-done.1 = f32[2,2,128,128]{3,2,1,0:T(8,128)S(1)} collective-permute-done((f32[2,2,128,128]{3,2,1,0:T(8,128)S(1)}, f32[2,2,128,128]{3,2,1,0:T(8,128)S(1)}, u32[]{:S(2)}, u32[]{:S(2)}) %collective-permute-start.1) | collective-permute-done | bytes 262176 | tf_op jit(solution)/shard_map/ppermute | solution.py:390
  23.7 1.6 %collective-permute-start.5 = (f32[2,128,128]{2,1,0:T(8,128)S(1)}, f32[2,128,128]{2,1,0:T(8,128)S(1)}, u32[]{:S(2)}, u32[]{:S(2)}) collective-permute-start(f32[2,128,128]{2,1,0:T(8,128)S(1)} %select_bitcast_fusion.5), channel_id=1, source_target_pairs={{0,4},{1,5},{2,6},{3,7},{4,0},{5,1},{6,2},{7,3},{8,12},{9,13},{10,... | collective-permute-start | bytes 393224 | tf_op jit(solution)/shard_map/ppermute | solution.py:400
  25.4 3.3 %collective-permute-done.5 = f32[2,128,128]{2,1,0:T(8,128)S(1)} collective-permute-done((f32[2,128,128]{2,1,0:T(8,128)S(1)}, f32[2,128,128]{2,1,0:T(8,128)S(1)}, u32[]{:S(2)}, u32[]{:S(2)}) %collective-permute-start.5) | collective-permute-done | bytes 131104 | tf_op jit(solution)/shard_map/ppermute | solution.py:400
  28.8 4.8 %collective-permute-start.8 = (f32[2,128,128]{2,1,0:T(8,128)S(1)}, f32[2,128,128]{2,1,0:T(8,128)S(1)}, u32[]{:S(2)}, u32[]{:S(2)}) collective-permute-start(f32[2,128,128]{2,1,0:T(8,128)S(1)} %bitcast_add_fusion), channel_id=1, source_target_pairs={{0,4},{1,5},{2,6},{3,7},{4,0},{5,1},{6,2},{7,3},{8,12},{9,13},{10,... | collective-permute-start | bytes 393224 | tf_op jit(solution)/shard_map/ppermute | solution.py:400
  33.6 2.9 %collective-permute-done.8 = f32[2,128,128]{2,1,0:T(8,128)S(1)} collective-permute-done((f32[2,128,128]{2,1,0:T(8,128)S(1)}, f32[2,128,128]{2,1,0:T(8,128)S(1)}, u32[]{:S(2)}, u32[]{:S(2)}) %collective-permute-start.8) | collective-permute-done | bytes 131104 | tf_op jit(solution)/shard_map/ppermute | solution.py:400
  36.7 0.7 collective-permute-start.10
  37.4 2.0 %collective-permute-start.9 = (f32[2,128,128]{2,1,0:T(8,128)S(1)}, f32[2,128,128]{2,1,0:T(8,128)S(1)}, u32[]{:S(2)}, u32[]{:S(2)}) collective-permute-start(f32[2,128,128]{2,1,0:T(8,128)S(1)} %bitcast_add_fusion.3), channel_id=1, source_target_pairs={{0,4},{1,5},{2,6},{3,7},{4,0},{5,1},{6,2},{7,3},{8,12},{9,13},{10,... | collective-permute-start | bytes 393224 | tf_op jit(solution)/shard_map/ppermute | solution.py:400
  39.5 2.9 %collective-permute-done.9 = f32[2,128,128]{2,1,0:T(8,128)S(1)} collective-permute-done((f32[2,128,128]{2,1,0:T(8,128)S(1)}, f32[2,128,128]{2,1,0:T(8,128)S(1)}, u32[]{:S(2)}, u32[]{:S(2)}) %collective-permute-start.9) | collective-permute-done | bytes 131104 | tf_op jit(solution)/shard_map/ppermute | solution.py:400
  42.4 0.8 collective-permute-done.10.refs_1_
  43.5 0.7 collective-permute-start.11
  45.0 0.7 shard_map.88
  46.2 4.2 %shard_map.87 = (bf16[128,2048]{1,0:T(8,128)(2,1)}, bf16[128,2048]{1,0:T(8,128)(2,1)}, bf16[128,2048]{1,0:T(8,128)(2,1)}) custom-call(f32[2,2,128,128]{3,2,1,0:T(8,128)S(1)} %get-tuple-element.93.refs_0_, f32[2,2,128,128]{3,2,1,0:T(8,128)S(1)} %collective-permute-done.10.refs_1_, f32[2,2,128,128]{3,2,1,0:T(8,128)S(1)} %collective-permute-done.13.refs_2_, ...), custom_call_target="tpu_custom_call" | custom-call | flops 4026531 | bytes 57671 | tf_op jit(solution)/shard_map/pallas_call | solution.py:59
  50.4 1.8 %collective-permute-done.11.refs_1_ = f32[2,2,128,128]{3,2,1,0:T(8,128)S(1)} collective-permute-done((f32[2,2,128,128]{3,2,1,0:T(8,128)S(1)}, f32[2,2,128,128]{3,2,1,0:T(8,128)S(1)}, u32[]{:S(2)}, u32[]{:S(2)}) %collective-permute-start.11) | collective-permute-done | bytes 262176 | tf_op jit(solution)/shard_map/ppermute | solution.py:390
  52.4 1.5 %collective-permute-done.15.refs_3_ = f32[2,2,128,128]{3,2,1,0:T(8,128)S(1)} collective-permute-done((f32[2,2,128,128]{3,2,1,0:T(8,128)S(1)}, f32[2,2,128,128]{3,2,1,0:T(8,128)S(1)}, u32[]{:S(2)}, u32[]{:S(2)}) %collective-permute-start.15) | collective-permute-done | bytes 262176 | tf_op jit(solution)/shard_map/ppermute | solution.py:386
  53.9 0.7 shard_map.89
  54.8 1.5 %collective-permute-done.17 = f32[8,64,128]{2,1,0:T(8,128)} collective-permute-done((f32[8,64,128]{2,1,0:T(8,128)S(1)}, f32[8,64,128]{2,1,0:T(8,128)}, u32[]{:S(2)}, u32[]{:S(2)}) %collective-permute-start.17) | collective-permute-done | bytes 262176 | tf_op jit(solution)/shard_map/ppermute | solution.py:386
  56.4 1.0 %add.234 = f32[8,64,128]{2,1,0:T(8,128)S(1)} add(f32[8,64,128]{2,1,0:T(8,128)S(1)} %get-tuple-element.80, f32[8,64,128]{2,1,0:T(8,128)} %collective-permute-done.17) | non-fusion elementwise | flops 65536 | bytes 786432 | tf_op jit(solution)/shard_map/add | solution.py:531
  58.1 1.6 %collective-permute-start.19 = (f32[4,64,128]{2,1,0:T(8,128)S(1)}, f32[4,64,128]{2,1,0:T(8,128)S(1)}, u32[]{:S(2)}, u32[]{:S(2)}) collective-permute-start(f32[4,64,128]{2,1,0:T(8,128)S(1)} %pad_maximum_fusion.3), channel_id=1, source_target_pairs={{0,16},{1,17},{2,18},{3,19},{4,20},{5,21},{6,22},{7,23},{8,24},{9,... | collective-permute-start | bytes 393224 | tf_op jit(solution)/shard_map/ppermute | solution.py:434
  60.3 1.4 %collective-permute-start.20 = (f32[4,64,128]{2,1,0:T(8,128)}, f32[4,64,128]{2,1,0:T(8,128)S(1)}, u32[]{:S(2)}, u32[]{:S(2)}) collective-permute-start(f32[4,64,128]{2,1,0:T(8,128)} %pad_maximum_fusion.4), channel_id=1, source_target_pairs={{0,18},{1,19},{2,16},{3,17},{4,22},{5,23},{6,20},{7,21},{8,26},{9,... | collective-permute-start | bytes 393224 | tf_op jit(solution)/shard_map/ppermute | solution.py:434
  61.7 4.2 %shard_map.90 = (bf16[128,2048]{1,0:T(8,128)(2,1)}, bf16[128,2048]{1,0:T(8,128)(2,1)}, bf16[128,2048]{1,0:T(8,128)(2,1)}) custom-call(f32[2,2,128,128]{3,2,1,0:T(8,128)S(1)} %get-tuple-element.95.refs_0_, f32[2,2,128,128]{3,2,1,0:T(8,128)S(1)} %collective-permute-done.11.refs_1_, ...), custom_call_target="tpu_custom_call", output_to_operand_aliasing={{0}: (10, {}), {1}: (11, {}), {2}: (12, {})} | custom-call | flops 4026531 | bytes 73400 | tf_op jit(solution)/shard_map/pallas_call | solution.py:59
  65.9 1.2 %collective-permute-done.20 = f32[4,64,128]{2,1,0:T(8,128)S(1)} collective-permute-done((f32[4,64,128]{2,1,0:T(8,128)}, f32[4,64,128]{2,1,0:T(8,128)S(1)}, u32[]{:S(2)}, u32[]{:S(2)}) %collective-permute-start.20) | collective-permute-done | bytes 131104 | tf_op jit(solution)/shard_map/ppermute | solution.py:434
  67.1 2.1 %collective-permute-start.21 = (f32[64,128]{1,0:T(8,128)S(1)}, f32[64,128]{1,0:T(8,128)S(1)}, u32[]{:S(2)}, u32[]{:S(2)}) collective-permute-start(f32[64,128]{1,0:T(8,128)S(1)} %get-tuple-element.110), channel_id=1, source_target_pairs={{0,4},{1,5},{2,6},{3,7},{4,8},{5,9},{6,10},{7,11},{8,12},{9,13},{1... | collective-permute-start | bytes 98312 | tf_op jit(solution)/shard_map/ppermute | solution.py:444
  69.2 1.9 %collective-permute-start.22 = (f32[64,128]{1,0:T(8,128)S(1)}, f32[64,128]{1,0:T(8,128)S(1)}, u32[]{:S(2)}, u32[]{:S(2)}) collective-permute-start(f32[64,128]{1,0:T(8,128)S(1)} %get-tuple-element.112), channel_id=1, source_target_pairs={{0,8},{1,9},{2,10},{3,11},{4,12},{5,13},{6,14},{7,15},{8,0},{9,1},... | collective-permute-start | bytes 98312 | tf_op jit(solution)/shard_map/ppermute | solution.py:444
  71.6 1.4 %collective-permute-done.21 = f32[64,128]{1,0:T(8,128)S(1)} collective-permute-done((f32[64,128]{1,0:T(8,128)S(1)}, f32[64,128]{1,0:T(8,128)S(1)}, u32[]{:S(2)}, u32[]{:S(2)}) %collective-permute-start.21) | collective-permute-done | bytes 32800 | tf_op jit(solution)/shard_map/ppermute | solution.py:444
  73.0 1.0 %collective-permute-done.22 = f32[64,128]{1,0:T(8,128)S(1)} collective-permute-done((f32[64,128]{1,0:T(8,128)S(1)}, f32[64,128]{1,0:T(8,128)S(1)}, u32[]{:S(2)}, u32[]{:S(2)}) %collective-permute-start.22) | collective-permute-done | bytes 32800 | tf_op jit(solution)/shard_map/ppermute | solution.py:444
  74.0 1.0 %collective-permute-done.23 = f32[64,128]{1,0:T(8,128)S(1)} collective-permute-done((f32[64,128]{1,0:T(8,128)S(1)}, f32[64,128]{1,0:T(8,128)S(1)}, u32[]{:S(2)}, u32[]{:S(2)}) %collective-permute-start.23) | collective-permute-done | bytes 32800 | tf_op jit(solution)/shard_map/ppermute | solution.py:444
  (66 shorter events, 5.9 us)
Async XLA Ops:
  3.6 3.6 %collective-permute-start.2 = (f32[2,2,2,128,128]{4,3,2,1,0:T(8,128)S(1)}, f32[2,2,2,128,128]{4,3,2,1,0:T(8,128)S(1)}, u32[]{:S(2)}, u32[]{:S(2)}) collective-permute-start(f32[2,2,2,128,128]{4,3,2,1,0:T(8,128)S(1)} %get-tuple-element.57), channel_id=1, source_target_pairs={{0,1},{1,0},{2,3},{3,2},{4,5},{5,4},{6,7},{7,6},{8,9},{9,8},{10,11... | collective-permute-start | bytes 1572872 | tf_op jit(solution)/shard_map/ppermute | solution.py:386
  7.1 8.4 %collective-permute-start = (f32[2,2,2,128,128]{4,3,2,1,0:T(8,128)S(1)}, f32[2,2,2,128,128]{4,3,2,1,0:T(8,128)S(1)}, u32[]{:S(2)}, u32[]{:S(2)}) collective-permute-start(f32[2,2,2,128,128]{4,3,2,1,0:T(8,128)S(1)} %get-tuple-element.49), channel_id=1, source_target_pairs={{0,1},{1,0},{2,3},{3,2},{4,5},{5,4},{6,7},{7,6},{8,9},{9,8},{10,11... | collective-permute-start | bytes 1572872 | tf_op jit(solution)/shard_map/ppermute | solution.py:386
  7.3 9.6 %collective-permute-start.3 = (f32[2,2,128,128]{3,2,1,0:T(8,128)S(1)}, f32[2,2,128,128]{3,2,1,0:T(8,128)S(1)}, u32[]{:S(2)}, u32[]{:S(2)}) collective-permute-start(f32[2,2,128,128]{3,2,1,0:T(8,128)S(1)} %fusion), channel_id=1, source_target_pairs={{0,2},{1,3},{2,0},{3,1},{4,6},{5,7},{6,4},{7,5},{8,10},{9,11},{10,... | collective-permute-start | bytes 786440 | tf_op jit(solution)/shard_map/ppermute | solution.py:390
  15.4 1.4 %copy-start.7 = (f32[2,2,2,128,128]{4,3,2,1,0:T(8,128)S(1)}, f32[2,2,2,128,128]{4,3,2,1,0:T(8,128)}, u32[]{:S(2)}) copy-start(f32[2,2,2,128,128]{4,3,2,1,0:T(8,128)} %get-tuple-element.56) | copy-start | bytes 1572868
  15.5 8.1 %collective-permute-start.1 = (f32[2,2,128,128]{3,2,1,0:T(8,128)S(1)}, f32[2,2,128,128]{3,2,1,0:T(8,128)S(1)}, u32[]{:S(2)}, u32[]{:S(2)}) collective-permute-start(f32[2,2,128,128]{3,2,1,0:T(8,128)S(1)} %fusion.2), channel_id=1, source_target_pairs={{0,2},{1,3},{2,0},{3,1},{4,6},{5,7},{6,4},{7,5},{8,10},{9,11},{10,... | collective-permute-start | bytes 786440 | tf_op jit(solution)/shard_map/ppermute | solution.py:390
  16.9 6.7 %copy-start.6 = (f32[2,2,2,128,128]{4,3,2,1,0:T(8,128)S(1)}, f32[2,2,2,128,128]{4,3,2,1,0:T(8,128)}, u32[]{:S(2)}) copy-start(f32[2,2,2,128,128]{4,3,2,1,0:T(8,128)} %get-tuple-element.48) | copy-start | bytes 1572868
  16.9 6.7 %collective-permute-start.4 = (f32[2,128,128]{2,1,0:T(8,128)S(1)}, f32[2,128,128]{2,1,0:T(8,128)S(1)}, u32[]{:S(2)}, u32[]{:S(2)}) collective-permute-start(f32[2,128,128]{2,1,0:T(8,128)S(1)} %select_bitcast_fusion.4), channel_id=1, source_target_pairs={{0,4},{1,5},{2,6},{3,7},{4,0},{5,1},{6,2},{7,3},{8,12},{9,13},{10,... | collective-permute-start | bytes 393224 | tf_op jit(solution)/shard_map/ppermute | solution.py:400
  23.7 5.0 %collective-permute-start.5 = (f32[2,128,128]{2,1,0:T(8,128)S(1)}, f32[2,128,128]{2,1,0:T(8,128)S(1)}, u32[]{:S(2)}, u32[]{:S(2)}) collective-permute-start(f32[2,128,128]{2,1,0:T(8,128)S(1)} %select_bitcast_fusion.5), channel_id=1, source_target_pairs={{0,4},{1,5},{2,6},{3,7},{4,0},{5,1},{6,2},{7,3},{8,12},{9,13},{10,... | collective-permute-start | bytes 393224 | tf_op jit(solution)/shard_map/ppermute | solution.py:400
  25.3 3.4 %collective-permute-start.6 = (f32[2,128,128]{2,1,0:T(8,128)S(1)}, f32[2,128,128]{2,1,0:T(8,128)S(1)}, u32[]{:S(2)}, u32[]{:S(2)}) collective-permute-start(f32[2,128,128]{2,1,0:T(8,128)S(1)} %bitcast_add_fusion.1), channel_id=1, source_target_pairs={{0,1},{1,0},{2,3},{3,2},{4,8},{5,9},{6,10},{7,11},{8,4},{9,5},{10,... | collective-permute-start | bytes 393224 | tf_op jit(solution)/shard_map/ppermute | solution.py:400
  28.7 4.9 %collective-permute-start.7 = (f32[2,128,128]{2,1,0:T(8,128)S(1)}, f32[2,128,128]{2,1,0:T(8,128)S(1)}, u32[]{:S(2)}, u32[]{:S(2)}) collective-permute-start(f32[2,128,128]{2,1,0:T(8,128)S(1)} %bitcast_add_fusion.2), channel_id=1, source_target_pairs={{0,1},{1,0},{2,3},{3,2},{4,8},{5,9},{6,10},{7,11},{8,4},{9,5},{10,... | collective-permute-start | bytes 393224 | tf_op jit(solution)/shard_map/ppermute | solution.py:400
  28.8 7.7 %collective-permute-start.8 = (f32[2,128,128]{2,1,0:T(8,128)S(1)}, f32[2,128,128]{2,1,0:T(8,128)S(1)}, u32[]{:S(2)}, u32[]{:S(2)}) collective-permute-start(f32[2,128,128]{2,1,0:T(8,128)S(1)} %bitcast_add_fusion), channel_id=1, source_target_pairs={{0,4},{1,5},{2,6},{3,7},{4,0},{5,1},{6,2},{7,3},{8,12},{9,13},{10,... | collective-permute-start | bytes 393224 | tf_op jit(solution)/shard_map/ppermute | solution.py:400
  36.7 6.4 %collective-permute-start.10 = (f32[2,2,128,128]{3,2,1,0:T(8,128)S(1)}, f32[2,2,128,128]{3,2,1,0:T(8,128)S(1)}, u32[]{:S(2)}, u32[]{:S(2)}) collective-permute-start(f32[2,2,128,128]{3,2,1,0:T(8,128)S(1)} %get-tuple-element.64), channel_id=1, source_target_pairs={{0,2},{1,3},{2,0},{3,1},{4,6},{5,7},{6,4},{7,5},{8,10},{9,11},{10,... | collective-permute-start | bytes 786440 | tf_op jit(solution)/shard_map/ppermute | solution.py:390
  37.4 5.0 %collective-permute-start.9 = (f32[2,128,128]{2,1,0:T(8,128)S(1)}, f32[2,128,128]{2,1,0:T(8,128)S(1)}, u32[]{:S(2)}, u32[]{:S(2)}) collective-permute-start(f32[2,128,128]{2,1,0:T(8,128)S(1)} %bitcast_add_fusion.3), channel_id=1, source_target_pairs={{0,4},{1,5},{2,6},{3,7},{4,0},{5,1},{6,2},{7,3},{8,12},{9,13},{10,... | collective-permute-start | bytes 393224 | tf_op jit(solution)/shard_map/ppermute | solution.py:400
  39.5 4.9 %collective-permute-start.13 = (f32[2,2,128,128]{3,2,1,0:T(8,128)S(1)}, f32[2,2,128,128]{3,2,1,0:T(8,128)S(1)}, u32[]{:S(2)}, u32[]{:S(2)}) collective-permute-start(f32[2,2,128,128]{3,2,1,0:T(8,128)S(1)} %get-tuple-element.92), channel_id=1, source_target_pairs={{0,1},{1,0},{2,3},{3,2},{4,5},{5,4},{6,7},{7,6},{8,9},{9,8},{10,11... | collective-permute-start | bytes 786440 | tf_op jit(solution)/shard_map/ppermute | solution.py:386
  43.2 1.8 %copy-start.4 = (f32[8,128,128]{2,1,0:T(8,128)S(1)}, f32[8,128,128]{2,1,0:T(8,128)}, u32[]{:S(2)}) copy-start(f32[8,128,128]{2,1,0:T(8,128)} %get-tuple-element.71.refs_5_) | copy-start | bytes 1572868
  43.2 1.8 %copy-start.5 = (bf16[2,8,128,128]{3,2,1,0:T(8,128)(2,1)S(1)}, bf16[2,8,128,128]{3,2,1,0:T(8,128)(2,1)}, u32[]{:S(2)}) copy-start(bf16[2,8,128,128]{3,2,1,0:T(8,128)(2,1)} %get-tuple-element.72.refs_6_) | copy-start | bytes 1572868
  43.4 1.6 %collective-permute-start.14 = (f32[2,2,128,128]{3,2,1,0:T(8,128)S(1)}, f32[2,2,128,128]{3,2,1,0:T(8,128)S(1)}, u32[]{:S(2)}, u32[]{:S(2)}) collective-permute-start(f32[2,2,128,128]{3,2,1,0:T(8,128)S(1)} %get-tuple-element.113), channel_id=1, source_target_pairs={{0,1},{1,0},{2,3},{3,2},{4,5},{5,4},{6,7},{7,6},{8,9},{9,8},{10,11... | collective-permute-start | bytes 786440 | tf_op jit(solution)/shard_map/ppermute | solution.py:386
  43.5 8.7 %collective-permute-start.11 = (f32[2,2,128,128]{3,2,1,0:T(8,128)S(1)}, f32[2,2,128,128]{3,2,1,0:T(8,128)S(1)}, u32[]{:S(2)}, u32[]{:S(2)}) collective-permute-start(f32[2,2,128,128]{3,2,1,0:T(8,128)S(1)} %get-tuple-element.97), channel_id=1, source_target_pairs={{0,2},{1,3},{2,0},{3,1},{4,6},{5,7},{6,4},{7,5},{8,10},{9,11},{10,... | collective-permute-start | bytes 786440 | tf_op jit(solution)/shard_map/ppermute | solution.py:390
  44.2 8.0 %collective-permute-start.12 = (f32[2,2,128,128]{3,2,1,0:T(8,128)S(1)}, f32[2,2,128,128]{3,2,1,0:T(8,128)S(1)}, u32[]{:S(2)}, u32[]{:S(2)}) collective-permute-start(f32[2,2,128,128]{3,2,1,0:T(8,128)S(1)} %get-tuple-element.94), channel_id=1, source_target_pairs={{0,1},{1,0},{2,3},{3,2},{4,5},{5,4},{6,7},{7,6},{8,9},{9,8},{10,11... | collective-permute-start | bytes 786440 | tf_op jit(solution)/shard_map/ppermute | solution.py:386
  45.0 1.0 %copy-start = (bf16[1,128,2048]{2,1,0:T(8,128)(2,1)S(1)}, bf16[1,128,2048]{2,1,0:T(8,128)(2,1)}, u32[]{:S(2)}) copy-start(bf16[1,128,2048]{2,1,0:T(8,128)(2,1)} %param.5) | copy-start | bytes 1572868
  45.0 1.2 %copy-start.1 = (bf16[1,128,2048]{2,1,0:T(8,128)(2,1)S(1)}, bf16[1,128,2048]{2,1,0:T(8,128)(2,1)}, u32[]{:S(2)}) copy-start(bf16[1,128,2048]{2,1,0:T(8,128)(2,1)} %param.6) | copy-start | bytes 1572868
  45.7 6.7 %collective-permute-start.16 = (f32[8,64,128]{2,1,0:T(8,128)S(1)}, f32[8,64,128]{2,1,0:T(8,128)S(1)}, u32[]{:S(2)}, u32[]{:S(2)}) collective-permute-start(f32[8,64,128]{2,1,0:T(8,128)S(1)} %get-tuple-element.74), channel_id=1, source_target_pairs={{0,1},{1,0},{2,3},{3,2},{4,5},{5,4},{6,7},{7,6},{8,9},{9,8},{10,11... | collective-permute-start | bytes 786440 | tf_op jit(solution)/shard_map/ppermute | solution.py:386
  52.2 1.7 %copy-start.3 = (bf16[2,8,128,128]{3,2,1,0:T(8,128)(2,1)S(1)}, bf16[2,8,128,128]{3,2,1,0:T(8,128)(2,1)}, u32[]{:S(2)}) copy-start(bf16[2,8,128,128]{3,2,1,0:T(8,128)(2,1)} %get-tuple-element.79.refs_6_) | copy-start | bytes 1572868
  52.3 1.6 %copy-start.2 = (f32[8,128,128]{2,1,0:T(8,128)S(1)}, f32[8,128,128]{2,1,0:T(8,128)}, u32[]{:S(2)}) copy-start(f32[8,128,128]{2,1,0:T(8,128)} %get-tuple-element.78.refs_5_) | copy-start | bytes 1572868
  52.3 1.6 %collective-permute-start.15 = (f32[2,2,128,128]{3,2,1,0:T(8,128)S(1)}, f32[2,2,128,128]{3,2,1,0:T(8,128)S(1)}, u32[]{:S(2)}, u32[]{:S(2)}) collective-permute-start(f32[2,2,128,128]{3,2,1,0:T(8,128)S(1)} %fusion.4), channel_id=1, source_target_pairs={{0,1},{1,0},{2,3},{3,2},{4,5},{5,4},{6,7},{7,6},{8,9},{9,8},{10,11... | collective-permute-start | bytes 786440 | tf_op jit(solution)/shard_map/ppermute | solution.py:386
  54.6 1.7 %collective-permute-start.17 = (f32[8,64,128]{2,1,0:T(8,128)S(1)}, f32[8,64,128]{2,1,0:T(8,128)}, u32[]{:S(2)}, u32[]{:S(2)}) collective-permute-start(f32[8,64,128]{2,1,0:T(8,128)S(1)} %get-tuple-element.81), channel_id=1, source_target_pairs={{0,1},{1,0},{2,3},{3,2},{4,5},{5,4},{6,7},{7,6},{8,9},{9,8},{10,11... | collective-permute-start | bytes 786440 | tf_op jit(solution)/shard_map/ppermute | solution.py:386
  57.4 8.5 %collective-permute-start.18 = (f32[4,64,128]{2,1,0:T(8,128)S(1)}, f32[4,64,128]{2,1,0:T(8,128)S(1)}, u32[]{:S(2)}, u32[]{:S(2)}) collective-permute-start(f32[4,64,128]{2,1,0:T(8,128)S(1)} %pad_maximum_fusion.2), channel_id=1, source_target_pairs={{0,2},{1,3},{2,0},{3,1},{4,6},{5,7},{6,4},{7,5},{8,10},{9,11},{10,... | collective-permute-start | bytes 393224 | tf_op jit(solution)/shard_map/ppermute | solution.py:434
  58.1 7.8 %collective-permute-start.19 = (f32[4,64,128]{2,1,0:T(8,128)S(1)}, f32[4,64,128]{2,1,0:T(8,128)S(1)}, u32[]{:S(2)}, u32[]{:S(2)}) collective-permute-start(f32[4,64,128]{2,1,0:T(8,128)S(1)} %pad_maximum_fusion.3), channel_id=1, source_target_pairs={{0,16},{1,17},{2,18},{3,19},{4,20},{5,21},{6,22},{7,23},{8,24},{9,... | collective-permute-start | bytes 393224 | tf_op jit(solution)/shard_map/ppermute | solution.py:434
  60.3 6.7 %collective-permute-start.20 = (f32[4,64,128]{2,1,0:T(8,128)}, f32[4,64,128]{2,1,0:T(8,128)S(1)}, u32[]{:S(2)}, u32[]{:S(2)}) collective-permute-start(f32[4,64,128]{2,1,0:T(8,128)} %pad_maximum_fusion.4), channel_id=1, source_target_pairs={{0,18},{1,19},{2,16},{3,17},{4,22},{5,23},{6,20},{7,21},{8,26},{9,... | collective-permute-start | bytes 393224 | tf_op jit(solution)/shard_map/ppermute | solution.py:434
  67.1 5.9 %collective-permute-start.21 = (f32[64,128]{1,0:T(8,128)S(1)}, f32[64,128]{1,0:T(8,128)S(1)}, u32[]{:S(2)}, u32[]{:S(2)}) collective-permute-start(f32[64,128]{1,0:T(8,128)S(1)} %get-tuple-element.110), channel_id=1, source_target_pairs={{0,4},{1,5},{2,6},{3,7},{4,8},{5,9},{6,10},{7,11},{8,12},{9,13},{1... | collective-permute-start | bytes 98312 | tf_op jit(solution)/shard_map/ppermute | solution.py:444
  69.2 4.8 %collective-permute-start.22 = (f32[64,128]{1,0:T(8,128)S(1)}, f32[64,128]{1,0:T(8,128)S(1)}, u32[]{:S(2)}, u32[]{:S(2)}) collective-permute-start(f32[64,128]{1,0:T(8,128)S(1)} %get-tuple-element.112), channel_id=1, source_target_pairs={{0,8},{1,9},{2,10},{3,11},{4,12},{5,13},{6,14},{7,15},{8,0},{9,1},... | collective-permute-start | bytes 98312 | tf_op jit(solution)/shard_map/ppermute | solution.py:444
  71.1 3.9 %collective-permute-start.23 = (f32[64,128]{1,0:T(8,128)S(1)}, f32[64,128]{1,0:T(8,128)S(1)}, u32[]{:S(2)}, u32[]{:S(2)}) collective-permute-start(f32[64,128]{1,0:T(8,128)S(1)} %get-tuple-element.111), channel_id=1, source_target_pairs={{0,12},{1,13},{2,14},{3,15},{4,0},{5,1},{6,2},{7,3},{8,4},{9,5},{1... | collective-permute-start | bytes 98312 | tf_op jit(solution)/shard_map/ppermute | solution.py:444
where the time goes:
time: 76 us; the launch traced here: 75.7 us
  waiting for transfers between devices  26 us (34%)
  starting transfers between devices  24.4 us (32%)
  Pallas kernels  20.9 us (28%)
  other arithmetic  3.1 us (4%)
  between operations  0.98 us (1%)
    pallas_call x7, Pallas kernels, call(): pl.pallas_call(body, out_shape=shapes, in_specs=specs(len(operands), near...  20.9 us
    ppermute x6, starting transfers between devices, chain_swap(): return lax.ppermute(state, 'context', steps)  10.4 us
    ppermute x6, waiting for transfers between devices, chain_swap(): return lax.ppermute(state, 'context', steps)  9.16 us
    ppermute x4, waiting for transfers between devices, swap_chip(): lax.ppermute(state, 'context', [(i, i ^ 2) for i in range(plan.ranks)])  8.58 us
    ppermute x4, starting transfers between devices, swap_chip(): lax.ppermute(state, 'context', [(i, i ^ 2) for i in range(plan.ranks)])  4.55 us
    ppermute x3, starting transfers between devices, group_sum(): result = result + lax.ppermute(sent, 'context', steps)  4.5 us
    ppermute x8, waiting for transfers between devices, swap_core(): lax.ppermute(state, 'context', [(i, i ^ 1) for i in range(plan.ranks)])  3.64 us
    ppermute x3, starting transfers between devices, plane_sums(): plane = plane + lax.ppermute(sent, ('dp', 'context'), steps)  3.62 us
  transfers between devices with their start and end apart: 24, of which 14 were waited for; matrix products, arithmetic and copies ran while one was open for 2% of the time, Pallas kernels for 23%

commit v1 on v0

--- a/solution.py
+++ b/solution.py
@@ -179,61 +179,50 @@
     return row >= column
 
 
-def inner_kernel(plan, *refs):
-    row_refs, maps_ref = refs[:4], refs[4]
-    out_refs = refs[5 : 5 + 2 * plan.chunks]
-    row_bufs, maps_buf = refs[-8:-4], refs[-4]
-    base_buf, pair_buf, sems = refs[-3:]
+def inner_kernel(plan, chunk, *refs):
+    row_refs, maps_ref, base_ref, pair_ref = refs[:4], refs[4], refs[5], refs[6]
+    row_bufs, maps_buf, base_buf, pair_buf, sems = refs[7:11], refs[11], refs[12], refs[13], refs[14]
     copies, width = Copies(sems), plan.width
-    started = [
-        load_chunk(plan, copies, chunk, chunk * plan.in_chunk, row_refs, maps_ref, row_bufs, maps_buf)
-        for chunk in range(plan.chunks)
-    ]
+    started = load_chunk(plan, copies, chunk, 0, row_refs, maps_ref, row_bufs, maps_buf)
     causal = causal_mask(plan.tokens)
     written = []
-    for chunk in range(plan.chunks):
-        wait(started[chunk])
-        for first in range(0, plan.in_chunk, 4):
-            places = range(first, first + 4)
-            at = [chunk * plan.in_chunk + place for place in places]
-            queries, keys, values, grads = [
-                [head_of(buf, n, width) for n in at] for buf in row_bufs
-            ]
-            scores = [
-                jnp.where(causal, dot(grad, value, 1, 1), 0.0).astype(BF16)
-                for grad, value in zip(grads, values)
-            ]
-            feats_query = [dot(x, maps_buf[n]).astype(BF16) for x, n in zip(queries, at)]
-            feats_key = [dot(x, maps_buf[n]).astype(BF16) for x, n in zip(keys, at)]
-            grads_a = [dot(s, feat).astype(BF16) for s, feat in zip(scores, feats_key)]
-            grads_b = [dot(s, feat, 0, 0).astype(BF16) for s, feat in zip(scores, feats_query)]
-            for n, place in enumerate(places):
-                pair_buf[chunk, 0, place] = dot(queries[n], grads[n], 0, 0).astype(BF16)
-                pair_buf[chunk, 1, place] = dot(keys[n], values[n], 0, 0).astype(BF16)
-                base_buf[chunk, place] = dot(queries[n], grads_a[n], 0, 0) + dot(
-                    keys[n], grads_b[n], 0, 0
-                )
-        written.append(copies.start(base_buf.at[chunk], out_refs[2 * chunk]))
-        written.append(copies.start(pair_buf.at[chunk], out_refs[2 * chunk + 1]))
+    size = 5 * max(1, 4 // plan.run)
+    for first in range(0, plan.in_chunk, 4):
+        places = range(first, first + 4)
+        wait(started[:size])
+        started = started[size:]
+        queries, keys, values, grads = [
+            [head_of(buf, n, width) for n in places] for buf in row_bufs
+        ]
+        scores = [
+            jnp.where(causal, dot(grad, value, 1, 1), 0.0).astype(BF16)
+            for grad, value in zip(grads, values)
+        ]
+        feats_query = [dot(x, maps_buf[n]).astype(BF16) for x, n in zip(queries, places)]
+        feats_key = [dot(x, maps_buf[n]).astype(BF16) for x, n in zip(keys, places)]
+        grads_a = [dot(s, feat).astype(BF16) for s, feat in zip(scores, feats_key)]
+        grads_b = [dot(s, feat, 0, 0).astype(BF16) for s, feat in zip(scores, feats_query)]
+        for n, place in enumerate(places):
+            pair_buf[0, place] = dot(queries[n], grads[n], 0, 0).astype(BF16)
+            pair_buf[1, place] = dot(keys[n], values[n], 0, 0).astype(BF16)
+            base_buf[place] = dot(queries[n], grads_a[n], 0, 0) + dot(keys[n], grads_b[n], 0, 0)
+        part = pl.ds(first, 4)
+        written.append(copies.start(base_buf.at[part], base_ref.at[part]))
+        written.append(copies.start(pair_buf.at[:, part], pair_ref.at[:, part]))
     wait(written)
 
 
-def inner(plan, rows, maps):
+def inner(plan, chunk, rows, maps):
     square = (plan.in_chunk, plan.width, plan.width)
-    outs = call(
-        functools.partial(inner_kernel, plan),
+    return call(
+        functools.partial(inner_kernel, plan, chunk),
         (*rows, maps),
-        [jax.ShapeDtypeStruct(square, F32), jax.ShapeDtypeStruct((2,) + square, BF16)]
-        * plan.chunks,
-        matmuls(plan, 9 * plan.heads),
-        row_scratch(plan, plan.heads)
-        + [
-            pltpu.VMEM((plan.chunks,) + square, F32),
-            pltpu.VMEM((plan.chunks, 2) + square, BF16),
-        ],
-        plan.chunks * (chunk_copies(plan) + 2),
-    )
-    return [outs[2 * chunk : 2 * chunk + 2] for chunk in range(plan.chunks)]
+        [jax.ShapeDtypeStruct(square, F32), jax.ShapeDtypeStruct((2,) + square, BF16)],
+        matmuls(plan, 9 * plan.in_chunk),
+        row_scratch(plan, plan.in_chunk)
+        + [pltpu.VMEM(square, F32), pltpu.VMEM((2,) + square, BF16)],
+        chunk_copies(plan) + plan.in_chunk // 2,
+    )
 
 
 def finish_states(plan, state_refs, extra_buf, state_buf):
@@ -463,6 +452,10 @@
     return before
 
 
+def after(value, *others):
+    return lax.optimization_barrier((value, *others))[0]
+
+
 def per_device(queries, key_rows, value_rows, out_grad, maps):
     tokens = queries.shape[1]
     heads, width, _ = maps.shape
@@ -470,24 +463,30 @@
     rows = [x.reshape(tokens, heads * width) for x in (queries, key_rows, value_rows, out_grad)]
     core, chip, group = device_place()
     side = jnp.arange(2).reshape(2, 1, 1, 1)
-    chunks, hops, tie = range(plan.chunks), plan.groups - 1, lax.optimization_barrier
-
-    kept, from_core, total, from_chip, group_state = [], [], [], [], []
+    chunks, hops, last = range(plan.chunks), plan.groups - 1, plan.chunks - 1
+
+    kept, from_core, given, terms = [], [], [], []
+    total, from_chip, group_state = [], [], []
     for chunk in chunks:
-        sent, kept_here, given = block_states(plan, chunk, rows, maps)
+        matrices = after(maps, given[-1]) if chunk else maps
+        sent, kept_here, given_here = block_states(plan, chunk, rows, matrices)
         kept.append(kept_here)
         from_core.append(swap_core(plan, sent))
-        given = given + from_core[chunk][1]
-        if chunk == plan.chunks - 1:
-            terms = inner(plan, rows, maps)
+        given_here = given_here + from_core[chunk][1]
         if chunk:
-            given, terms = tie((given, terms))
+            terms.append(inner(plan, 0, rows, after(maps, sent)))
+            given_here = after(given_here, *terms[0])
+        given.append(given_here)
         total.append(kept_here[0] + from_core[chunk][0])
-        from_chip.append(swap_chip(plan, given))
+        from_chip.append(swap_chip(plan, given_here))
         group_state.append(total[chunk] + from_chip[chunk])
+    terms.append(inner(plan, last, rows, after(maps, given[last])))
 
     def for_other_chip(chunk, before):
         return before + jnp.where(side == chip, total[chunk], 0.0)
+
+    def for_other_core(chunk, turn, state):
+        return state + jnp.where(side == core, kept[chunk][turn], 0.0)
 
     before, got, down = [None] * plan.chunks, [[] for _ in chunks], [None] * plan.chunks
     if plan.groups % 2:
@@ -495,25 +494,28 @@
             before[chunk] = scan_alone(plan, group_state[chunk])
             down[chunk] = swap_chip(plan, for_other_chip(chunk, before[chunk]))
     else:
-        for stage in range(hops + plan.chunks - 1):
+        ahead = None
+        for stage in range(hops + last):
             for chunk in chunks:
                 hop = stage - chunk
+                if chunk == 0 and hop == hops:
+                    before[0] = select_group(plan, got[0])
+                    ahead = for_other_chip(0, before[0])
+                    down[0] = swap_chip(plan, ahead)
                 if not 0 <= hop < hops:
                     continue
                 send = jnp.where(group == hop, group_state[chunk][0], group_state[chunk][1])
                 if hop:
                     send = send + got[chunk][-1]
-                if chunk and hop < hops - 1:
-                    send, got[0][hop] = tie((send, got[0][hop]))
-                if chunk and hop == hops - 1:
-                    before[0] = select_group(plan, got[0])
-                    mate = for_other_chip(0, before[0])
-                    send, mate = tie((send, mate))
-                    down[0] = swap_chip(plan, mate)
+                if chunk:
+                    send = after(send, ahead, *(terms[last] if hop == 0 else ()))
+                else:
+                    if last and hop < 2:
+                        send = after(send, (given, from_chip)[hop][last])
+                    ahead = send
                 got[chunk].append(chain_swap(plan, send, hop))
-        last = plan.chunks - 1
         if last:
-            got[last][-1], down[0] = tie((got[last][-1], down[0]))
+            got[last][-1] = after(got[last][-1], for_other_core(0, 1, down[0]))
         before[last] = select_group(plan, got[last])
         down[last] = swap_chip(plan, for_other_chip(last, before[last]))
 
@@ -522,16 +524,14 @@
         states = [before[chunk] + jnp.where(side != chip, from_chip[chunk], 0.0), down[chunk]]
         for turn in range(2):
             if turn and done:
-                states[1], states[2], done = tie((states[1], states[2], done))
-            mine = jnp.where(side == core, kept[chunk][turn], 0.0)
-            states.append(swap_core(plan, states[turn] + mine))
+                states[1] = after(states[1], states[2], *done)
+            states.append(swap_core(plan, for_other_core(chunk, turn, states[turn])))
         if halves:
-            states[3], halves = tie((states[3], halves))
+            states[3] = after(states[3], *halves)
         for_mate, own = maps_term(plan, states, from_core[chunk], *terms[chunk])
         halves.append(own + swap_core(plan, for_mate))
         done = output_rows(plan, chunk, rows, maps, states, from_core[chunk], done)
-    plane = plane_sums(plan, halves)
-    plane, done = tie((plane, done))
+    plane = after(plane_sums(plan, halves), *done)
     query_grad, key_grad, value_grad = done
     maps_grad = group_sum(plan, plane) * plan.norm
     return (query_grad[None], key_grad[None], value_grad[None], maps_grad)

time: 76 us -> 74.4 us (0.979)
  waiting for transfers between devices: 26 us -> 17.3 us
  starting transfers between devices: 24.4 us -> 28.5 us
  Pallas kernels: 20.9 us -> 22.8 us
  local copies, waits for them, and re-layouts: 0.36 us -> 1.29 us
    ppermute x6, waiting for transfers between devices: 9.16 us -> 3.93 us  [chain_swap(): return lax.ppermute(state, 'context', steps)]
    ppermute x4, waiting for transfers between devices: 8.58 us -> 6.1 us  [swap_chip(): lax.ppermute(state, 'context', [(i, i ^ 2) for i in range(plan.ranks)])]
    ppermute x6, starting transfers between devices: 10.4 us -> 12.6 us  [chain_swap(): return lax.ppermute(state, 'context', steps)]
    pallas_call x7 -> x8, Pallas kernels: 20.9 us -> 22.8 us  [call(): pl.pallas_call(body, out_shape=shapes, in_specs=specs(len(operands), near...]
    ppermute x3, waiting for transfers between devices: 3.41 us -> 1.6 us  [group_sum(): result = result + lax.ppermute(sent, 'context', steps)]
    ppermute x3, starting transfers between devices: 4.5 us -> 5.95 us  [group_sum(): result = result + lax.ppermute(sent, 'context', steps)]
    unnamed x16, local copies, waits for them, and re-layouts: 0.29 us -> 1.22 us
    ppermute x8, waiting for transfers between devices: 3.64 us -> 4.53 us  [swap_core(): lax.ppermute(state, 'context', [(i, i ^ 1) for i in range(plan.ranks)])]
  transfers between devices with their start and end apart: 24 -> 24, of which waited for: 14 -> 13; matrix products, arithmetic and copies ran while one was open for 2% -> 2% of each run, Pallas kernels for 23% -> 26%
where the time goes in v1:
time: 74.4 us; the launch traced here: 74 us
  starting transfers between devices  28.5 us (38%)
  Pallas kernels  22.8 us (31%)
  waiting for transfers between devices  17.3 us (23%)
  other arithmetic  3.15 us (4%)
  local copies, waits for them, and re-layouts  1.29 us (2%)
  between operations  1.03 us (1%)
    pallas_call x8, Pallas kernels, call(): pl.pallas_call(body, out_shape=shapes, in_specs=specs(len(operands), near...  22.8 us
    ppermute x6, starting transfers between devices, chain_swap(): return lax.ppermute(state, 'context', steps)  12.6 us
    ppermute x4, waiting for transfers between devices, swap_chip(): lax.ppermute(state, 'context', [(i, i ^ 2) for i in range(plan.ranks)])  6.1 us
    ppermute x3, starting transfers between devices, group_sum(): result = result + lax.ppermute(sent, 'context', steps)  5.95 us
    ppermute x4, starting transfers between devices, swap_chip(): lax.ppermute(state, 'context', [(i, i ^ 2) for i in range(plan.ranks)])  5.32 us
    ppermute x8, waiting for transfers between devices, swap_core(): lax.ppermute(state, 'context', [(i, i ^ 1) for i in range(plan.ranks)])  4.53 us
    ppermute x6, waiting for transfers between devices, chain_swap(): return lax.ppermute(state, 'context', steps)  3.93 us
    ppermute x3, starting transfers between devices, plane_sums(): plane = plane + lax.ppermute(sent, ('dp', 'context'), steps)  3.62 us
  transfers between devices with their start and end apart: 24, of which 13 were waited for; matrix products, arithmetic and copies ran while one was open for 2% of the time, Pallas kernels for 26%

profile of v1, /device:TPU:0, one launch (start us, length us, event | category | flops | bytes accessed | tf_op | source)
XLA Modules:
  0.0 74.0 jit_solution(12299825014767983829)
XLA Ops:
  0.6 3.0 %shard_map.84 = (f32[2,2,2,128,128]{4,3,2,1,0:T(8,128)S(1)}, f32[2,2,2,128,128]{4,3,2,1,0:T(8,128)}, f32[2,2,128,128]{3,2,1,0:T(8,128)S(1)}) custom-call(bf16[128,2048]{1,0:T(8,128)(2,1)} %bitcast.109, bf16[128,2048]{1,0:T(8,128)(2,1)} %bitcast.115, bf16[128,2048]{1,0:T(8,128)(2,1)} %bitcast.121, bf16[128,2048]{1,0:T(8,128)(2,1)} %bitcast.127, ...), custom_call_target="tpu_custom_call" | custom-call | flops 134217728 | bytes 3932160 | tf_op jit(solution)/shard_map/pallas_call | solution.py:59
  4.1 1.5 %collective-permute-done.refs_4_ = f32[2,2,2,128,128]{4,3,2,1,0:T(8,128)S(1)} collective-permute-done((f32[2,2,2,128,128]{4,3,2,1,0:T(8,128)S(1)}, f32[2,2,2,128,128]{4,3,2,1,0:T(8,128)S(1)}, u32[]{:S(2)}, u32[]{:S(2)}) %collective-permute-start) | collective-permute-done | bytes 524320 | tf_op jit(solution)/shard_map/ppermute | solution.py:375
  5.7 3.0 %collective-permute-start.3 = (f32[2,2,128,128]{3,2,1,0:T(8,128)S(1)}, f32[2,2,128,128]{3,2,1,0:T(8,128)S(1)}, u32[]{:S(2)}, u32[]{:S(2)}) collective-permute-start(f32[2,2,128,128]{3,2,1,0:T(8,128)S(1)} %fusion.3), channel_id=1, source_target_pairs={{0,2},{1,3},{2,0},{3,1},{4,6},{5,7},{6,4},{7,5},{8,10},{9,11},{10,... | collective-permute-start | bytes 786440 | tf_op jit(solution)/shard_map/ppermute | solution.py:379
  8.7 3.0 %shard_map.85 = (f32[2,2,2,128,128]{4,3,2,1,0:T(8,128)S(1)}, f32[2,2,2,128,128]{4,3,2,1,0:T(8,128)}, f32[2,2,128,128]{3,2,1,0:T(8,128)S(1)}) custom-call(bf16[128,2048]{1,0:T(8,128)(2,1)} %bitcast.110, bf16[128,2048]{1,0:T(8,128)(2,1)} %bitcast.116, bf16[128,2048]{1,0:T(8,128)(2,1)} %bitcast.122, bf16[128,2048]{1,0:T(8,128)(2,1)} %bitcast.128, ...), custom_call_target="tpu_custom_call" | custom-call | flops 134217728 | bytes 3932160 | tf_op jit(solution)/shard_map/pallas_call | solution.py:59
  11.8 3.5 %shard_map.86 = (f32[8,128,128]{2,1,0:T(8,128)}, bf16[2,8,128,128]{3,2,1,0:T(8,128)(2,1)}) custom-call(bf16[128,2048]{1,0:T(8,128)(2,1)} %bitcast.111, bf16[128,2048]{1,0:T(8,128)(2,1)} %bitcast.117, bf16[128,2048]{1,0:T(8,128)(2,1)} %bitcast.123, bf16[128,2048]{1,0:T(8,128)(2,1)} %bitcast.129, bf16[16,128,128]{2,1,0:T(8,128)(2,1)} %refs_9_.3), custom_call_target="tpu_custom_call" | custom-call | flops 301989888 | bytes 3670016 | tf_op jit(solution)/shard_map/pallas_call | solution.py:59
  15.5 1.8 %collective-permute-start.4 = (f32[2,128,128]{2,1,0:T(8,128)S(1)}, f32[2,128,128]{2,1,0:T(8,128)S(1)}, u32[]{:S(2)}, u32[]{:S(2)}) collective-permute-start(f32[2,128,128]{2,1,0:T(8,128)S(1)} %select_bitcast_fusion.4), channel_id=1, source_target_pairs={{0,4},{1,5},{2,6},{3,7},{4,0},{5,1},{6,2},{7,3},{8,12},{9,13},{10,... | collective-permute-start | bytes 393224 | tf_op jit(solution)/shard_map/ppermute | solution.py:389
  17.3 1.5 %collective-permute-start.2 = (f32[2,2,128,128]{3,2,1,0:T(8,128)S(1)}, f32[2,2,128,128]{3,2,1,0:T(8,128)S(1)}, u32[]{:S(2)}, u32[]{:S(2)}) collective-permute-start(f32[2,2,128,128]{3,2,1,0:T(8,128)S(1)} %fusion.1), channel_id=1, source_target_pairs={{0,2},{1,3},{2,0},{3,1},{4,6},{5,7},{6,4},{7,5},{8,10},{9,11},{10,... | collective-permute-start | bytes 786440 | tf_op jit(solution)/shard_map/ppermute | solution.py:379
  18.8 3.5 %shard_map.87 = (f32[8,128,128]{2,1,0:T(8,128)}, bf16[2,8,128,128]{3,2,1,0:T(8,128)(2,1)}) custom-call(bf16[128,2048]{1,0:T(8,128)(2,1)} %bitcast.112, bf16[128,2048]{1,0:T(8,128)(2,1)} %bitcast.118, bf16[128,2048]{1,0:T(8,128)(2,1)} %bitcast.124, bf16[128,2048]{1,0:T(8,128)(2,1)} %bitcast.130, bf16[16,128,128]{2,1,0:T(8,128)(2,1)} %refs_9_.3), custom_call_target="tpu_custom_call" | custom-call | flops 301989888 | bytes 3670016 | tf_op jit(solution)/shard_map/pallas_call | solution.py:59
  22.3 3.2 %collective-permute-done.2 = f32[2,2,128,128]{3,2,1,0:T(8,128)S(1)} collective-permute-done((f32[2,2,128,128]{3,2,1,0:T(8,128)S(1)}, f32[2,2,128,128]{3,2,1,0:T(8,128)S(1)}, u32[]{:S(2)}, u32[]{:S(2)}) %collective-permute-start.2) | collective-permute-done | bytes 262176 | tf_op jit(solution)/shard_map/ppermute | solution.py:379
  25.6 3.2 %collective-permute-start.5 = (f32[2,128,128]{2,1,0:T(8,128)S(1)}, f32[2,128,128]{2,1,0:T(8,128)S(1)}, u32[]{:S(2)}, u32[]{:S(2)}) collective-permute-start(f32[2,128,128]{2,1,0:T(8,128)S(1)} %select_bitcast_fusion.5), channel_id=1, source_target_pairs={{0,4},{1,5},{2,6},{3,7},{4,0},{5,1},{6,2},{7,3},{8,12},{9,13},{10,... | collective-permute-start | bytes 393224 | tf_op jit(solution)/shard_map/ppermute | solution.py:389
  28.8 2.9 %collective-permute-start.8 = (f32[2,128,128]{2,1,0:T(8,128)S(1)}, f32[2,128,128]{2,1,0:T(8,128)S(1)}, u32[]{:S(2)}, u32[]{:S(2)}) collective-permute-start(f32[2,128,128]{2,1,0:T(8,128)S(1)} %bitcast_add_fusion), channel_id=1, source_target_pairs={{0,4},{1,5},{2,6},{3,7},{4,0},{5,1},{6,2},{7,3},{8,12},{9,13},{10,... | collective-permute-start | bytes 393224 | tf_op jit(solution)/shard_map/ppermute | solution.py:389
  31.7 1.0 %collective-permute-done.5 = f32[2,128,128]{2,1,0:T(8,128)S(1)} collective-permute-done((f32[2,128,128]{2,1,0:T(8,128)S(1)}, f32[2,128,128]{2,1,0:T(8,128)S(1)}, u32[]{:S(2)}, u32[]{:S(2)}) %collective-permute-start.5) | collective-permute-done | bytes 131104 | tf_op jit(solution)/shard_map/ppermute | solution.py:389
  32.8 1.8 %collective-permute-done.8 = f32[2,128,128]{2,1,0:T(8,128)S(1)} collective-permute-done((f32[2,128,128]{2,1,0:T(8,128)S(1)}, f32[2,128,128]{2,1,0:T(8,128)S(1)}, u32[]{:S(2)}, u32[]{:S(2)}) %collective-permute-start.8) | collective-permute-done | bytes 131104 | tf_op jit(solution)/shard_map/ppermute | solution.py:389
  35.4 4.6 %collective-permute-start.9 = (f32[2,128,128]{2,1,0:T(8,128)S(1)}, f32[2,128,128]{2,1,0:T(8,128)S(1)}, u32[]{:S(2)}, u32[]{:S(2)}) collective-permute-start(f32[2,128,128]{2,1,0:T(8,128)S(1)} %bitcast_add_fusion.3), channel_id=1, source_target_pairs={{0,4},{1,5},{2,6},{3,7},{4,0},{5,1},{6,2},{7,3},{8,12},{9,13},{10,... | collective-permute-start | bytes 393224 | tf_op jit(solution)/shard_map/ppermute | solution.py:389
  40.1 1.7 %collective-permute-done.10.refs_1_ = f32[2,2,128,128]{3,2,1,0:T(8,128)S(1)} collective-permute-done((f32[2,2,128,128]{3,2,1,0:T(8,128)S(1)}, f32[2,2,128,128]{3,2,1,0:T(8,128)S(1)}, u32[]{:S(2)}, u32[]{:S(2)}) %collective-permute-start.10) | collective-permute-done | bytes 262176 | tf_op jit(solution)/shard_map/ppermute | solution.py:379
  41.9 1.1 %collective-permute-done.9 = f32[2,128,128]{2,1,0:T(8,128)S(1)} collective-permute-done((f32[2,128,128]{2,1,0:T(8,128)S(1)}, f32[2,128,128]{2,1,0:T(8,128)S(1)}, u32[]{:S(2)}, u32[]{:S(2)}) %collective-permute-start.9) | collective-permute-done | bytes 131104 | tf_op jit(solution)/shard_map/ppermute | solution.py:389
  44.3 0.7 shard_map.89
  45.5 4.2 %shard_map.88 = (bf16[128,2048]{1,0:T(8,128)(2,1)}, bf16[128,2048]{1,0:T(8,128)(2,1)}, bf16[128,2048]{1,0:T(8,128)(2,1)}) custom-call(f32[2,2,128,128]{3,2,1,0:T(8,128)S(1)} %get-tuple-element.71.refs_0_, f32[2,2,128,128]{3,2,1,0:T(8,128)S(1)} %collective-permute-done.10.refs_1_, f32[2,2,128,128]{3,2,1,0:T(8,128)S(1)} %collective-permute-done.13.refs_2_, ...), custom_call_target="tpu_custom_call" | custom-call | flops 4026531 | bytes 57671 | tf_op jit(solution)/shard_map/pallas_call | solution.py:59
  49.7 1.3 %collective-permute-done.11.refs_1_ = f32[2,2,128,128]{3,2,1,0:T(8,128)S(1)} collective-permute-done((f32[2,2,128,128]{3,2,1,0:T(8,128)S(1)}, f32[2,2,128,128]{3,2,1,0:T(8,128)S(1)}, u32[]{:S(2)}, u32[]{:S(2)}) %collective-permute-start.11) | collective-permute-done | bytes 262176 | tf_op jit(solution)/shard_map/ppermute | solution.py:379
  51.2 1.5 %collective-permute-done.15.refs_3_ = f32[2,2,128,128]{3,2,1,0:T(8,128)S(1)} collective-permute-done((f32[2,2,128,128]{3,2,1,0:T(8,128)S(1)}, f32[2,2,128,128]{3,2,1,0:T(8,128)S(1)}, u32[]{:S(2)}, u32[]{:S(2)}) %collective-permute-start.15) | collective-permute-done | bytes 262176 | tf_op jit(solution)/shard_map/ppermute | solution.py:375
  52.6 0.7 shard_map.91
  53.6 1.5 %collective-permute-done.17 = f32[8,64,128]{2,1,0:T(8,128)} collective-permute-done((f32[8,64,128]{2,1,0:T(8,128)S(1)}, f32[8,64,128]{2,1,0:T(8,128)}, u32[]{:S(2)}, u32[]{:S(2)}) %collective-permute-start.17) | collective-permute-done | bytes 262176 | tf_op jit(solution)/shard_map/ppermute | solution.py:375
  55.1 1.0 %add.235 = f32[8,64,128]{2,1,0:T(8,128)S(1)} add(f32[8,64,128]{2,1,0:T(8,128)S(1)} %get-tuple-element.67, f32[8,64,128]{2,1,0:T(8,128)} %collective-permute-done.17) | non-fusion elementwise | flops 65536 | bytes 786432 | tf_op jit(solution)/shard_map/add | solution.py:532
  56.1 0.9 %collective-permute-start.18 = (f32[4,64,128]{2,1,0:T(8,128)S(1)}, f32[4,64,128]{2,1,0:T(8,128)S(1)}, u32[]{:S(2)}, u32[]{:S(2)}) collective-permute-start(f32[4,64,128]{2,1,0:T(8,128)S(1)} %pad_maximum_fusion.2), channel_id=1, source_target_pairs={{0,2},{1,3},{2,0},{3,1},{4,6},{5,7},{6,4},{7,5},{8,10},{9,11},{10,... | collective-permute-start | bytes 393224 | tf_op jit(solution)/shard_map/ppermute | solution.py:423
  57.0 1.5 %collective-permute-start.19 = (f32[4,64,128]{2,1,0:T(8,128)S(1)}, f32[4,64,128]{2,1,0:T(8,128)S(1)}, u32[]{:S(2)}, u32[]{:S(2)}) collective-permute-start(f32[4,64,128]{2,1,0:T(8,128)S(1)} %pad_maximum_fusion.3), channel_id=1, source_target_pairs={{0,16},{1,17},{2,18},{3,19},{4,20},{5,21},{6,22},{7,23},{8,24},{9,... | collective-permute-start | bytes 393224 | tf_op jit(solution)/shard_map/ppermute | solution.py:423
  59.2 1.2 %collective-permute-start.20 = (f32[4,64,128]{2,1,0:T(8,128)}, f32[4,64,128]{2,1,0:T(8,128)S(1)}, u32[]{:S(2)}, u32[]{:S(2)}) collective-permute-start(f32[4,64,128]{2,1,0:T(8,128)} %pad_maximum_fusion.4), channel_id=1, source_target_pairs={{0,18},{1,19},{2,16},{3,17},{4,22},{5,23},{6,20},{7,21},{8,26},{9,... | collective-permute-start | bytes 393224 | tf_op jit(solution)/shard_map/ppermute | solution.py:423
  60.4 4.2 %shard_map.90 = (bf16[128,2048]{1,0:T(8,128)(2,1)}, bf16[128,2048]{1,0:T(8,128)(2,1)}, bf16[128,2048]{1,0:T(8,128)(2,1)}) custom-call(f32[2,2,128,128]{3,2,1,0:T(8,128)S(1)} %get-tuple-element.73.refs_0_, f32[2,2,128,128]{3,2,1,0:T(8,128)S(1)} %collective-permute-done.11.refs_1_, ...), custom_call_target="tpu_custom_call", output_to_operand_aliasing={{0}: (10, {}), {1}: (11, {}), {2}: (12, {})} | custom-call | flops 4026531 | bytes 73400 | tf_op jit(solution)/shard_map/pallas_call | solution.py:59
  64.6 1.2 %collective-permute-done.20 = f32[4,64,128]{2,1,0:T(8,128)S(1)} collective-permute-done((f32[4,64,128]{2,1,0:T(8,128)}, f32[4,64,128]{2,1,0:T(8,128)S(1)}, u32[]{:S(2)}, u32[]{:S(2)}) %collective-permute-start.20) | collective-permute-done | bytes 131104 | tf_op jit(solution)/shard_map/ppermute | solution.py:423
  65.9 1.8 %collective-permute-start.21 = (f32[64,128]{1,0:T(8,128)S(1)}, f32[64,128]{1,0:T(8,128)S(1)}, u32[]{:S(2)}, u32[]{:S(2)}) collective-permute-start(f32[64,128]{1,0:T(8,128)S(1)} %get-tuple-element.88), channel_id=1, source_target_pairs={{0,4},{1,5},{2,6},{3,7},{4,8},{5,9},{6,10},{7,11},{8,12},{9,13},{1... | collective-permute-start | bytes 98312 | tf_op jit(solution)/shard_map/ppermute | solution.py:433
  67.7 1.3 %collective-permute-start.22 = (f32[64,128]{1,0:T(8,128)S(1)}, f32[64,128]{1,0:T(8,128)S(1)}, u32[]{:S(2)}, u32[]{:S(2)}) collective-permute-start(f32[64,128]{1,0:T(8,128)S(1)} %get-tuple-element.90), channel_id=1, source_target_pairs={{0,8},{1,9},{2,10},{3,11},{4,12},{5,13},{6,14},{7,15},{8,0},{9,1},... | collective-permute-start | bytes 98312 | tf_op jit(solution)/shard_map/ppermute | solution.py:433
  69.0 2.8 %collective-permute-start.23 = (f32[64,128]{1,0:T(8,128)S(1)}, f32[64,128]{1,0:T(8,128)S(1)}, u32[]{:S(2)}, u32[]{:S(2)}) collective-permute-start(f32[64,128]{1,0:T(8,128)S(1)} %get-tuple-element.89), channel_id=1, source_target_pairs={{0,12},{1,13},{2,14},{3,15},{4,0},{5,1},{6,2},{7,3},{8,4},{9,5},{1... | collective-permute-start | bytes 98312 | tf_op jit(solution)/shard_map/ppermute | solution.py:433
  72.5 0.9 %collective-permute-done.23 = f32[64,128]{1,0:T(8,128)S(1)} collective-permute-done((f32[64,128]{1,0:T(8,128)S(1)}, f32[64,128]{1,0:T(8,128)S(1)}, u32[]{:S(2)}, u32[]{:S(2)}) %collective-permute-start.23) | collective-permute-done | bytes 32800 | tf_op jit(solution)/shard_map/ppermute | solution.py:433
  (68 shorter events, 6.1 us)
Async XLA Ops:
  3.6 2.0 %collective-permute-start = (f32[2,2,2,128,128]{4,3,2,1,0:T(8,128)S(1)}, f32[2,2,2,128,128]{4,3,2,1,0:T(8,128)S(1)}, u32[]{:S(2)}, u32[]{:S(2)}) collective-permute-start(f32[2,2,2,128,128]{4,3,2,1,0:T(8,128)S(1)} %get-tuple-element.38), channel_id=1, source_target_pairs={{0,1},{1,0},{2,3},{3,2},{4,5},{5,4},{6,7},{7,6},{8,9},{9,8},{10,11... | collective-permute-start | bytes 1572872 | tf_op jit(solution)/shard_map/ppermute | solution.py:375
  5.7 9.6 %collective-permute-start.3 = (f32[2,2,128,128]{3,2,1,0:T(8,128)S(1)}, f32[2,2,128,128]{3,2,1,0:T(8,128)S(1)}, u32[]{:S(2)}, u32[]{:S(2)}) collective-permute-start(f32[2,2,128,128]{3,2,1,0:T(8,128)S(1)} %fusion.3), channel_id=1, source_target_pairs={{0,2},{1,3},{2,0},{3,1},{4,6},{5,7},{6,4},{7,5},{8,10},{9,11},{10,... | collective-permute-start | bytes 786440 | tf_op jit(solution)/shard_map/ppermute | solution.py:379
  11.6 3.8 %collective-permute-start.1 = (f32[2,2,2,128,128]{4,3,2,1,0:T(8,128)S(1)}, f32[2,2,2,128,128]{4,3,2,1,0:T(8,128)S(1)}, u32[]{:S(2)}, u32[]{:S(2)}) collective-permute-start(f32[2,2,2,128,128]{4,3,2,1,0:T(8,128)S(1)} %get-tuple-element.41), channel_id=1, source_target_pairs={{0,1},{1,0},{2,3},{3,2},{4,5},{5,4},{6,7},{7,6},{8,9},{9,8},{10,11... | collective-permute-start | bytes 1572872 | tf_op jit(solution)/shard_map/ppermute | solution.py:375
  11.8 3.6 %copy-start.7 = (f32[2,2,2,128,128]{4,3,2,1,0:T(8,128)S(1)}, f32[2,2,2,128,128]{4,3,2,1,0:T(8,128)}, u32[]{:S(2)}) copy-start(f32[2,2,2,128,128]{4,3,2,1,0:T(8,128)} %get-tuple-element.47) | copy-start | bytes 1572868
  15.5 6.8 %collective-permute-start.4 = (f32[2,128,128]{2,1,0:T(8,128)S(1)}, f32[2,128,128]{2,1,0:T(8,128)S(1)}, u32[]{:S(2)}, u32[]{:S(2)}) collective-permute-start(f32[2,128,128]{2,1,0:T(8,128)S(1)} %select_bitcast_fusion.4), channel_id=1, source_target_pairs={{0,4},{1,5},{2,6},{3,7},{4,0},{5,1},{6,2},{7,3},{8,12},{9,13},{10,... | collective-permute-start | bytes 393224 | tf_op jit(solution)/shard_map/ppermute | solution.py:389
  17.3 8.2 %collective-permute-start.2 = (f32[2,2,128,128]{3,2,1,0:T(8,128)S(1)}, f32[2,2,128,128]{3,2,1,0:T(8,128)S(1)}, u32[]{:S(2)}, u32[]{:S(2)}) collective-permute-start(f32[2,2,128,128]{3,2,1,0:T(8,128)S(1)} %fusion.1), channel_id=1, source_target_pairs={{0,2},{1,3},{2,0},{3,1},{4,6},{5,7},{6,4},{7,5},{8,10},{9,11},{10,... | collective-permute-start | bytes 786440 | tf_op jit(solution)/shard_map/ppermute | solution.py:379
  22.3 3.2 %copy-start.6 = (f32[2,2,2,128,128]{4,3,2,1,0:T(8,128)S(1)}, f32[2,2,2,128,128]{4,3,2,1,0:T(8,128)}, u32[]{:S(2)}) copy-start(f32[2,2,2,128,128]{4,3,2,1,0:T(8,128)} %get-tuple-element.40) | copy-start | bytes 1572868
  25.5 3.3 %collective-permute-start.6 = (f32[2,128,128]{2,1,0:T(8,128)S(1)}, f32[2,128,128]{2,1,0:T(8,128)S(1)}, u32[]{:S(2)}, u32[]{:S(2)}) collective-permute-start(f32[2,128,128]{2,1,0:T(8,128)S(1)} %bitcast_add_fusion.1), channel_id=1, source_target_pairs={{0,1},{1,0},{2,3},{3,2},{4,8},{5,9},{6,10},{7,11},{8,4},{9,5},{10,... | collective-permute-start | bytes 393224 | tf_op jit(solution)/shard_map/ppermute | solution.py:389
  25.6 7.1 %collective-permute-start.5 = (f32[2,128,128]{2,1,0:T(8,128)S(1)}, f32[2,128,128]{2,1,0:T(8,128)S(1)}, u32[]{:S(2)}, u32[]{:S(2)}) collective-permute-start(f32[2,128,128]{2,1,0:T(8,128)S(1)} %select_bitcast_fusion.5), channel_id=1, source_target_pairs={{0,4},{1,5},{2,6},{3,7},{4,0},{5,1},{6,2},{7,3},{8,12},{9,13},{10,... | collective-permute-start | bytes 393224 | tf_op jit(solution)/shard_map/ppermute | solution.py:389
  28.8 5.8 %collective-permute-start.8 = (f32[2,128,128]{2,1,0:T(8,128)S(1)}, f32[2,128,128]{2,1,0:T(8,128)S(1)}, u32[]{:S(2)}, u32[]{:S(2)}) collective-permute-start(f32[2,128,128]{2,1,0:T(8,128)S(1)} %bitcast_add_fusion), channel_id=1, source_target_pairs={{0,4},{1,5},{2,6},{3,7},{4,0},{5,1},{6,2},{7,3},{8,12},{9,13},{10,... | collective-permute-start | bytes 393224 | tf_op jit(solution)/shard_map/ppermute | solution.py:389
  32.7 2.7 %collective-permute-start.7 = (f32[2,128,128]{2,1,0:T(8,128)S(1)}, f32[2,128,128]{2,1,0:T(8,128)S(1)}, u32[]{:S(2)}, u32[]{:S(2)}) collective-permute-start(f32[2,128,128]{2,1,0:T(8,128)S(1)} %bitcast_add_fusion.2), channel_id=1, source_target_pairs={{0,1},{1,0},{2,3},{3,2},{4,8},{5,9},{6,10},{7,11},{8,4},{9,5},{10,... | collective-permute-start | bytes 393224 | tf_op jit(solution)/shard_map/ppermute | solution.py:389
  34.8 6.9 %collective-permute-start.10 = (f32[2,2,128,128]{3,2,1,0:T(8,128)S(1)}, f32[2,2,128,128]{3,2,1,0:T(8,128)S(1)}, u32[]{:S(2)}, u32[]{:S(2)}) collective-permute-start(f32[2,2,128,128]{3,2,1,0:T(8,128)S(1)} %get-tuple-element.74), channel_id=1, source_target_pairs={{0,2},{1,3},{2,0},{3,1},{4,6},{5,7},{6,4},{7,5},{8,10},{9,11},{10,... | collective-permute-start | bytes 786440 | tf_op jit(solution)/shard_map/ppermute | solution.py:379
  35.4 8.1 %collective-permute-start.13 = (f32[2,2,128,128]{3,2,1,0:T(8,128)S(1)}, f32[2,2,128,128]{3,2,1,0:T(8,128)S(1)}, u32[]{:S(2)}, u32[]{:S(2)}) collective-permute-start(f32[2,2,128,128]{3,2,1,0:T(8,128)S(1)} %get-tuple-element.70), channel_id=1, source_target_pairs={{0,1},{1,0},{2,3},{3,2},{4,5},{5,4},{6,7},{7,6},{8,9},{9,8},{10,11... | collective-permute-start | bytes 786440 | tf_op jit(solution)/shard_map/ppermute | solution.py:375
  35.4 7.6 %collective-permute-start.9 = (f32[2,128,128]{2,1,0:T(8,128)S(1)}, f32[2,128,128]{2,1,0:T(8,128)S(1)}, u32[]{:S(2)}, u32[]{:S(2)}) collective-permute-start(f32[2,128,128]{2,1,0:T(8,128)S(1)} %bitcast_add_fusion.3), channel_id=1, source_target_pairs={{0,4},{1,5},{2,6},{3,7},{4,0},{5,1},{6,2},{7,3},{8,12},{9,13},{10,... | collective-permute-start | bytes 393224 | tf_op jit(solution)/shard_map/ppermute | solution.py:389
  41.9 1.6 %collective-permute-start.14 = (f32[2,2,128,128]{3,2,1,0:T(8,128)S(1)}, f32[2,2,128,128]{3,2,1,0:T(8,128)S(1)}, u32[]{:S(2)}, u32[]{:S(2)}) collective-permute-start(f32[2,2,128,128]{3,2,1,0:T(8,128)S(1)} %fusion.5), channel_id=1, source_target_pairs={{0,1},{1,0},{2,3},{3,2},{4,5},{5,4},{6,7},{7,6},{8,9},{9,8},{10,11... | collective-permute-start | bytes 786440 | tf_op jit(solution)/shard_map/ppermute | solution.py:375
  43.1 1.0 %copy-start.4 = (f32[8,128,128]{2,1,0:T(8,128)S(1)}, f32[8,128,128]{2,1,0:T(8,128)}, u32[]{:S(2)}) copy-start(f32[8,128,128]{2,1,0:T(8,128)} %get-tuple-element.44.refs_5_) | copy-start | bytes 1572868
  43.1 1.2 %copy-start.5 = (bf16[2,8,128,128]{3,2,1,0:T(8,128)(2,1)S(1)}, bf16[2,8,128,128]{3,2,1,0:T(8,128)(2,1)}, u32[]{:S(2)}) copy-start(bf16[2,8,128,128]{3,2,1,0:T(8,128)(2,1)} %get-tuple-element.45.refs_6_) | copy-start | bytes 1572868
  43.2 7.7 %collective-permute-start.11 = (f32[2,2,128,128]{3,2,1,0:T(8,128)S(1)}, f32[2,2,128,128]{3,2,1,0:T(8,128)S(1)}, u32[]{:S(2)}, u32[]{:S(2)}) collective-permute-start(f32[2,2,128,128]{3,2,1,0:T(8,128)S(1)} %get-tuple-element.75), channel_id=1, source_target_pairs={{0,2},{1,3},{2,0},{3,1},{4,6},{5,7},{6,4},{7,5},{8,10},{9,11},{10,... | collective-permute-start | bytes 786440 | tf_op jit(solution)/shard_map/ppermute | solution.py:379
  43.5 7.5 %collective-permute-start.12 = (f32[2,2,128,128]{3,2,1,0:T(8,128)S(1)}, f32[2,2,128,128]{3,2,1,0:T(8,128)S(1)}, u32[]{:S(2)}, u32[]{:S(2)}) collective-permute-start(f32[2,2,128,128]{3,2,1,0:T(8,128)S(1)} %get-tuple-element.72), channel_id=1, source_target_pairs={{0,1},{1,0},{2,3},{3,2},{4,5},{5,4},{6,7},{7,6},{8,9},{9,8},{10,11... | collective-permute-start | bytes 786440 | tf_op jit(solution)/shard_map/ppermute | solution.py:375
  44.3 1.0 %copy-start = (bf16[1,128,2048]{2,1,0:T(8,128)(2,1)S(1)}, bf16[1,128,2048]{2,1,0:T(8,128)(2,1)}, u32[]{:S(2)}) copy-start(bf16[1,128,2048]{2,1,0:T(8,128)(2,1)} %param.5) | copy-start | bytes 1572868
  44.3 1.2 %copy-start.1 = (bf16[1,128,2048]{2,1,0:T(8,128)(2,1)S(1)}, bf16[1,128,2048]{2,1,0:T(8,128)(2,1)}, u32[]{:S(2)}) copy-start(bf16[1,128,2048]{2,1,0:T(8,128)(2,1)} %param.6) | copy-start | bytes 1572868
  45.0 6.2 %collective-permute-start.16 = (f32[8,64,128]{2,1,0:T(8,128)S(1)}, f32[8,64,128]{2,1,0:T(8,128)S(1)}, u32[]{:S(2)}, u32[]{:S(2)}) collective-permute-start(f32[8,64,128]{2,1,0:T(8,128)S(1)} %get-tuple-element.62), channel_id=1, source_target_pairs={{0,1},{1,0},{2,3},{3,2},{4,5},{5,4},{6,7},{7,6},{8,9},{9,8},{10,11... | collective-permute-start | bytes 786440 | tf_op jit(solution)/shard_map/ppermute | solution.py:375
  50.9 1.7 %copy-start.3 = (bf16[2,8,128,128]{3,2,1,0:T(8,128)(2,1)S(1)}, bf16[2,8,128,128]{3,2,1,0:T(8,128)(2,1)}, u32[]{:S(2)}) copy-start(bf16[2,8,128,128]{3,2,1,0:T(8,128)(2,1)} %get-tuple-element.52.refs_6_) | copy-start | bytes 1572868
  51.0 1.6 %copy-start.2 = (f32[8,128,128]{2,1,0:T(8,128)S(1)}, f32[8,128,128]{2,1,0:T(8,128)}, u32[]{:S(2)}) copy-start(f32[8,128,128]{2,1,0:T(8,128)} %get-tuple-element.51.refs_5_) | copy-start | bytes 1572868
  51.0 1.6 %collective-permute-start.15 = (f32[2,2,128,128]{3,2,1,0:T(8,128)S(1)}, f32[2,2,128,128]{3,2,1,0:T(8,128)S(1)}, u32[]{:S(2)}, u32[]{:S(2)}) collective-permute-start(f32[2,2,128,128]{3,2,1,0:T(8,128)S(1)} %fusion.4), channel_id=1, source_target_pairs={{0,1},{1,0},{2,3},{3,2},{4,5},{5,4},{6,7},{7,6},{8,9},{9,8},{10,11... | collective-permute-start | bytes 786440 | tf_op jit(solution)/shard_map/ppermute | solution.py:375
  53.3 1.7 %collective-permute-start.17 = (f32[8,64,128]{2,1,0:T(8,128)S(1)}, f32[8,64,128]{2,1,0:T(8,128)}, u32[]{:S(2)}, u32[]{:S(2)}) collective-permute-start(f32[8,64,128]{2,1,0:T(8,128)S(1)} %get-tuple-element.68), channel_id=1, source_target_pairs={{0,1},{1,0},{2,3},{3,2},{4,5},{5,4},{6,7},{7,6},{8,9},{9,8},{10,11... | collective-permute-start | bytes 786440 | tf_op jit(solution)/shard_map/ppermute | solution.py:375
  56.1 8.5 %collective-permute-start.18 = (f32[4,64,128]{2,1,0:T(8,128)S(1)}, f32[4,64,128]{2,1,0:T(8,128)S(1)}, u32[]{:S(2)}, u32[]{:S(2)}) collective-permute-start(f32[4,64,128]{2,1,0:T(8,128)S(1)} %pad_maximum_fusion.2), channel_id=1, source_target_pairs={{0,2},{1,3},{2,0},{3,1},{4,6},{5,7},{6,4},{7,5},{8,10},{9,11},{10,... | collective-permute-start | bytes 393224 | tf_op jit(solution)/shard_map/ppermute | solution.py:423
  57.0 7.6 %collective-permute-start.19 = (f32[4,64,128]{2,1,0:T(8,128)S(1)}, f32[4,64,128]{2,1,0:T(8,128)S(1)}, u32[]{:S(2)}, u32[]{:S(2)}) collective-permute-start(f32[4,64,128]{2,1,0:T(8,128)S(1)} %pad_maximum_fusion.3), channel_id=1, source_target_pairs={{0,16},{1,17},{2,18},{3,19},{4,20},{5,21},{6,22},{7,23},{8,24},{9,... | collective-permute-start | bytes 393224 | tf_op jit(solution)/shard_map/ppermute | solution.py:423
  59.2 6.6 %collective-permute-start.20 = (f32[4,64,128]{2,1,0:T(8,128)}, f32[4,64,128]{2,1,0:T(8,128)S(1)}, u32[]{:S(2)}, u32[]{:S(2)}) collective-permute-start(f32[4,64,128]{2,1,0:T(8,128)} %pad_maximum_fusion.4), channel_id=1, source_target_pairs={{0,18},{1,19},{2,16},{3,17},{4,22},{5,23},{6,20},{7,21},{8,26},{9,... | collective-permute-start | bytes 393224 | tf_op jit(solution)/shard_map/ppermute | solution.py:423
  65.9 6.1 %collective-permute-start.21 = (f32[64,128]{1,0:T(8,128)S(1)}, f32[64,128]{1,0:T(8,128)S(1)}, u32[]{:S(2)}, u32[]{:S(2)}) collective-permute-start(f32[64,128]{1,0:T(8,128)S(1)} %get-tuple-element.88), channel_id=1, source_target_pairs={{0,4},{1,5},{2,6},{3,7},{4,8},{5,9},{6,10},{7,11},{8,12},{9,13},{1... | collective-permute-start | bytes 98312 | tf_op jit(solution)/shard_map/ppermute | solution.py:433
  67.7 4.8 %collective-permute-start.22 = (f32[64,128]{1,0:T(8,128)S(1)}, f32[64,128]{1,0:T(8,128)S(1)}, u32[]{:S(2)}, u32[]{:S(2)}) collective-permute-start(f32[64,128]{1,0:T(8,128)S(1)} %get-tuple-element.90), channel_id=1, source_target_pairs={{0,8},{1,9},{2,10},{3,11},{4,12},{5,13},{6,14},{7,15},{8,0},{9,1},... | collective-permute-start | bytes 98312 | tf_op jit(solution)/shard_map/ppermute | solution.py:433
  69.0 4.4 %collective-permute-start.23 = (f32[64,128]{1,0:T(8,128)S(1)}, f32[64,128]{1,0:T(8,128)S(1)}, u32[]{:S(2)}, u32[]{:S(2)}) collective-permute-start(f32[64,128]{1,0:T(8,128)S(1)} %get-tuple-element.89), channel_id=1, source_target_pairs={{0,12},{1,13},{2,14},{3,15},{4,0},{5,1},{6,2},{7,3},{8,4},{9,5},{1... | collective-permute-start | bytes 98312 | tf_op jit(solution)/shard_map/ppermute | solution.py:433

commit v2 on v1

--- a/solution.py
+++ b/solution.py
@@ -473,14 +473,11 @@
         kept.append(kept_here)
         from_core.append(swap_core(plan, sent))
         given_here = given_here + from_core[chunk][1]
-        if chunk:
-            terms.append(inner(plan, 0, rows, after(maps, sent)))
-            given_here = after(given_here, *terms[0])
         given.append(given_here)
         total.append(kept_here[0] + from_core[chunk][0])
         from_chip.append(swap_chip(plan, given_here))
         group_state.append(total[chunk] + from_chip[chunk])
-    terms.append(inner(plan, last, rows, after(maps, given[last])))
+    terms.append(inner(plan, 0, rows, after(maps, given[last])))
 
     def for_other_chip(chunk, before):
         return before + jnp.where(side == chip, total[chunk], 0.0)
@@ -494,7 +491,7 @@
             before[chunk] = scan_alone(plan, group_state[chunk])
             down[chunk] = swap_chip(plan, for_other_chip(chunk, before[chunk]))
     else:
-        ahead = None
+        ahead = behind = given[last]
         for stage in range(hops + last):
             for chunk in chunks:
                 hop = stage - chunk
@@ -507,18 +504,20 @@
                 send = jnp.where(group == hop, group_state[chunk][0], group_state[chunk][1])
                 if hop:
                     send = send + got[chunk][-1]
+                if chunk and hop == 1:
+                    terms.append(inner(plan, last, rows, after(maps, behind)))
                 if chunk:
-                    send = after(send, ahead, *(terms[last] if hop == 0 else ()))
-                else:
-                    if last and hop < 2:
-                        send = after(send, (given, from_chip)[hop][last])
-                    ahead = send
+                    behind = send = after(send, ahead, *(terms[1] if hop == hops - 1 else ()))
+                elif last:
+                    ahead = send = after(send, *(terms[0] if hop == 1 else (behind,)))
                 got[chunk].append(chain_swap(plan, send, hop))
         if last:
             got[last][-1] = after(got[last][-1], for_other_core(0, 1, down[0]))
         before[last] = select_group(plan, got[last])
         down[last] = swap_chip(plan, for_other_chip(last, before[last]))
 
+    if len(terms) < plan.chunks:
+        terms.append(inner(plan, last, rows, maps))
     halves, done = [], ()
     for chunk in chunks:
         states = [before[chunk] + jnp.where(side != chip, from_chip[chunk], 0.0), down[chunk]]

time: 74.4 us -> 76.1 us (1.023)
  waiting for transfers between devices: 17.3 us -> 23.7 us
  starting transfers between devices: 28.5 us -> 24.8 us
  local copies, waits for them, and re-layouts: 1.29 us -> 0.34 us
    ppermute x6, starting transfers between devices: 12.6 us -> 7.99 us  [chain_swap(): return lax.ppermute(state, 'context', steps)]
    ppermute x4, waiting for transfers between devices: 6.1 us -> 8.26 us  [swap_chip(): lax.ppermute(state, 'context', [(i, i ^ 2) for i in range(plan.ranks)])]
    ppermute x6, waiting for transfers between devices: 3.93 us -> 6.08 us  [chain_swap(): return lax.ppermute(state, 'context', steps)]
    ppermute x3, waiting for transfers between devices: 1.6 us -> 3.64 us  [group_sum(): result = result + lax.ppermute(sent, 'context', steps)]
    ppermute x4, starting transfers between devices: 5.32 us -> 6.89 us  [swap_chip(): lax.ppermute(state, 'context', [(i, i ^ 2) for i in range(plan.ranks)])]
    unnamed x16, local copies, waits for them, and re-layouts: 1.22 us -> 0.27 us
    ppermute x3, starting transfers between devices: 5.95 us -> 5.05 us  [group_sum(): result = result + lax.ppermute(sent, 'context', steps)]
  transfers between devices with their start and end apart: 24 -> 24, of which waited for: 13 -> 14; matrix products, arithmetic and copies ran while one was open for 2% -> 2% of each run, Pallas kernels for 26% -> 25%
where the time goes in v2:
time: 76.1 us; the launch traced here: 75.8 us
  starting transfers between devices  24.8 us (33%)
  waiting for transfers between devices  23.7 us (31%)
  Pallas kernels  22.8 us (30%)
  other arithmetic  3.15 us (4%)
  between operations  1.05 us (1%)
    pallas_call x8, Pallas kernels, call(): pl.pallas_call(body, out_shape=shapes, in_specs=specs(len(operands), near...  22.8 us
    ppermute x4, waiting for transfers between devices, swap_chip(): lax.ppermute(state, 'context', [(i, i ^ 2) for i in range(plan.ranks)])  8.26 us
    ppermute x6, starting transfers between devices, chain_swap(): return lax.ppermute(state, 'context', steps)  7.99 us
    ppermute x4, starting transfers between devices, swap_chip(): lax.ppermute(state, 'context', [(i, i ^ 2) for i in range(plan.ranks)])  6.89 us
    ppermute x6, waiting for transfers between devices, chain_swap(): return lax.ppermute(state, 'context', steps)  6.08 us
    ppermute x3, starting transfers between devices, group_sum(): result = result + lax.ppermute(sent, 'context', steps)  5.05 us
    ppermute x8, waiting for transfers between devices, swap_core(): lax.ppermute(state, 'context', [(i, i ^ 1) for i in range(plan.ranks)])  4.52 us
    ppermute x3, waiting for transfers between devices, group_sum(): result = result + lax.ppermute(sent, 'context', steps)  3.64 us
  transfers between devices with their start and end apart: 24, of which 14 were waited for; matrix products, arithmetic and copies ran while one was open for 2% of the time, Pallas kernels for 25%

profile of v2, /device:TPU:0, one launch (start us, length us, event | category | flops | bytes accessed | tf_op | source)
XLA Modules:
  0.0 75.8 jit_solution(9595467835878817723)
XLA Ops:
  0.6 3.0 %shard_map.84 = (f32[2,2,2,128,128]{4,3,2,1,0:T(8,128)S(1)}, f32[2,2,2,128,128]{4,3,2,1,0:T(8,128)}, f32[2,2,128,128]{3,2,1,0:T(8,128)S(1)}) custom-call(bf16[128,2048]{1,0:T(8,128)(2,1)} %bitcast.109, bf16[128,2048]{1,0:T(8,128)(2,1)} %bitcast.115, bf16[128,2048]{1,0:T(8,128)(2,1)} %bitcast.121, bf16[128,2048]{1,0:T(8,128)(2,1)} %bitcast.127, ...), custom_call_target="tpu_custom_call" | custom-call | flops 134217728 | bytes 3932160 | tf_op jit(solution)/shard_map/pallas_call | solution.py:59
  4.1 1.5 %collective-permute-done.refs_4_ = f32[2,2,2,128,128]{4,3,2,1,0:T(8,128)S(1)} collective-permute-done((f32[2,2,2,128,128]{4,3,2,1,0:T(8,128)S(1)}, f32[2,2,2,128,128]{4,3,2,1,0:T(8,128)S(1)}, u32[]{:S(2)}, u32[]{:S(2)}) %collective-permute-start) | collective-permute-done | bytes 524320 | tf_op jit(solution)/shard_map/ppermute | solution.py:375
  5.7 3.0 %collective-permute-start.3 = (f32[2,2,128,128]{3,2,1,0:T(8,128)S(1)}, f32[2,2,128,128]{3,2,1,0:T(8,128)S(1)}, u32[]{:S(2)}, u32[]{:S(2)}) collective-permute-start(f32[2,2,128,128]{3,2,1,0:T(8,128)S(1)} %fusion.3), channel_id=1, source_target_pairs={{0,2},{1,3},{2,0},{3,1},{4,6},{5,7},{6,4},{7,5},{8,10},{9,11},{10,... | collective-permute-start | bytes 786440 | tf_op jit(solution)/shard_map/ppermute | solution.py:379
  8.7 3.0 %shard_map.85 = (f32[2,2,2,128,128]{4,3,2,1,0:T(8,128)S(1)}, f32[2,2,2,128,128]{4,3,2,1,0:T(8,128)}, f32[2,2,128,128]{3,2,1,0:T(8,128)S(1)}) custom-call(bf16[128,2048]{1,0:T(8,128)(2,1)} %bitcast.110, bf16[128,2048]{1,0:T(8,128)(2,1)} %bitcast.116, bf16[128,2048]{1,0:T(8,128)(2,1)} %bitcast.122, bf16[128,2048]{1,0:T(8,128)(2,1)} %bitcast.128, ...), custom_call_target="tpu_custom_call" | custom-call | flops 134217728 | bytes 3932160 | tf_op jit(solution)/shard_map/pallas_call | solution.py:59
  11.8 3.4 %collective-permute-done.3 = f32[2,2,128,128]{3,2,1,0:T(8,128)S(1)} collective-permute-done((f32[2,2,128,128]{3,2,1,0:T(8,128)S(1)}, f32[2,2,128,128]{3,2,1,0:T(8,128)S(1)}, u32[]{:S(2)}, u32[]{:S(2)}) %collective-permute-start.3) | collective-permute-done | bytes 262176 | tf_op jit(solution)/shard_map/ppermute | solution.py:379
  15.4 1.9 %collective-permute-start.4 = (f32[2,128,128]{2,1,0:T(8,128)S(1)}, f32[2,128,128]{2,1,0:T(8,128)S(1)}, u32[]{:S(2)}, u32[]{:S(2)}) collective-permute-start(f32[2,128,128]{2,1,0:T(8,128)S(1)} %select_bitcast_fusion.4), channel_id=1, source_target_pairs={{0,4},{1,5},{2,6},{3,7},{4,0},{5,1},{6,2},{7,3},{8,12},{9,13},{10,... | collective-permute-start | bytes 393224 | tf_op jit(solution)/shard_map/ppermute | solution.py:389
  17.3 1.5 %collective-permute-start.2 = (f32[2,2,128,128]{3,2,1,0:T(8,128)S(1)}, f32[2,2,128,128]{3,2,1,0:T(8,128)S(1)}, u32[]{:S(2)}, u32[]{:S(2)}) collective-permute-start(f32[2,2,128,128]{3,2,1,0:T(8,128)S(1)} %fusion.1), channel_id=1, source_target_pairs={{0,2},{1,3},{2,0},{3,1},{4,6},{5,7},{6,4},{7,5},{8,10},{9,11},{10,... | collective-permute-start | bytes 786440 | tf_op jit(solution)/shard_map/ppermute | solution.py:379
  18.8 3.5 %shard_map.86 = (f32[8,128,128]{2,1,0:T(8,128)}, bf16[2,8,128,128]{3,2,1,0:T(8,128)(2,1)}) custom-call(bf16[128,2048]{1,0:T(8,128)(2,1)} %bitcast.111, bf16[128,2048]{1,0:T(8,128)(2,1)} %bitcast.117, bf16[128,2048]{1,0:T(8,128)(2,1)} %bitcast.123, bf16[128,2048]{1,0:T(8,128)(2,1)} %bitcast.129, bf16[16,128,128]{2,1,0:T(8,128)(2,1)} %refs_9_.3), custom_call_target="tpu_custom_call" | custom-call | flops 301989888 | bytes 3670016 | tf_op jit(solution)/shard_map/pallas_call | solution.py:59
  22.4 2.1 %collective-permute-done.2 = f32[2,2,128,128]{3,2,1,0:T(8,128)S(1)} collective-permute-done((f32[2,2,128,128]{3,2,1,0:T(8,128)S(1)}, f32[2,2,128,128]{3,2,1,0:T(8,128)S(1)}, u32[]{:S(2)}, u32[]{:S(2)}) %collective-permute-start.2) | collective-permute-done | bytes 262176 | tf_op jit(solution)/shard_map/ppermute | solution.py:379
  24.6 1.1 %collective-permute-start.5 = (f32[2,128,128]{2,1,0:T(8,128)S(1)}, f32[2,128,128]{2,1,0:T(8,128)S(1)}, u32[]{:S(2)}, u32[]{:S(2)}) collective-permute-start(f32[2,128,128]{2,1,0:T(8,128)S(1)} %select_bitcast_fusion.5), channel_id=1, source_target_pairs={{0,4},{1,5},{2,6},{3,7},{4,0},{5,1},{6,2},{7,3},{8,12},{9,13},{10,... | collective-permute-start | bytes 393224 | tf_op jit(solution)/shard_map/ppermute | solution.py:389
  25.7 2.9 %collective-permute-start.8 = (f32[2,128,128]{2,1,0:T(8,128)S(1)}, f32[2,128,128]{2,1,0:T(8,128)S(1)}, u32[]{:S(2)}, u32[]{:S(2)}) collective-permute-start(f32[2,128,128]{2,1,0:T(8,128)S(1)} %bitcast_add_fusion), channel_id=1, source_target_pairs={{0,4},{1,5},{2,6},{3,7},{4,0},{5,1},{6,2},{7,3},{8,12},{9,13},{10,... | collective-permute-start | bytes 393224 | tf_op jit(solution)/shard_map/ppermute | solution.py:389
  28.6 1.5 %collective-permute-done.5 = f32[2,128,128]{2,1,0:T(8,128)S(1)} collective-permute-done((f32[2,128,128]{2,1,0:T(8,128)S(1)}, f32[2,128,128]{2,1,0:T(8,128)S(1)}, u32[]{:S(2)}, u32[]{:S(2)}) %collective-permute-start.5) | collective-permute-done | bytes 131104 | tf_op jit(solution)/shard_map/ppermute | solution.py:389
  30.2 1.3 %collective-permute-done.8 = f32[2,128,128]{2,1,0:T(8,128)S(1)} collective-permute-done((f32[2,128,128]{2,1,0:T(8,128)S(1)}, f32[2,128,128]{2,1,0:T(8,128)S(1)}, u32[]{:S(2)}, u32[]{:S(2)}) %collective-permute-start.8) | collective-permute-done | bytes 131104 | tf_op jit(solution)/shard_map/ppermute | solution.py:389
  31.7 1.1 %collective-permute-start.10 = (f32[2,2,128,128]{3,2,1,0:T(8,128)S(1)}, f32[2,2,128,128]{3,2,1,0:T(8,128)S(1)}, u32[]{:S(2)}, u32[]{:S(2)}) collective-permute-start(f32[2,2,128,128]{3,2,1,0:T(8,128)S(1)} %get-tuple-element.74), channel_id=1, source_target_pairs={{0,2},{1,3},{2,0},{3,1},{4,6},{5,7},{6,4},{7,5},{8,10},{9,11},{10,... | collective-permute-start | bytes 786440 | tf_op jit(solution)/shard_map/ppermute | solution.py:379
  32.8 3.5 %shard_map.87 = (f32[8,128,128]{2,1,0:T(8,128)}, bf16[2,8,128,128]{3,2,1,0:T(8,128)(2,1)}) custom-call(bf16[128,2048]{1,0:T(8,128)(2,1)} %bitcast.112, bf16[128,2048]{1,0:T(8,128)(2,1)} %bitcast.118, bf16[128,2048]{1,0:T(8,128)(2,1)} %bitcast.124, bf16[128,2048]{1,0:T(8,128)(2,1)} %bitcast.130, bf16[16,128,128]{2,1,0:T(8,128)(2,1)} %refs_9_.3), custom_call_target="tpu_custom_call" | custom-call | flops 301989888 | bytes 3670016 | tf_op jit(solution)/shard_map/pallas_call | solution.py:59
  36.4 2.0 %collective-permute-start.9 = (f32[2,128,128]{2,1,0:T(8,128)S(1)}, f32[2,128,128]{2,1,0:T(8,128)S(1)}, u32[]{:S(2)}, u32[]{:S(2)}) collective-permute-start(f32[2,128,128]{2,1,0:T(8,128)S(1)} %bitcast_add_fusion.3), channel_id=1, source_target_pairs={{0,4},{1,5},{2,6},{3,7},{4,0},{5,1},{6,2},{7,3},{8,12},{9,13},{10,... | collective-permute-start | bytes 393224 | tf_op jit(solution)/shard_map/ppermute | solution.py:389
  39.4 3.2 %collective-permute-done.9 = f32[2,128,128]{2,1,0:T(8,128)S(1)} collective-permute-done((f32[2,128,128]{2,1,0:T(8,128)S(1)}, f32[2,128,128]{2,1,0:T(8,128)S(1)}, u32[]{:S(2)}, u32[]{:S(2)}) %collective-permute-start.9) | collective-permute-done | bytes 131104 | tf_op jit(solution)/shard_map/ppermute | solution.py:389
  42.9 1.3 %collective-permute-start.11 = (f32[2,2,128,128]{3,2,1,0:T(8,128)S(1)}, f32[2,2,128,128]{3,2,1,0:T(8,128)S(1)}, u32[]{:S(2)}, u32[]{:S(2)}) collective-permute-start(f32[2,2,128,128]{3,2,1,0:T(8,128)S(1)} %get-tuple-element.75), channel_id=1, source_target_pairs={{0,2},{1,3},{2,0},{3,1},{4,6},{5,7},{6,4},{7,5},{8,10},{9,11},{10,... | collective-permute-start | bytes 786440 | tf_op jit(solution)/shard_map/ppermute | solution.py:379
  45.4 4.2 %shard_map.88 = (bf16[128,2048]{1,0:T(8,128)(2,1)}, bf16[128,2048]{1,0:T(8,128)(2,1)}, bf16[128,2048]{1,0:T(8,128)(2,1)}) custom-call(f32[2,2,128,128]{3,2,1,0:T(8,128)S(1)} %get-tuple-element.71.refs_0_, f32[2,2,128,128]{3,2,1,0:T(8,128)S(1)} %collective-permute-done.10.refs_1_, f32[2,2,128,128]{3,2,1,0:T(8,128)S(1)} %collective-permute-done.13.refs_2_, ...), custom_call_target="tpu_custom_call" | custom-call | flops 4026531 | bytes 57671 | tf_op jit(solution)/shard_map/pallas_call | solution.py:59
  49.6 2.0 %collective-permute-done.11.refs_1_ = f32[2,2,128,128]{3,2,1,0:T(8,128)S(1)} collective-permute-done((f32[2,2,128,128]{3,2,1,0:T(8,128)S(1)}, f32[2,2,128,128]{3,2,1,0:T(8,128)S(1)}, u32[]{:S(2)}, u32[]{:S(2)}) %collective-permute-start.11) | collective-permute-done | bytes 262176 | tf_op jit(solution)/shard_map/ppermute | solution.py:379
  51.8 1.5 %collective-permute-done.15.refs_3_ = f32[2,2,128,128]{3,2,1,0:T(8,128)S(1)} collective-permute-done((f32[2,2,128,128]{3,2,1,0:T(8,128)S(1)}, f32[2,2,128,128]{3,2,1,0:T(8,128)S(1)}, u32[]{:S(2)}, u32[]{:S(2)}) %collective-permute-start.15) | collective-permute-done | bytes 262176 | tf_op jit(solution)/shard_map/ppermute | solution.py:375
  54.2 1.5 %collective-permute-done.17 = f32[8,64,128]{2,1,0:T(8,128)} collective-permute-done((f32[8,64,128]{2,1,0:T(8,128)S(1)}, f32[8,64,128]{2,1,0:T(8,128)}, u32[]{:S(2)}, u32[]{:S(2)}) %collective-permute-start.17) | collective-permute-done | bytes 262176 | tf_op jit(solution)/shard_map/ppermute | solution.py:375
  55.7 1.0 %add.235 = f32[8,64,128]{2,1,0:T(8,128)S(1)} add(f32[8,64,128]{2,1,0:T(8,128)S(1)} %get-tuple-element.67, f32[8,64,128]{2,1,0:T(8,128)} %collective-permute-done.17) | non-fusion elementwise | flops 65536 | bytes 786432 | tf_op jit(solution)/shard_map/add | solution.py:531
  56.8 1.3 %collective-permute-start.18 = (f32[4,64,128]{2,1,0:T(8,128)S(1)}, f32[4,64,128]{2,1,0:T(8,128)S(1)}, u32[]{:S(2)}, u32[]{:S(2)}) collective-permute-start(f32[4,64,128]{2,1,0:T(8,128)S(1)} %pad_maximum_fusion.2), channel_id=1, source_target_pairs={{0,2},{1,3},{2,0},{3,1},{4,6},{5,7},{6,4},{7,5},{8,10},{9,11},{10,... | collective-permute-start | bytes 393224 | tf_op jit(solution)/shard_map/ppermute | solution.py:423
  58.1 1.5 %collective-permute-start.19 = (f32[4,64,128]{2,1,0:T(8,128)S(1)}, f32[4,64,128]{2,1,0:T(8,128)S(1)}, u32[]{:S(2)}, u32[]{:S(2)}) collective-permute-start(f32[4,64,128]{2,1,0:T(8,128)S(1)} %pad_maximum_fusion.3), channel_id=1, source_target_pairs={{0,16},{1,17},{2,18},{3,19},{4,20},{5,21},{6,22},{7,23},{8,24},{9,... | collective-permute-start | bytes 393224 | tf_op jit(solution)/shard_map/ppermute | solution.py:423
  61.1 4.2 %shard_map.90 = (bf16[128,2048]{1,0:T(8,128)(2,1)}, bf16[128,2048]{1,0:T(8,128)(2,1)}, bf16[128,2048]{1,0:T(8,128)(2,1)}) custom-call(f32[2,2,128,128]{3,2,1,0:T(8,128)S(1)} %get-tuple-element.73.refs_0_, f32[2,2,128,128]{3,2,1,0:T(8,128)S(1)} %collective-permute-done.11.refs_1_, ...), custom_call_target="tpu_custom_call", output_to_operand_aliasing={{0}: (10, {}), {1}: (11, {}), {2}: (12, {})} | custom-call | flops 4026531 | bytes 73400 | tf_op jit(solution)/shard_map/pallas_call | solution.py:59
  65.3 1.2 %collective-permute-done.20 = f32[4,64,128]{2,1,0:T(8,128)S(1)} collective-permute-done((f32[4,64,128]{2,1,0:T(8,128)}, f32[4,64,128]{2,1,0:T(8,128)S(1)}, u32[]{:S(2)}, u32[]{:S(2)}) %collective-permute-start.20) | collective-permute-done | bytes 131104 | tf_op jit(solution)/shard_map/ppermute | solution.py:423
  66.5 1.8 %collective-permute-start.21 = (f32[64,128]{1,0:T(8,128)S(1)}, f32[64,128]{1,0:T(8,128)S(1)}, u32[]{:S(2)}, u32[]{:S(2)}) collective-permute-start(f32[64,128]{1,0:T(8,128)S(1)} %get-tuple-element.88), channel_id=1, source_target_pairs={{0,4},{1,5},{2,6},{3,7},{4,8},{5,9},{6,10},{7,11},{8,12},{9,13},{1... | collective-permute-start | bytes 98312 | tf_op jit(solution)/shard_map/ppermute | solution.py:433
  68.3 2.1 %collective-permute-start.23 = (f32[64,128]{1,0:T(8,128)S(1)}, f32[64,128]{1,0:T(8,128)S(1)}, u32[]{:S(2)}, u32[]{:S(2)}) collective-permute-start(f32[64,128]{1,0:T(8,128)S(1)} %get-tuple-element.89), channel_id=1, source_target_pairs={{0,12},{1,13},{2,14},{3,15},{4,0},{5,1},{6,2},{7,3},{8,4},{9,5},{1... | collective-permute-start | bytes 98312 | tf_op jit(solution)/shard_map/ppermute | solution.py:433
  70.4 1.2 %collective-permute-start.22 = (f32[64,128]{1,0:T(8,128)S(1)}, f32[64,128]{1,0:T(8,128)S(1)}, u32[]{:S(2)}, u32[]{:S(2)}) collective-permute-start(f32[64,128]{1,0:T(8,128)S(1)} %get-tuple-element.90), channel_id=1, source_target_pairs={{0,8},{1,9},{2,10},{3,11},{4,12},{5,13},{6,14},{7,15},{8,0},{9,1},... | collective-permute-start | bytes 98312 | tf_op jit(solution)/shard_map/ppermute | solution.py:433
  71.6 0.8 %collective-permute-done.21 = f32[64,128]{1,0:T(8,128)S(1)} collective-permute-done((f32[64,128]{1,0:T(8,128)S(1)}, f32[64,128]{1,0:T(8,128)S(1)}, u32[]{:S(2)}, u32[]{:S(2)}) %collective-permute-start.21) | collective-permute-done | bytes 32800 | tf_op jit(solution)/shard_map/ppermute | solution.py:433
  72.9 2.3 %collective-permute-done.22 = f32[64,128]{1,0:T(8,128)S(1)} collective-permute-done((f32[64,128]{1,0:T(8,128)S(1)}, f32[64,128]{1,0:T(8,128)S(1)}, u32[]{:S(2)}, u32[]{:S(2)}) %collective-permute-start.22) | collective-permute-done | bytes 32800 | tf_op jit(solution)/shard_map/ppermute | solution.py:433
  (68 shorter events, 7.4 us)
Async XLA Ops:
  3.6 2.0 %collective-permute-start = (f32[2,2,2,128,128]{4,3,2,1,0:T(8,128)S(1)}, f32[2,2,2,128,128]{4,3,2,1,0:T(8,128)S(1)}, u32[]{:S(2)}, u32[]{:S(2)}) collective-permute-start(f32[2,2,2,128,128]{4,3,2,1,0:T(8,128)S(1)} %get-tuple-element.38), channel_id=1, source_target_pairs={{0,1},{1,0},{2,3},{3,2},{4,5},{5,4},{6,7},{7,6},{8,9},{9,8},{10,11... | collective-permute-start | bytes 1572872 | tf_op jit(solution)/shard_map/ppermute | solution.py:375
  5.7 9.6 %collective-permute-start.3 = (f32[2,2,128,128]{3,2,1,0:T(8,128)S(1)}, f32[2,2,128,128]{3,2,1,0:T(8,128)S(1)}, u32[]{:S(2)}, u32[]{:S(2)}) collective-permute-start(f32[2,2,128,128]{3,2,1,0:T(8,128)S(1)} %fusion.3), channel_id=1, source_target_pairs={{0,2},{1,3},{2,0},{3,1},{4,6},{5,7},{6,4},{7,5},{8,10},{9,11},{10,... | collective-permute-start | bytes 786440 | tf_op jit(solution)/shard_map/ppermute | solution.py:379
  8.7 6.6 %copy-start.7 = (f32[2,2,2,128,128]{4,3,2,1,0:T(8,128)S(1)}, f32[2,2,2,128,128]{4,3,2,1,0:T(8,128)}, u32[]{:S(2)}) copy-start(f32[2,2,2,128,128]{4,3,2,1,0:T(8,128)} %get-tuple-element.43) | copy-start | bytes 1572868
  11.7 3.6 %collective-permute-start.1 = (f32[2,2,2,128,128]{4,3,2,1,0:T(8,128)S(1)}, f32[2,2,2,128,128]{4,3,2,1,0:T(8,128)S(1)}, u32[]{:S(2)}, u32[]{:S(2)}) collective-permute-start(f32[2,2,2,128,128]{4,3,2,1,0:T(8,128)S(1)} %get-tuple-element.41), channel_id=1, source_target_pairs={{0,1},{1,0},{2,3},{3,2},{4,5},{5,4},{6,7},{7,6},{8,9},{9,8},{10,11... | collective-permute-start | bytes 1572872 | tf_op jit(solution)/shard_map/ppermute | solution.py:375
  15.4 6.9 %collective-permute-start.4 = (f32[2,128,128]{2,1,0:T(8,128)S(1)}, f32[2,128,128]{2,1,0:T(8,128)S(1)}, u32[]{:S(2)}, u32[]{:S(2)}) collective-permute-start(f32[2,128,128]{2,1,0:T(8,128)S(1)} %select_bitcast_fusion.4), channel_id=1, source_target_pairs={{0,4},{1,5},{2,6},{3,7},{4,0},{5,1},{6,2},{7,3},{8,12},{9,13},{10,... | collective-permute-start | bytes 393224 | tf_op jit(solution)/shard_map/ppermute | solution.py:389
  17.3 7.2 %collective-permute-start.2 = (f32[2,2,128,128]{3,2,1,0:T(8,128)S(1)}, f32[2,2,128,128]{3,2,1,0:T(8,128)S(1)}, u32[]{:S(2)}, u32[]{:S(2)}) collective-permute-start(f32[2,2,128,128]{3,2,1,0:T(8,128)S(1)} %fusion.1), channel_id=1, source_target_pairs={{0,2},{1,3},{2,0},{3,1},{4,6},{5,7},{6,4},{7,5},{8,10},{9,11},{10,... | collective-permute-start | bytes 786440 | tf_op jit(solution)/shard_map/ppermute | solution.py:379
  22.3 2.2 %copy-start.6 = (f32[2,2,2,128,128]{4,3,2,1,0:T(8,128)S(1)}, f32[2,2,2,128,128]{4,3,2,1,0:T(8,128)}, u32[]{:S(2)}) copy-start(f32[2,2,2,128,128]{4,3,2,1,0:T(8,128)} %get-tuple-element.40) | copy-start | bytes 1572868
  22.3 3.4 %collective-permute-start.6 = (f32[2,128,128]{2,1,0:T(8,128)S(1)}, f32[2,128,128]{2,1,0:T(8,128)S(1)}, u32[]{:S(2)}, u32[]{:S(2)}) collective-permute-start(f32[2,128,128]{2,1,0:T(8,128)S(1)} %bitcast_add_fusion.1), channel_id=1, source_target_pairs={{0,1},{1,0},{2,3},{3,2},{4,8},{5,9},{6,10},{7,11},{8,4},{9,5},{10,... | collective-permute-start | bytes 393224 | tf_op jit(solution)/shard_map/ppermute | solution.py:389
  24.6 5.5 %collective-permute-start.5 = (f32[2,128,128]{2,1,0:T(8,128)S(1)}, f32[2,128,128]{2,1,0:T(8,128)S(1)}, u32[]{:S(2)}, u32[]{:S(2)}) collective-permute-start(f32[2,128,128]{2,1,0:T(8,128)S(1)} %select_bitcast_fusion.5), channel_id=1, source_target_pairs={{0,4},{1,5},{2,6},{3,7},{4,0},{5,1},{6,2},{7,3},{8,12},{9,13},{10,... | collective-permute-start | bytes 393224 | tf_op jit(solution)/shard_map/ppermute | solution.py:389
  25.7 5.8 %collective-permute-start.8 = (f32[2,128,128]{2,1,0:T(8,128)S(1)}, f32[2,128,128]{2,1,0:T(8,128)S(1)}, u32[]{:S(2)}, u32[]{:S(2)}) collective-permute-start(f32[2,128,128]{2,1,0:T(8,128)S(1)} %bitcast_add_fusion), channel_id=1, source_target_pairs={{0,4},{1,5},{2,6},{3,7},{4,0},{5,1},{6,2},{7,3},{8,12},{9,13},{10,... | collective-permute-start | bytes 393224 | tf_op jit(solution)/shard_map/ppermute | solution.py:389
  30.1 6.2 %collective-permute-start.7 = (f32[2,128,128]{2,1,0:T(8,128)S(1)}, f32[2,128,128]{2,1,0:T(8,128)S(1)}, u32[]{:S(2)}, u32[]{:S(2)}) collective-permute-start(f32[2,128,128]{2,1,0:T(8,128)S(1)} %bitcast_add_fusion.2), channel_id=1, source_target_pairs={{0,1},{1,0},{2,3},{3,2},{4,8},{5,9},{6,10},{7,11},{8,4},{9,5},{10,... | collective-permute-start | bytes 393224 | tf_op jit(solution)/shard_map/ppermute | solution.py:389
  31.7 7.5 %collective-permute-start.10 = (f32[2,2,128,128]{3,2,1,0:T(8,128)S(1)}, f32[2,2,128,128]{3,2,1,0:T(8,128)S(1)}, u32[]{:S(2)}, u32[]{:S(2)}) collective-permute-start(f32[2,2,128,128]{3,2,1,0:T(8,128)S(1)} %get-tuple-element.74), channel_id=1, source_target_pairs={{0,2},{1,3},{2,0},{3,1},{4,6},{5,7},{6,4},{7,5},{8,10},{9,11},{10,... | collective-permute-start | bytes 786440 | tf_op jit(solution)/shard_map/ppermute | solution.py:379
  36.3 7.9 %collective-permute-start.13 = (f32[2,2,128,128]{3,2,1,0:T(8,128)S(1)}, f32[2,2,128,128]{3,2,1,0:T(8,128)S(1)}, u32[]{:S(2)}, u32[]{:S(2)}) collective-permute-start(f32[2,2,128,128]{3,2,1,0:T(8,128)S(1)} %get-tuple-element.70), channel_id=1, source_target_pairs={{0,1},{1,0},{2,3},{3,2},{4,5},{5,4},{6,7},{7,6},{8,9},{9,8},{10,11... | collective-permute-start | bytes 786440 | tf_op jit(solution)/shard_map/ppermute | solution.py:375
  36.4 6.2 %collective-permute-start.9 = (f32[2,128,128]{2,1,0:T(8,128)S(1)}, f32[2,128,128]{2,1,0:T(8,128)S(1)}, u32[]{:S(2)}, u32[]{:S(2)}) collective-permute-start(f32[2,128,128]{2,1,0:T(8,128)S(1)} %bitcast_add_fusion.3), channel_id=1, source_target_pairs={{0,4},{1,5},{2,6},{3,7},{4,0},{5,1},{6,2},{7,3},{8,12},{9,13},{10,... | collective-permute-start | bytes 393224 | tf_op jit(solution)/shard_map/ppermute | solution.py:389
  39.3 4.9 %collective-permute-start.14 = (f32[2,2,128,128]{3,2,1,0:T(8,128)S(1)}, f32[2,2,128,128]{3,2,1,0:T(8,128)S(1)}, u32[]{:S(2)}, u32[]{:S(2)}) collective-permute-start(f32[2,2,128,128]{3,2,1,0:T(8,128)S(1)} %fusion.5), channel_id=1, source_target_pairs={{0,1},{1,0},{2,3},{3,2},{4,5},{5,4},{6,7},{7,6},{8,9},{9,8},{10,11... | collective-permute-start | bytes 786440 | tf_op jit(solution)/shard_map/ppermute | solution.py:375
  42.6 1.6 %copy-start.2 = (f32[8,128,128]{2,1,0:T(8,128)S(1)}, f32[8,128,128]{2,1,0:T(8,128)}, u32[]{:S(2)}) copy-start(f32[8,128,128]{2,1,0:T(8,128)} %get-tuple-element.46.refs_5_) | copy-start | bytes 1572868
  42.6 1.6 %copy-start.3 = (bf16[2,8,128,128]{3,2,1,0:T(8,128)(2,1)S(1)}, bf16[2,8,128,128]{3,2,1,0:T(8,128)(2,1)}, u32[]{:S(2)}) copy-start(bf16[2,8,128,128]{3,2,1,0:T(8,128)(2,1)} %get-tuple-element.47.refs_6_) | copy-start | bytes 1572868
  42.8 6.8 %collective-permute-start.12 = (f32[2,2,128,128]{3,2,1,0:T(8,128)S(1)}, f32[2,2,128,128]{3,2,1,0:T(8,128)S(1)}, u32[]{:S(2)}, u32[]{:S(2)}) collective-permute-start(f32[2,2,128,128]{3,2,1,0:T(8,128)S(1)} %get-tuple-element.72), channel_id=1, source_target_pairs={{0,1},{1,0},{2,3},{3,2},{4,5},{5,4},{6,7},{7,6},{8,9},{9,8},{10,11... | collective-permute-start | bytes 786440 | tf_op jit(solution)/shard_map/ppermute | solution.py:375
  42.9 8.7 %collective-permute-start.11 = (f32[2,2,128,128]{3,2,1,0:T(8,128)S(1)}, f32[2,2,128,128]{3,2,1,0:T(8,128)S(1)}, u32[]{:S(2)}, u32[]{:S(2)}) collective-permute-start(f32[2,2,128,128]{3,2,1,0:T(8,128)S(1)} %get-tuple-element.75), channel_id=1, source_target_pairs={{0,2},{1,3},{2,0},{3,1},{4,6},{5,7},{6,4},{7,5},{8,10},{9,11},{10,... | collective-permute-start | bytes 786440 | tf_op jit(solution)/shard_map/ppermute | solution.py:379
  44.2 1.0 %copy-start = (bf16[1,128,2048]{2,1,0:T(8,128)(2,1)S(1)}, bf16[1,128,2048]{2,1,0:T(8,128)(2,1)}, u32[]{:S(2)}) copy-start(bf16[1,128,2048]{2,1,0:T(8,128)(2,1)} %param.5) | copy-start | bytes 1572868
  44.2 1.2 %copy-start.1 = (bf16[1,128,2048]{2,1,0:T(8,128)(2,1)S(1)}, bf16[1,128,2048]{2,1,0:T(8,128)(2,1)}, u32[]{:S(2)}) copy-start(bf16[1,128,2048]{2,1,0:T(8,128)(2,1)} %param.6) | copy-start | bytes 1572868
  45.0 6.8 %collective-permute-start.16 = (f32[8,64,128]{2,1,0:T(8,128)S(1)}, f32[8,64,128]{2,1,0:T(8,128)S(1)}, u32[]{:S(2)}, u32[]{:S(2)}) collective-permute-start(f32[8,64,128]{2,1,0:T(8,128)S(1)} %get-tuple-element.62), channel_id=1, source_target_pairs={{0,1},{1,0},{2,3},{3,2},{4,5},{5,4},{6,7},{7,6},{8,9},{9,8},{10,11... | collective-permute-start | bytes 786440 | tf_op jit(solution)/shard_map/ppermute | solution.py:375
  51.6 1.7 %copy-start.5 = (bf16[2,8,128,128]{3,2,1,0:T(8,128)(2,1)S(1)}, bf16[2,8,128,128]{3,2,1,0:T(8,128)(2,1)}, u32[]{:S(2)}) copy-start(bf16[2,8,128,128]{3,2,1,0:T(8,128)(2,1)} %get-tuple-element.54.refs_6_) | copy-start | bytes 1572868
  51.7 1.6 %copy-start.4 = (f32[8,128,128]{2,1,0:T(8,128)S(1)}, f32[8,128,128]{2,1,0:T(8,128)}, u32[]{:S(2)}) copy-start(f32[8,128,128]{2,1,0:T(8,128)} %get-tuple-element.53.refs_5_) | copy-start | bytes 1572868
  51.7 1.6 %collective-permute-start.15 = (f32[2,2,128,128]{3,2,1,0:T(8,128)S(1)}, f32[2,2,128,128]{3,2,1,0:T(8,128)S(1)}, u32[]{:S(2)}, u32[]{:S(2)}) collective-permute-start(f32[2,2,128,128]{3,2,1,0:T(8,128)S(1)} %fusion.4), channel_id=1, source_target_pairs={{0,1},{1,0},{2,3},{3,2},{4,5},{5,4},{6,7},{7,6},{8,9},{9,8},{10,11... | collective-permute-start | bytes 786440 | tf_op jit(solution)/shard_map/ppermute | solution.py:375
  54.0 1.7 %collective-permute-start.17 = (f32[8,64,128]{2,1,0:T(8,128)S(1)}, f32[8,64,128]{2,1,0:T(8,128)}, u32[]{:S(2)}, u32[]{:S(2)}) collective-permute-start(f32[8,64,128]{2,1,0:T(8,128)S(1)} %get-tuple-element.68), channel_id=1, source_target_pairs={{0,1},{1,0},{2,3},{3,2},{4,5},{5,4},{6,7},{7,6},{8,9},{9,8},{10,11... | collective-permute-start | bytes 786440 | tf_op jit(solution)/shard_map/ppermute | solution.py:375
  56.8 8.5 %collective-permute-start.18 = (f32[4,64,128]{2,1,0:T(8,128)S(1)}, f32[4,64,128]{2,1,0:T(8,128)S(1)}, u32[]{:S(2)}, u32[]{:S(2)}) collective-permute-start(f32[4,64,128]{2,1,0:T(8,128)S(1)} %pad_maximum_fusion.2), channel_id=1, source_target_pairs={{0,2},{1,3},{2,0},{3,1},{4,6},{5,7},{6,4},{7,5},{8,10},{9,11},{10,... | collective-permute-start | bytes 393224 | tf_op jit(solution)/shard_map/ppermute | solution.py:423
  58.1 7.2 %collective-permute-start.19 = (f32[4,64,128]{2,1,0:T(8,128)S(1)}, f32[4,64,128]{2,1,0:T(8,128)S(1)}, u32[]{:S(2)}, u32[]{:S(2)}) collective-permute-start(f32[4,64,128]{2,1,0:T(8,128)S(1)} %pad_maximum_fusion.3), channel_id=1, source_target_pairs={{0,16},{1,17},{2,18},{3,19},{4,20},{5,21},{6,22},{7,23},{8,24},{9,... | collective-permute-start | bytes 393224 | tf_op jit(solution)/shard_map/ppermute | solution.py:423
  60.3 6.1 %collective-permute-start.20 = (f32[4,64,128]{2,1,0:T(8,128)}, f32[4,64,128]{2,1,0:T(8,128)S(1)}, u32[]{:S(2)}, u32[]{:S(2)}) collective-permute-start(f32[4,64,128]{2,1,0:T(8,128)} %pad_maximum_fusion.4), channel_id=1, source_target_pairs={{0,18},{1,19},{2,16},{3,17},{4,22},{5,23},{6,20},{7,21},{8,26},{9,... | collective-permute-start | bytes 393224 | tf_op jit(solution)/shard_map/ppermute | solution.py:423
  66.5 5.9 %collective-permute-start.21 = (f32[64,128]{1,0:T(8,128)S(1)}, f32[64,128]{1,0:T(8,128)S(1)}, u32[]{:S(2)}, u32[]{:S(2)}) collective-permute-start(f32[64,128]{1,0:T(8,128)S(1)} %get-tuple-element.88), channel_id=1, source_target_pairs={{0,4},{1,5},{2,6},{3,7},{4,8},{5,9},{6,10},{7,11},{8,12},{9,13},{1... | collective-permute-start | bytes 98312 | tf_op jit(solution)/shard_map/ppermute | solution.py:433
  68.3 4.6 %collective-permute-start.23 = (f32[64,128]{1,0:T(8,128)S(1)}, f32[64,128]{1,0:T(8,128)S(1)}, u32[]{:S(2)}, u32[]{:S(2)}) collective-permute-start(f32[64,128]{1,0:T(8,128)S(1)} %get-tuple-element.89), channel_id=1, source_target_pairs={{0,12},{1,13},{2,14},{3,15},{4,0},{5,1},{6,2},{7,3},{8,4},{9,5},{1... | collective-permute-start | bytes 98312 | tf_op jit(solution)/shard_map/ppermute | solution.py:433
  70.4 4.8 %collective-permute-start.22 = (f32[64,128]{1,0:T(8,128)S(1)}, f32[64,128]{1,0:T(8,128)S(1)}, u32[]{:S(2)}, u32[]{:S(2)}) collective-permute-start(f32[64,128]{1,0:T(8,128)S(1)} %get-tuple-element.90), channel_id=1, source_target_pairs={{0,8},{1,9},{2,10},{3,11},{4,12},{5,13},{6,14},{7,15},{8,0},{9,1},... | collective-permute-start | bytes 98312 | tf_op jit(solution)/shard_map/ppermute | solution.py:433

commit v3 on v2

--- a/solution.py
+++ b/solution.py
@@ -465,8 +465,8 @@
     side = jnp.arange(2).reshape(2, 1, 1, 1)
     chunks, hops, last = range(plan.chunks), plan.groups - 1, plan.chunks - 1
 
-    kept, from_core, given, terms = [], [], [], []
-    total, from_chip, group_state = [], [], []
+    kept, from_core, given = [], [], []
+    total, from_chip = [], []
     for chunk in chunks:
         matrices = after(maps, given[-1]) if chunk else maps
         sent, kept_here, given_here = block_states(plan, chunk, rows, matrices)
@@ -476,8 +476,11 @@
         given.append(given_here)
         total.append(kept_here[0] + from_core[chunk][0])
         from_chip.append(swap_chip(plan, given_here))
-        group_state.append(total[chunk] + from_chip[chunk])
-    terms.append(inner(plan, 0, rows, after(maps, given[last])))
+    ready = [given[-1]] * last + [sent]
+    terms = [inner(plan, chunk, rows, after(maps, ready[chunk])) for chunk in chunks]
+    if last:
+        from_chip[0] = after(from_chip[0], *terms[last])
+    group_state = [total[chunk] + from_chip[chunk] for chunk in chunks]
 
     def for_other_chip(chunk, before):
         return before + jnp.where(side == chip, total[chunk], 0.0)
@@ -504,10 +507,8 @@
                 send = jnp.where(group == hop, group_state[chunk][0], group_state[chunk][1])
                 if hop:
                     send = send + got[chunk][-1]
-                if chunk and hop == 1:
-                    terms.append(inner(plan, last, rows, after(maps, behind)))
                 if chunk:
-                    behind = send = after(send, ahead, *(terms[1] if hop == hops - 1 else ()))
+                    behind = send = after(send, ahead)
                 elif last:
                     ahead = send = after(send, *(terms[0] if hop == 1 else (behind,)))
                 got[chunk].append(chain_swap(plan, send, hop))
@@ -516,8 +517,6 @@
         before[last] = select_group(plan, got[last])
         down[last] = swap_chip(plan, for_other_chip(last, before[last]))
 
-    if len(terms) < plan.chunks:
-        terms.append(inner(plan, last, rows, maps))
     halves, done = [], ()
     for chunk in chunks:
         states = [before[chunk] + jnp.where(side != chip, from_chip[chunk], 0.0), down[chunk]]
@@ -529,7 +528,8 @@
             states[3] = after(states[3], *halves)
         for_mate, own = maps_term(plan, states, from_core[chunk], *terms[chunk])
         halves.append(own + swap_core(plan, for_mate))
-        done = output_rows(plan, chunk, rows, maps, states, from_core[chunk], done)
+        matrices = after(maps, for_mate)
+        done = output_rows(plan, chunk, rows, matrices, states, from_core[chunk], done)
     plane = after(plane_sums(plan, halves), *done)
     query_grad, key_grad, value_grad = done
     maps_grad = group_sum(plan, plane) * plan.norm

time: 76.1 us -> 73.6 us (0.967)
  starting transfers between devices: 24.8 us -> 23.6 us
  waiting for transfers between devices: 23.7 us -> 22.5 us
    ppermute x6, waiting for transfers between devices: 6.08 us -> 4.4 us  [chain_swap(): return lax.ppermute(state, 'context', steps)]
    ppermute x3, starting transfers between devices: 5.05 us -> 3.76 us  [group_sum(): result = result + lax.ppermute(sent, 'context', steps)]
    ppermute x3, waiting for transfers between devices: 3.64 us -> 4.48 us  [group_sum(): result = result + lax.ppermute(sent, 'context', steps)]
  transfers between devices with their start and end apart: 24 -> 24, of which waited for: 14 -> 14; matrix products, arithmetic and copies ran while one was open for 2% -> 2% of each run, Pallas kernels for 25% -> 26%
where the time goes in v3:
time: 73.6 us; the launch traced here: 73.3 us
  starting transfers between devices  23.6 us (32%)
  Pallas kernels  22.8 us (31%)
  waiting for transfers between devices  22.5 us (31%)
  other arithmetic  3.15 us (4%)
  between operations  1.03 us (1%)
    pallas_call x8, Pallas kernels, call(): pl.pallas_call(body, out_shape=shapes, in_specs=specs(len(operands), near...  22.8 us
    ppermute x6, starting transfers between devices, chain_swap(): return lax.ppermute(state, 'context', steps)  8.69 us
    ppermute x4, waiting for transfers between devices, swap_chip(): lax.ppermute(state, 'context', [(i, i ^ 2) for i in range(plan.ranks)])  7.96 us
    ppermute x4, starting transfers between devices, swap_chip(): lax.ppermute(state, 'context', [(i, i ^ 2) for i in range(plan.ranks)])  6.13 us
    ppermute x8, waiting for transfers between devices, swap_core(): lax.ppermute(state, 'context', [(i, i ^ 1) for i in range(plan.ranks)])  4.81 us
    ppermute x3, waiting for transfers between devices, group_sum(): result = result + lax.ppermute(sent, 'context', steps)  4.48 us
    ppermute x6, waiting for transfers between devices, chain_swap(): return lax.ppermute(state, 'context', steps)  4.4 us
    ppermute x3, starting transfers between devices, group_sum(): result = result + lax.ppermute(sent, 'context', steps)  3.76 us
  transfers between devices with their start and end apart: 24, of which 14 were waited for; matrix products, arithmetic and copies ran while one was open for 2% of the time, Pallas kernels for 26%

profile of v3, /device:TPU:0, one launch (start us, length us, event | category | flops | bytes accessed | tf_op | source)
XLA Modules:
  0.0 73.3 jit_solution(11324741435180526850)
XLA Ops:
  0.6 3.0 %shard_map.84 = (f32[2,2,2,128,128]{4,3,2,1,0:T(8,128)S(1)}, f32[2,2,2,128,128]{4,3,2,1,0:T(8,128)}, f32[2,2,128,128]{3,2,1,0:T(8,128)S(1)}) custom-call(bf16[128,2048]{1,0:T(8,128)(2,1)} %bitcast.109, bf16[128,2048]{1,0:T(8,128)(2,1)} %bitcast.115, bf16[128,2048]{1,0:T(8,128)(2,1)} %bitcast.121, bf16[128,2048]{1,0:T(8,128)(2,1)} %bitcast.127, ...), custom_call_target="tpu_custom_call" | custom-call | flops 134217728 | bytes 3932160 | tf_op jit(solution)/shard_map/pallas_call | solution.py:59
  4.1 1.5 %collective-permute-done.refs_4_ = f32[2,2,2,128,128]{4,3,2,1,0:T(8,128)S(1)} collective-permute-done((f32[2,2,2,128,128]{4,3,2,1,0:T(8,128)S(1)}, f32[2,2,2,128,128]{4,3,2,1,0:T(8,128)S(1)}, u32[]{:S(2)}, u32[]{:S(2)}) %collective-permute-start) | collective-permute-done | bytes 524320 | tf_op jit(solution)/shard_map/ppermute | solution.py:375
  5.7 3.0 %collective-permute-start.3 = (f32[2,2,128,128]{3,2,1,0:T(8,128)S(1)}, f32[2,2,128,128]{3,2,1,0:T(8,128)S(1)}, u32[]{:S(2)}, u32[]{:S(2)}) collective-permute-start(f32[2,2,128,128]{3,2,1,0:T(8,128)S(1)} %fusion.3), channel_id=1, source_target_pairs={{0,2},{1,3},{2,0},{3,1},{4,6},{5,7},{6,4},{7,5},{8,10},{9,11},{10,... | collective-permute-start | bytes 786440 | tf_op jit(solution)/shard_map/ppermute | solution.py:379
  8.7 3.0 %shard_map.85 = (f32[2,2,2,128,128]{4,3,2,1,0:T(8,128)S(1)}, f32[2,2,2,128,128]{4,3,2,1,0:T(8,128)}, f32[2,2,128,128]{3,2,1,0:T(8,128)S(1)}) custom-call(bf16[128,2048]{1,0:T(8,128)(2,1)} %bitcast.110, bf16[128,2048]{1,0:T(8,128)(2,1)} %bitcast.116, bf16[128,2048]{1,0:T(8,128)(2,1)} %bitcast.122, bf16[128,2048]{1,0:T(8,128)(2,1)} %bitcast.128, ...), custom_call_target="tpu_custom_call" | custom-call | flops 134217728 | bytes 3932160 | tf_op jit(solution)/shard_map/pallas_call | solution.py:59
  11.8 3.6 %shard_map.86 = (f32[8,128,128]{2,1,0:T(8,128)}, bf16[2,8,128,128]{3,2,1,0:T(8,128)(2,1)}) custom-call(bf16[128,2048]{1,0:T(8,128)(2,1)} %bitcast.111, bf16[128,2048]{1,0:T(8,128)(2,1)} %bitcast.117, bf16[128,2048]{1,0:T(8,128)(2,1)} %bitcast.123, bf16[128,2048]{1,0:T(8,128)(2,1)} %bitcast.129, bf16[16,128,128]{2,1,0:T(8,128)(2,1)} %refs_9_.1), custom_call_target="tpu_custom_call" | custom-call | flops 301989888 | bytes 3670016 | tf_op jit(solution)/shard_map/pallas_call | solution.py:59
  15.5 1.8 %collective-permute-start.4 = (f32[2,128,128]{2,1,0:T(8,128)S(1)}, f32[2,128,128]{2,1,0:T(8,128)S(1)}, u32[]{:S(2)}, u32[]{:S(2)}) collective-permute-start(f32[2,128,128]{2,1,0:T(8,128)S(1)} %select_bitcast_fusion.4), channel_id=1, source_target_pairs={{0,4},{1,5},{2,6},{3,7},{4,0},{5,1},{6,2},{7,3},{8,12},{9,13},{10,... | collective-permute-start | bytes 393224 | tf_op jit(solution)/shard_map/ppermute | solution.py:389
  17.3 1.5 %collective-permute-start.2 = (f32[2,2,128,128]{3,2,1,0:T(8,128)S(1)}, f32[2,2,128,128]{3,2,1,0:T(8,128)S(1)}, u32[]{:S(2)}, u32[]{:S(2)}) collective-permute-start(f32[2,2,128,128]{3,2,1,0:T(8,128)S(1)} %fusion.1), channel_id=1, source_target_pairs={{0,2},{1,3},{2,0},{3,1},{4,6},{5,7},{6,4},{7,5},{8,10},{9,11},{10,... | collective-permute-start | bytes 786440 | tf_op jit(solution)/shard_map/ppermute | solution.py:379
  18.8 3.5 %shard_map.87 = (f32[8,128,128]{2,1,0:T(8,128)}, bf16[2,8,128,128]{3,2,1,0:T(8,128)(2,1)}) custom-call(bf16[128,2048]{1,0:T(8,128)(2,1)} %bitcast.112, bf16[128,2048]{1,0:T(8,128)(2,1)} %bitcast.118, bf16[128,2048]{1,0:T(8,128)(2,1)} %bitcast.124, bf16[128,2048]{1,0:T(8,128)(2,1)} %bitcast.130, bf16[16,128,128]{2,1,0:T(8,128)(2,1)} %refs_9_.1), custom_call_target="tpu_custom_call" | custom-call | flops 301989888 | bytes 3670016 | tf_op jit(solution)/shard_map/pallas_call | solution.py:59
  22.4 3.1 %collective-permute-done.2 = f32[2,2,128,128]{3,2,1,0:T(8,128)S(1)} collective-permute-done((f32[2,2,128,128]{3,2,1,0:T(8,128)S(1)}, f32[2,2,128,128]{3,2,1,0:T(8,128)S(1)}, u32[]{:S(2)}, u32[]{:S(2)}) %collective-permute-start.2) | collective-permute-done | bytes 262176 | tf_op jit(solution)/shard_map/ppermute | solution.py:379
  26.1 2.4 %collective-permute-start.8 = (f32[2,128,128]{2,1,0:T(8,128)S(1)}, f32[2,128,128]{2,1,0:T(8,128)S(1)}, u32[]{:S(2)}, u32[]{:S(2)}) collective-permute-start(f32[2,128,128]{2,1,0:T(8,128)S(1)} %bitcast_add_fusion), channel_id=1, source_target_pairs={{0,4},{1,5},{2,6},{3,7},{4,0},{5,1},{6,2},{7,3},{8,12},{9,13},{10,... | collective-permute-start | bytes 393224 | tf_op jit(solution)/shard_map/ppermute | solution.py:389
  28.6 3.1 %collective-permute-done.5 = f32[2,128,128]{2,1,0:T(8,128)S(1)} collective-permute-done((f32[2,128,128]{2,1,0:T(8,128)S(1)}, f32[2,128,128]{2,1,0:T(8,128)S(1)}, u32[]{:S(2)}, u32[]{:S(2)}) %collective-permute-start.5) | collective-permute-done | bytes 131104 | tf_op jit(solution)/shard_map/ppermute | solution.py:389
  31.8 1.3 %collective-permute-done.8 = f32[2,128,128]{2,1,0:T(8,128)S(1)} collective-permute-done((f32[2,128,128]{2,1,0:T(8,128)S(1)}, f32[2,128,128]{2,1,0:T(8,128)S(1)}, u32[]{:S(2)}, u32[]{:S(2)}) %collective-permute-start.8) | collective-permute-done | bytes 131104 | tf_op jit(solution)/shard_map/ppermute | solution.py:389
  33.2 0.8 %collective-permute-start.10 = (f32[2,2,128,128]{3,2,1,0:T(8,128)S(1)}, f32[2,2,128,128]{3,2,1,0:T(8,128)S(1)}, u32[]{:S(2)}, u32[]{:S(2)}) collective-permute-start(f32[2,2,128,128]{3,2,1,0:T(8,128)S(1)} %get-tuple-element.80), channel_id=1, source_target_pairs={{0,2},{1,3},{2,0},{3,1},{4,6},{5,7},{6,4},{7,5},{8,10},{9,11},{10,... | collective-permute-start | bytes 786440 | tf_op jit(solution)/shard_map/ppermute | solution.py:379
  34.1 3.8 %collective-permute-start.9 = (f32[2,128,128]{2,1,0:T(8,128)S(1)}, f32[2,128,128]{2,1,0:T(8,128)S(1)}, u32[]{:S(2)}, u32[]{:S(2)}) collective-permute-start(f32[2,128,128]{2,1,0:T(8,128)S(1)} %bitcast_add_fusion.3), channel_id=1, source_target_pairs={{0,4},{1,5},{2,6},{3,7},{4,0},{5,1},{6,2},{7,3},{8,12},{9,13},{10,... | collective-permute-start | bytes 393224 | tf_op jit(solution)/shard_map/ppermute | solution.py:389
  37.9 2.8 %collective-permute-done.10.refs_1_ = f32[2,2,128,128]{3,2,1,0:T(8,128)S(1)} collective-permute-done((f32[2,2,128,128]{3,2,1,0:T(8,128)S(1)}, f32[2,2,128,128]{3,2,1,0:T(8,128)S(1)}, u32[]{:S(2)}, u32[]{:S(2)}) %collective-permute-start.10) | collective-permute-done | bytes 262176 | tf_op jit(solution)/shard_map/ppermute | solution.py:379
  41.1 0.8 %collective-permute-start.11 = (f32[2,2,128,128]{3,2,1,0:T(8,128)S(1)}, f32[2,2,128,128]{3,2,1,0:T(8,128)S(1)}, u32[]{:S(2)}, u32[]{:S(2)}) collective-permute-start(f32[2,2,128,128]{3,2,1,0:T(8,128)S(1)} %get-tuple-element.81), channel_id=1, source_target_pairs={{0,2},{1,3},{2,0},{3,1},{4,6},{5,7},{6,4},{7,5},{8,10},{9,11},{10,... | collective-permute-start | bytes 786440 | tf_op jit(solution)/shard_map/ppermute | solution.py:379
  42.4 0.7 shard_map.88
  43.6 4.2 %shard_map.89 = (bf16[128,2048]{1,0:T(8,128)(2,1)}, bf16[128,2048]{1,0:T(8,128)(2,1)}, bf16[128,2048]{1,0:T(8,128)(2,1)}) custom-call(f32[2,2,128,128]{3,2,1,0:T(8,128)S(1)} %get-tuple-element.77.refs_0_, f32[2,2,128,128]{3,2,1,0:T(8,128)S(1)} %collective-permute-done.10.refs_1_, f32[2,2,128,128]{3,2,1,0:T(8,128)S(1)} %collective-permute-done.13.refs_2_, ...), custom_call_target="tpu_custom_call" | custom-call | flops 4026531 | bytes 57671 | tf_op jit(solution)/shard_map/pallas_call | solution.py:59
  47.8 2.1 %collective-permute-done.11.refs_1_ = f32[2,2,128,128]{3,2,1,0:T(8,128)S(1)} collective-permute-done((f32[2,2,128,128]{3,2,1,0:T(8,128)S(1)}, f32[2,2,128,128]{3,2,1,0:T(8,128)S(1)}, u32[]{:S(2)}, u32[]{:S(2)}) %collective-permute-start.11) | collective-permute-done | bytes 262176 | tf_op jit(solution)/shard_map/ppermute | solution.py:379
  50.1 1.5 %collective-permute-done.15.refs_3_ = f32[2,2,128,128]{3,2,1,0:T(8,128)S(1)} collective-permute-done((f32[2,2,128,128]{3,2,1,0:T(8,128)S(1)}, f32[2,2,128,128]{3,2,1,0:T(8,128)S(1)}, u32[]{:S(2)}, u32[]{:S(2)}) %collective-permute-start.15) | collective-permute-done | bytes 262176 | tf_op jit(solution)/shard_map/ppermute | solution.py:375
  51.6 0.7 shard_map.90
  52.5 1.5 %collective-permute-done.17 = f32[8,64,128]{2,1,0:T(8,128)} collective-permute-done((f32[8,64,128]{2,1,0:T(8,128)S(1)}, f32[8,64,128]{2,1,0:T(8,128)}, u32[]{:S(2)}, u32[]{:S(2)}) %collective-permute-start.17) | collective-permute-done | bytes 262176 | tf_op jit(solution)/shard_map/ppermute | solution.py:375
  54.1 1.0 %add.235 = f32[8,64,128]{2,1,0:T(8,128)S(1)} add(f32[8,64,128]{2,1,0:T(8,128)S(1)} %get-tuple-element.74, f32[8,64,128]{2,1,0:T(8,128)} %collective-permute-done.17) | non-fusion elementwise | flops 65536 | bytes 786432 | tf_op jit(solution)/shard_map/add | solution.py:530
  55.1 1.7 %collective-permute-start.20 = (f32[4,64,128]{2,1,0:T(8,128)S(1)}, f32[4,64,128]{2,1,0:T(8,128)S(1)}, u32[]{:S(2)}, u32[]{:S(2)}) collective-permute-start(f32[4,64,128]{2,1,0:T(8,128)S(1)} %pad_maximum_fusion.4), channel_id=1, source_target_pairs={{0,18},{1,19},{2,16},{3,17},{4,22},{5,23},{6,20},{7,21},{8,26},{9,... | collective-permute-start | bytes 393224 | tf_op jit(solution)/shard_map/ppermute | solution.py:423
  57.4 0.7 pad_maximum_fusion.2
  58.1 1.3 %collective-permute-start.18 = (f32[4,64,128]{2,1,0:T(8,128)}, f32[4,64,128]{2,1,0:T(8,128)S(1)}, u32[]{:S(2)}, u32[]{:S(2)}) collective-permute-start(f32[4,64,128]{2,1,0:T(8,128)} %pad_maximum_fusion.2), channel_id=1, source_target_pairs={{0,2},{1,3},{2,0},{3,1},{4,6},{5,7},{6,4},{7,5},{8,10},{9,11},{10,... | collective-permute-start | bytes 393224 | tf_op jit(solution)/shard_map/ppermute | solution.py:423
  59.4 4.2 %shard_map.91 = (bf16[128,2048]{1,0:T(8,128)(2,1)}, bf16[128,2048]{1,0:T(8,128)(2,1)}, bf16[128,2048]{1,0:T(8,128)(2,1)}) custom-call(f32[2,2,128,128]{3,2,1,0:T(8,128)S(1)} %get-tuple-element.79.refs_0_, f32[2,2,128,128]{3,2,1,0:T(8,128)S(1)} %collective-permute-done.11.refs_1_, ...), custom_call_target="tpu_custom_call", output_to_operand_aliasing={{0}: (10, {}), {1}: (11, {}), {2}: (12, {})} | custom-call | flops 4026531 | bytes 73400 | tf_op jit(solution)/shard_map/pallas_call | solution.py:59
  63.7 0.7 collective-permute-done.18
  64.5 2.5 %collective-permute-start.23 = (f32[64,128]{1,0:T(8,128)S(1)}, f32[64,128]{1,0:T(8,128)S(1)}, u32[]{:S(2)}, u32[]{:S(2)}) collective-permute-start(f32[64,128]{1,0:T(8,128)S(1)} %get-tuple-element.95), channel_id=1, source_target_pairs={{0,12},{1,13},{2,14},{3,15},{4,0},{5,1},{6,2},{7,3},{8,4},{9,5},{1... | collective-permute-start | bytes 98312 | tf_op jit(solution)/shard_map/ppermute | solution.py:433
  67.0 1.2 %collective-permute-start.21 = (f32[64,128]{1,0:T(8,128)S(1)}, f32[64,128]{1,0:T(8,128)S(1)}, u32[]{:S(2)}, u32[]{:S(2)}) collective-permute-start(f32[64,128]{1,0:T(8,128)S(1)} %get-tuple-element.94), channel_id=1, source_target_pairs={{0,4},{1,5},{2,6},{3,7},{4,8},{5,9},{6,10},{7,11},{8,12},{9,13},{1... | collective-permute-start | bytes 98312 | tf_op jit(solution)/shard_map/ppermute | solution.py:433
  68.6 3.2 %collective-permute-done.22 = f32[64,128]{1,0:T(8,128)S(1)} collective-permute-done((f32[64,128]{1,0:T(8,128)S(1)}, f32[64,128]{1,0:T(8,128)S(1)}, u32[]{:S(2)}, u32[]{:S(2)}) %collective-permute-start.22) | collective-permute-done | bytes 32800 | tf_op jit(solution)/shard_map/ppermute | solution.py:433
  71.8 0.9 %collective-permute-done.21 = f32[64,128]{1,0:T(8,128)S(1)} collective-permute-done((f32[64,128]{1,0:T(8,128)S(1)}, f32[64,128]{1,0:T(8,128)S(1)}, u32[]{:S(2)}, u32[]{:S(2)}) %collective-permute-start.21) | collective-permute-done | bytes 32800 | tf_op jit(solution)/shard_map/ppermute | solution.py:433
  (68 shorter events, 5.2 us)
Async XLA Ops:
  3.6 2.0 %collective-permute-start = (f32[2,2,2,128,128]{4,3,2,1,0:T(8,128)S(1)}, f32[2,2,2,128,128]{4,3,2,1,0:T(8,128)S(1)}, u32[]{:S(2)}, u32[]{:S(2)}) collective-permute-start(f32[2,2,2,128,128]{4,3,2,1,0:T(8,128)S(1)} %get-tuple-element.41), channel_id=1, source_target_pairs={{0,1},{1,0},{2,3},{3,2},{4,5},{5,4},{6,7},{7,6},{8,9},{9,8},{10,11... | collective-permute-start | bytes 1572872 | tf_op jit(solution)/shard_map/ppermute | solution.py:375
  5.7 9.7 %collective-permute-start.3 = (f32[2,2,128,128]{3,2,1,0:T(8,128)S(1)}, f32[2,2,128,128]{3,2,1,0:T(8,128)S(1)}, u32[]{:S(2)}, u32[]{:S(2)}) collective-permute-start(f32[2,2,128,128]{3,2,1,0:T(8,128)S(1)} %fusion.3), channel_id=1, source_target_pairs={{0,2},{1,3},{2,0},{3,1},{4,6},{5,7},{6,4},{7,5},{8,10},{9,11},{10,... | collective-permute-start | bytes 786440 | tf_op jit(solution)/shard_map/ppermute | solution.py:379
  11.6 3.8 %collective-permute-start.1 = (f32[2,2,2,128,128]{4,3,2,1,0:T(8,128)S(1)}, f32[2,2,2,128,128]{4,3,2,1,0:T(8,128)S(1)}, u32[]{:S(2)}, u32[]{:S(2)}) collective-permute-start(f32[2,2,2,128,128]{4,3,2,1,0:T(8,128)S(1)} %get-tuple-element.44), channel_id=1, source_target_pairs={{0,1},{1,0},{2,3},{3,2},{4,5},{5,4},{6,7},{7,6},{8,9},{9,8},{10,11... | collective-permute-start | bytes 1572872 | tf_op jit(solution)/shard_map/ppermute | solution.py:375
  11.8 3.6 %copy-start.7 = (f32[2,2,2,128,128]{4,3,2,1,0:T(8,128)S(1)}, f32[2,2,2,128,128]{4,3,2,1,0:T(8,128)}, u32[]{:S(2)}) copy-start(f32[2,2,2,128,128]{4,3,2,1,0:T(8,128)} %get-tuple-element.46) | copy-start | bytes 1572868
  15.5 6.8 %collective-permute-start.4 = (f32[2,128,128]{2,1,0:T(8,128)S(1)}, f32[2,128,128]{2,1,0:T(8,128)S(1)}, u32[]{:S(2)}, u32[]{:S(2)}) collective-permute-start(f32[2,128,128]{2,1,0:T(8,128)S(1)} %select_bitcast_fusion.4), channel_id=1, source_target_pairs={{0,4},{1,5},{2,6},{3,7},{4,0},{5,1},{6,2},{7,3},{8,12},{9,13},{10,... | collective-permute-start | bytes 393224 | tf_op jit(solution)/shard_map/ppermute | solution.py:389
  17.3 8.3 %collective-permute-start.2 = (f32[2,2,128,128]{3,2,1,0:T(8,128)S(1)}, f32[2,2,128,128]{3,2,1,0:T(8,128)S(1)}, u32[]{:S(2)}, u32[]{:S(2)}) collective-permute-start(f32[2,2,128,128]{3,2,1,0:T(8,128)S(1)} %fusion.1), channel_id=1, source_target_pairs={{0,2},{1,3},{2,0},{3,1},{4,6},{5,7},{6,4},{7,5},{8,10},{9,11},{10,... | collective-permute-start | bytes 786440 | tf_op jit(solution)/shard_map/ppermute | solution.py:379
  22.3 3.3 %copy-start.6 = (f32[2,2,2,128,128]{4,3,2,1,0:T(8,128)S(1)}, f32[2,2,2,128,128]{4,3,2,1,0:T(8,128)}, u32[]{:S(2)}) copy-start(f32[2,2,2,128,128]{4,3,2,1,0:T(8,128)} %get-tuple-element.43) | copy-start | bytes 1572868
  22.3 3.8 %collective-permute-start.6 = (f32[2,128,128]{2,1,0:T(8,128)S(1)}, f32[2,128,128]{2,1,0:T(8,128)S(1)}, u32[]{:S(2)}, u32[]{:S(2)}) collective-permute-start(f32[2,128,128]{2,1,0:T(8,128)S(1)} %bitcast_add_fusion.1), channel_id=1, source_target_pairs={{0,1},{1,0},{2,3},{3,2},{4,8},{5,9},{6,10},{7,11},{8,4},{9,5},{10,... | collective-permute-start | bytes 393224 | tf_op jit(solution)/shard_map/ppermute | solution.py:389
  25.6 6.1 %collective-permute-start.5 = (f32[2,128,128]{2,1,0:T(8,128)S(1)}, f32[2,128,128]{2,1,0:T(8,128)S(1)}, u32[]{:S(2)}, u32[]{:S(2)}) collective-permute-start(f32[2,128,128]{2,1,0:T(8,128)S(1)} %select_bitcast_fusion.5), channel_id=1, source_target_pairs={{0,4},{1,5},{2,6},{3,7},{4,0},{5,1},{6,2},{7,3},{8,12},{9,13},{10,... | collective-permute-start | bytes 393224 | tf_op jit(solution)/shard_map/ppermute | solution.py:389
  26.1 6.9 %collective-permute-start.8 = (f32[2,128,128]{2,1,0:T(8,128)S(1)}, f32[2,128,128]{2,1,0:T(8,128)S(1)}, u32[]{:S(2)}, u32[]{:S(2)}) collective-permute-start(f32[2,128,128]{2,1,0:T(8,128)S(1)} %bitcast_add_fusion), channel_id=1, source_target_pairs={{0,4},{1,5},{2,6},{3,7},{4,0},{5,1},{6,2},{7,3},{8,12},{9,13},{10,... | collective-permute-start | bytes 393224 | tf_op jit(solution)/shard_map/ppermute | solution.py:389
  31.7 2.4 %collective-permute-start.7 = (f32[2,128,128]{2,1,0:T(8,128)S(1)}, f32[2,128,128]{2,1,0:T(8,128)S(1)}, u32[]{:S(2)}, u32[]{:S(2)}) collective-permute-start(f32[2,128,128]{2,1,0:T(8,128)S(1)} %bitcast_add_fusion.2), channel_id=1, source_target_pairs={{0,1},{1,0},{2,3},{3,2},{4,8},{5,9},{6,10},{7,11},{8,4},{9,5},{10,... | collective-permute-start | bytes 393224 | tf_op jit(solution)/shard_map/ppermute | solution.py:389
  33.2 7.5 %collective-permute-start.10 = (f32[2,2,128,128]{3,2,1,0:T(8,128)S(1)}, f32[2,2,128,128]{3,2,1,0:T(8,128)S(1)}, u32[]{:S(2)}, u32[]{:S(2)}) collective-permute-start(f32[2,2,128,128]{3,2,1,0:T(8,128)S(1)} %get-tuple-element.80), channel_id=1, source_target_pairs={{0,2},{1,3},{2,0},{3,1},{4,6},{5,7},{6,4},{7,5},{8,10},{9,11},{10,... | collective-permute-start | bytes 786440 | tf_op jit(solution)/shard_map/ppermute | solution.py:379
  34.1 8.1 %collective-permute-start.13 = (f32[2,2,128,128]{3,2,1,0:T(8,128)S(1)}, f32[2,2,128,128]{3,2,1,0:T(8,128)S(1)}, u32[]{:S(2)}, u32[]{:S(2)}) collective-permute-start(f32[2,2,128,128]{3,2,1,0:T(8,128)S(1)} %get-tuple-element.76), channel_id=1, source_target_pairs={{0,1},{1,0},{2,3},{3,2},{4,5},{5,4},{6,7},{7,6},{8,9},{9,8},{10,11... | collective-permute-start | bytes 786440 | tf_op jit(solution)/shard_map/ppermute | solution.py:375
  34.1 6.8 %collective-permute-start.9 = (f32[2,128,128]{2,1,0:T(8,128)S(1)}, f32[2,128,128]{2,1,0:T(8,128)S(1)}, u32[]{:S(2)}, u32[]{:S(2)}) collective-permute-start(f32[2,128,128]{2,1,0:T(8,128)S(1)} %bitcast_add_fusion.3), channel_id=1, source_target_pairs={{0,4},{1,5},{2,6},{3,7},{4,0},{5,1},{6,2},{7,3},{8,12},{9,13},{10,... | collective-permute-start | bytes 393224 | tf_op jit(solution)/shard_map/ppermute | solution.py:389
  40.8 1.6 %collective-permute-start.14 = (f32[2,2,128,128]{3,2,1,0:T(8,128)S(1)}, f32[2,2,128,128]{3,2,1,0:T(8,128)S(1)}, u32[]{:S(2)}, u32[]{:S(2)}) collective-permute-start(f32[2,2,128,128]{3,2,1,0:T(8,128)S(1)} %fusion.5), channel_id=1, source_target_pairs={{0,1},{1,0},{2,3},{3,2},{4,5},{5,4},{6,7},{7,6},{8,9},{9,8},{10,11... | collective-permute-start | bytes 786440 | tf_op jit(solution)/shard_map/ppermute | solution.py:375
  41.0 1.5 %copy-start.4 = (f32[8,128,128]{2,1,0:T(8,128)S(1)}, f32[8,128,128]{2,1,0:T(8,128)}, u32[]{:S(2)}) copy-start(f32[8,128,128]{2,1,0:T(8,128)} %get-tuple-element.53.refs_5_) | copy-start | bytes 1572868
  41.0 1.5 %copy-start.5 = (bf16[2,8,128,128]{3,2,1,0:T(8,128)(2,1)S(1)}, bf16[2,8,128,128]{3,2,1,0:T(8,128)(2,1)}, u32[]{:S(2)}) copy-start(bf16[2,8,128,128]{3,2,1,0:T(8,128)(2,1)} %get-tuple-element.54.refs_6_) | copy-start | bytes 1572868
  41.1 8.8 %collective-permute-start.11 = (f32[2,2,128,128]{3,2,1,0:T(8,128)S(1)}, f32[2,2,128,128]{3,2,1,0:T(8,128)S(1)}, u32[]{:S(2)}, u32[]{:S(2)}) collective-permute-start(f32[2,2,128,128]{3,2,1,0:T(8,128)S(1)} %get-tuple-element.81), channel_id=1, source_target_pairs={{0,2},{1,3},{2,0},{3,1},{4,6},{5,7},{6,4},{7,5},{8,10},{9,11},{10,... | collective-permute-start | bytes 786440 | tf_op jit(solution)/shard_map/ppermute | solution.py:379
  42.0 7.9 %collective-permute-start.12 = (f32[2,2,128,128]{3,2,1,0:T(8,128)S(1)}, f32[2,2,128,128]{3,2,1,0:T(8,128)S(1)}, u32[]{:S(2)}, u32[]{:S(2)}) collective-permute-start(f32[2,2,128,128]{3,2,1,0:T(8,128)S(1)} %get-tuple-element.78), channel_id=1, source_target_pairs={{0,1},{1,0},{2,3},{3,2},{4,5},{5,4},{6,7},{7,6},{8,9},{9,8},{10,11... | collective-permute-start | bytes 786440 | tf_op jit(solution)/shard_map/ppermute | solution.py:375
  42.4 1.0 %copy-start = (bf16[1,128,2048]{2,1,0:T(8,128)(2,1)S(1)}, bf16[1,128,2048]{2,1,0:T(8,128)(2,1)}, u32[]{:S(2)}) copy-start(bf16[1,128,2048]{2,1,0:T(8,128)(2,1)} %param.5) | copy-start | bytes 1572868
  42.4 1.2 %copy-start.1 = (bf16[1,128,2048]{2,1,0:T(8,128)(2,1)S(1)}, bf16[1,128,2048]{2,1,0:T(8,128)(2,1)}, u32[]{:S(2)}) copy-start(bf16[1,128,2048]{2,1,0:T(8,128)(2,1)} %param.6) | copy-start | bytes 1572868
  43.2 6.9 %collective-permute-start.16 = (f32[8,64,128]{2,1,0:T(8,128)S(1)}, f32[8,64,128]{2,1,0:T(8,128)S(1)}, u32[]{:S(2)}, u32[]{:S(2)}) collective-permute-start(f32[8,64,128]{2,1,0:T(8,128)S(1)} %get-tuple-element.61), channel_id=1, source_target_pairs={{0,1},{1,0},{2,3},{3,2},{4,5},{5,4},{6,7},{7,6},{8,9},{9,8},{10,11... | collective-permute-start | bytes 786440 | tf_op jit(solution)/shard_map/ppermute | solution.py:375
  49.9 1.7 %copy-start.3 = (bf16[2,8,128,128]{3,2,1,0:T(8,128)(2,1)S(1)}, bf16[2,8,128,128]{3,2,1,0:T(8,128)(2,1)}, u32[]{:S(2)}) copy-start(bf16[2,8,128,128]{3,2,1,0:T(8,128)(2,1)} %get-tuple-element.49.refs_6_) | copy-start | bytes 1572868
  50.0 1.6 %copy-start.2 = (f32[8,128,128]{2,1,0:T(8,128)S(1)}, f32[8,128,128]{2,1,0:T(8,128)}, u32[]{:S(2)}) copy-start(f32[8,128,128]{2,1,0:T(8,128)} %get-tuple-element.48.refs_5_) | copy-start | bytes 1572868
  50.0 1.6 %collective-permute-start.15 = (f32[2,2,128,128]{3,2,1,0:T(8,128)S(1)}, f32[2,2,128,128]{3,2,1,0:T(8,128)S(1)}, u32[]{:S(2)}, u32[]{:S(2)}) collective-permute-start(f32[2,2,128,128]{3,2,1,0:T(8,128)S(1)} %fusion.4), channel_id=1, source_target_pairs={{0,1},{1,0},{2,3},{3,2},{4,5},{5,4},{6,7},{7,6},{8,9},{9,8},{10,11... | collective-permute-start | bytes 786440 | tf_op jit(solution)/shard_map/ppermute | solution.py:375
  52.3 1.7 %collective-permute-start.17 = (f32[8,64,128]{2,1,0:T(8,128)S(1)}, f32[8,64,128]{2,1,0:T(8,128)}, u32[]{:S(2)}, u32[]{:S(2)}) collective-permute-start(f32[8,64,128]{2,1,0:T(8,128)S(1)} %get-tuple-element.69), channel_id=1, source_target_pairs={{0,1},{1,0},{2,3},{3,2},{4,5},{5,4},{6,7},{7,6},{8,9},{9,8},{10,11... | collective-permute-start | bytes 786440 | tf_op jit(solution)/shard_map/ppermute | solution.py:375
  55.1 8.5 %collective-permute-start.20 = (f32[4,64,128]{2,1,0:T(8,128)S(1)}, f32[4,64,128]{2,1,0:T(8,128)S(1)}, u32[]{:S(2)}, u32[]{:S(2)}) collective-permute-start(f32[4,64,128]{2,1,0:T(8,128)S(1)} %pad_maximum_fusion.4), channel_id=1, source_target_pairs={{0,18},{1,19},{2,16},{3,17},{4,22},{5,23},{6,20},{7,21},{8,26},{9,... | collective-permute-start | bytes 393224 | tf_op jit(solution)/shard_map/ppermute | solution.py:423
  56.8 6.9 %collective-permute-start.19 = (f32[4,64,128]{2,1,0:T(8,128)S(1)}, f32[4,64,128]{2,1,0:T(8,128)S(1)}, u32[]{:S(2)}, u32[]{:S(2)}) collective-permute-start(f32[4,64,128]{2,1,0:T(8,128)S(1)} %pad_maximum_fusion.3), channel_id=1, source_target_pairs={{0,16},{1,17},{2,18},{3,19},{4,20},{5,21},{6,22},{7,23},{8,24},{9,... | collective-permute-start | bytes 393224 | tf_op jit(solution)/shard_map/ppermute | solution.py:423
  58.1 6.3 %collective-permute-start.18 = (f32[4,64,128]{2,1,0:T(8,128)}, f32[4,64,128]{2,1,0:T(8,128)S(1)}, u32[]{:S(2)}, u32[]{:S(2)}) collective-permute-start(f32[4,64,128]{2,1,0:T(8,128)} %pad_maximum_fusion.2), channel_id=1, source_target_pairs={{0,2},{1,3},{2,0},{3,1},{4,6},{5,7},{6,4},{7,5},{8,10},{9,11},{10,... | collective-permute-start | bytes 393224 | tf_op jit(solution)/shard_map/ppermute | solution.py:423
  64.5 4.1 %collective-permute-start.23 = (f32[64,128]{1,0:T(8,128)S(1)}, f32[64,128]{1,0:T(8,128)S(1)}, u32[]{:S(2)}, u32[]{:S(2)}) collective-permute-start(f32[64,128]{1,0:T(8,128)S(1)} %get-tuple-element.95), channel_id=1, source_target_pairs={{0,12},{1,13},{2,14},{3,15},{4,0},{5,1},{6,2},{7,3},{8,4},{9,5},{1... | collective-permute-start | bytes 98312 | tf_op jit(solution)/shard_map/ppermute | solution.py:433
  67.0 4.8 %collective-permute-start.22 = (f32[64,128]{1,0:T(8,128)S(1)}, f32[64,128]{1,0:T(8,128)S(1)}, u32[]{:S(2)}, u32[]{:S(2)}) collective-permute-start(f32[64,128]{1,0:T(8,128)S(1)} %get-tuple-element.96), channel_id=1, source_target_pairs={{0,8},{1,9},{2,10},{3,11},{4,12},{5,13},{6,14},{7,15},{8,0},{9,1},... | collective-permute-start | bytes 98312 | tf_op jit(solution)/shard_map/ppermute | solution.py:433
  67.0 5.7 %collective-permute-start.21 = (f32[64,128]{1,0:T(8,128)S(1)}, f32[64,128]{1,0:T(8,128)S(1)}, u32[]{:S(2)}, u32[]{:S(2)}) collective-permute-start(f32[64,128]{1,0:T(8,128)S(1)} %get-tuple-element.94), channel_id=1, source_target_pairs={{0,4},{1,5},{2,6},{3,7},{4,8},{5,9},{6,10},{7,11},{8,12},{9,13},{1... | collective-permute-start | bytes 98312 | tf_op jit(solution)/shard_map/ppermute | solution.py:433

commit v4 on v3

--- a/solution.py
+++ b/solution.py
@@ -427,9 +427,14 @@
 def group_sum(plan, plane):
     _, _, group = device_place()
     result = lax.dynamic_index_in_dim(plane, group, 0, keepdims=False)
+    in_pairs = plan.groups & (plan.groups - 1) == 0
     for turn in range(1, plan.groups):
-        steps = [(i, (i + 4 * turn) % plan.ranks) for i in range(plan.ranks)]
-        sent = lax.dynamic_index_in_dim(plane, (group + turn) % plan.groups, 0, keepdims=False)
+
+        def partner(place):
+            return place ^ turn if in_pairs else (place + turn) % plan.groups
+
+        steps = [(i, 4 * partner(i // 4) + i % 4) for i in range(plan.ranks)]
+        sent = lax.dynamic_index_in_dim(plane, partner(group), 0, keepdims=False)
         result = result + lax.ppermute(sent, "context", steps)
     return result
 

time: 73.6 us -> 72.8 us (0.989)
  waiting for transfers between devices: 22.5 us -> 20.9 us
    ppermute x3, waiting for transfers between devices: 4.48 us -> 2.9 us  [group_sum(): result = result + lax.ppermute(sent, 'context', steps)]
  transfers between devices with their start and end apart: 24 -> 24, of which waited for: 14 -> 13; matrix products, arithmetic and copies ran while one was open for 2% -> 2% of each run, Pallas kernels for 26% -> 26%
where the time goes in v4:
time: 72.8 us; the launch traced here: 72.5 us
  starting transfers between devices  24.3 us (33%)
  Pallas kernels  22.8 us (31%)
  waiting for transfers between devices  20.9 us (29%)
  other arithmetic  3.16 us (4%)
  between operations  1.03 us (1%)
    pallas_call x8, Pallas kernels, call(): pl.pallas_call(body, out_shape=shapes, in_specs=specs(len(operands), near...  22.8 us
    ppermute x6, starting transfers between devices, chain_swap(): return lax.ppermute(state, 'context', steps)  8.69 us
    ppermute x4, waiting for transfers between devices, swap_chip(): lax.ppermute(state, 'context', [(i, i ^ 2) for i in range(plan.ranks)])  7.96 us
    ppermute x4, starting transfers between devices, swap_chip(): lax.ppermute(state, 'context', [(i, i ^ 2) for i in range(plan.ranks)])  6.13 us
    ppermute x8, waiting for transfers between devices, swap_core(): lax.ppermute(state, 'context', [(i, i ^ 1) for i in range(plan.ranks)])  4.81 us
    ppermute x3, starting transfers between devices, group_sum(): result = result + lax.ppermute(sent, 'context', steps)  4.45 us
    ppermute x6, waiting for transfers between devices, chain_swap(): return lax.ppermute(state, 'context', steps)  4.4 us
    ppermute x3, starting transfers between devices, plane_sums(): plane = plane + lax.ppermute(sent, ('dp', 'context'), steps)  3.62 us
  transfers between devices with their start and end apart: 24, of which 13 were waited for; matrix products, arithmetic and copies ran while one was open for 2% of the time, Pallas kernels for 26%

profile of v4, /device:TPU:0, one launch (start us, length us, event | category | flops | bytes accessed | tf_op | source)
XLA Modules:
  0.0 72.5 jit_solution(4198216554803180893)
XLA Ops:
  0.6 3.0 %shard_map.84 = (f32[2,2,2,128,128]{4,3,2,1,0:T(8,128)S(1)}, f32[2,2,2,128,128]{4,3,2,1,0:T(8,128)}, f32[2,2,128,128]{3,2,1,0:T(8,128)S(1)}) custom-call(bf16[128,2048]{1,0:T(8,128)(2,1)} %bitcast.109, bf16[128,2048]{1,0:T(8,128)(2,1)} %bitcast.115, bf16[128,2048]{1,0:T(8,128)(2,1)} %bitcast.121, bf16[128,2048]{1,0:T(8,128)(2,1)} %bitcast.127, ...), custom_call_target="tpu_custom_call" | custom-call | flops 134217728 | bytes 3932160 | tf_op jit(solution)/shard_map/pallas_call | solution.py:59
  4.1 1.5 %collective-permute-done.refs_4_ = f32[2,2,2,128,128]{4,3,2,1,0:T(8,128)S(1)} collective-permute-done((f32[2,2,2,128,128]{4,3,2,1,0:T(8,128)S(1)}, f32[2,2,2,128,128]{4,3,2,1,0:T(8,128)S(1)}, u32[]{:S(2)}, u32[]{:S(2)}) %collective-permute-start) | collective-permute-done | bytes 524320 | tf_op jit(solution)/shard_map/ppermute | solution.py:375
  5.7 3.0 %collective-permute-start.3 = (f32[2,2,128,128]{3,2,1,0:T(8,128)S(1)}, f32[2,2,128,128]{3,2,1,0:T(8,128)S(1)}, u32[]{:S(2)}, u32[]{:S(2)}) collective-permute-start(f32[2,2,128,128]{3,2,1,0:T(8,128)S(1)} %fusion.3), channel_id=1, source_target_pairs={{0,2},{1,3},{2,0},{3,1},{4,6},{5,7},{6,4},{7,5},{8,10},{9,11},{10,... | collective-permute-start | bytes 786440 | tf_op jit(solution)/shard_map/ppermute | solution.py:379
  8.7 3.0 %shard_map.85 = (f32[2,2,2,128,128]{4,3,2,1,0:T(8,128)S(1)}, f32[2,2,2,128,128]{4,3,2,1,0:T(8,128)}, f32[2,2,128,128]{3,2,1,0:T(8,128)S(1)}) custom-call(bf16[128,2048]{1,0:T(8,128)(2,1)} %bitcast.110, bf16[128,2048]{1,0:T(8,128)(2,1)} %bitcast.116, bf16[128,2048]{1,0:T(8,128)(2,1)} %bitcast.122, bf16[128,2048]{1,0:T(8,128)(2,1)} %bitcast.128, ...), custom_call_target="tpu_custom_call" | custom-call | flops 134217728 | bytes 3932160 | tf_op jit(solution)/shard_map/pallas_call | solution.py:59
  11.8 3.6 %shard_map.86 = (f32[8,128,128]{2,1,0:T(8,128)}, bf16[2,8,128,128]{3,2,1,0:T(8,128)(2,1)}) custom-call(bf16[128,2048]{1,0:T(8,128)(2,1)} %bitcast.111, bf16[128,2048]{1,0:T(8,128)(2,1)} %bitcast.117, bf16[128,2048]{1,0:T(8,128)(2,1)} %bitcast.123, bf16[128,2048]{1,0:T(8,128)(2,1)} %bitcast.129, bf16[16,128,128]{2,1,0:T(8,128)(2,1)} %refs_9_.1), custom_call_target="tpu_custom_call" | custom-call | flops 301989888 | bytes 3670016 | tf_op jit(solution)/shard_map/pallas_call | solution.py:59
  15.5 1.8 %collective-permute-start.4 = (f32[2,128,128]{2,1,0:T(8,128)S(1)}, f32[2,128,128]{2,1,0:T(8,128)S(1)}, u32[]{:S(2)}, u32[]{:S(2)}) collective-permute-start(f32[2,128,128]{2,1,0:T(8,128)S(1)} %select_bitcast_fusion.4), channel_id=1, source_target_pairs={{0,4},{1,5},{2,6},{3,7},{4,0},{5,1},{6,2},{7,3},{8,12},{9,13},{10,... | collective-permute-start | bytes 393224 | tf_op jit(solution)/shard_map/ppermute | solution.py:389
  17.3 1.5 %collective-permute-start.2 = (f32[2,2,128,128]{3,2,1,0:T(8,128)S(1)}, f32[2,2,128,128]{3,2,1,0:T(8,128)S(1)}, u32[]{:S(2)}, u32[]{:S(2)}) collective-permute-start(f32[2,2,128,128]{3,2,1,0:T(8,128)S(1)} %fusion.1), channel_id=1, source_target_pairs={{0,2},{1,3},{2,0},{3,1},{4,6},{5,7},{6,4},{7,5},{8,10},{9,11},{10,... | collective-permute-start | bytes 786440 | tf_op jit(solution)/shard_map/ppermute | solution.py:379
  18.8 3.5 %shard_map.87 = (f32[8,128,128]{2,1,0:T(8,128)}, bf16[2,8,128,128]{3,2,1,0:T(8,128)(2,1)}) custom-call(bf16[128,2048]{1,0:T(8,128)(2,1)} %bitcast.112, bf16[128,2048]{1,0:T(8,128)(2,1)} %bitcast.118, bf16[128,2048]{1,0:T(8,128)(2,1)} %bitcast.124, bf16[128,2048]{1,0:T(8,128)(2,1)} %bitcast.130, bf16[16,128,128]{2,1,0:T(8,128)(2,1)} %refs_9_.1), custom_call_target="tpu_custom_call" | custom-call | flops 301989888 | bytes 3670016 | tf_op jit(solution)/shard_map/pallas_call | solution.py:59
  22.4 3.1 %collective-permute-done.2 = f32[2,2,128,128]{3,2,1,0:T(8,128)S(1)} collective-permute-done((f32[2,2,128,128]{3,2,1,0:T(8,128)S(1)}, f32[2,2,128,128]{3,2,1,0:T(8,128)S(1)}, u32[]{:S(2)}, u32[]{:S(2)}) %collective-permute-start.2) | collective-permute-done | bytes 262176 | tf_op jit(solution)/shard_map/ppermute | solution.py:379
  26.1 2.4 %collective-permute-start.8 = (f32[2,128,128]{2,1,0:T(8,128)S(1)}, f32[2,128,128]{2,1,0:T(8,128)S(1)}, u32[]{:S(2)}, u32[]{:S(2)}) collective-permute-start(f32[2,128,128]{2,1,0:T(8,128)S(1)} %bitcast_add_fusion), channel_id=1, source_target_pairs={{0,4},{1,5},{2,6},{3,7},{4,0},{5,1},{6,2},{7,3},{8,12},{9,13},{10,... | collective-permute-start | bytes 393224 | tf_op jit(solution)/shard_map/ppermute | solution.py:389
  28.6 3.1 %collective-permute-done.5 = f32[2,128,128]{2,1,0:T(8,128)S(1)} collective-permute-done((f32[2,128,128]{2,1,0:T(8,128)S(1)}, f32[2,128,128]{2,1,0:T(8,128)S(1)}, u32[]{:S(2)}, u32[]{:S(2)}) %collective-permute-start.5) | collective-permute-done | bytes 131104 | tf_op jit(solution)/shard_map/ppermute | solution.py:389
  31.8 1.3 %collective-permute-done.8 = f32[2,128,128]{2,1,0:T(8,128)S(1)} collective-permute-done((f32[2,128,128]{2,1,0:T(8,128)S(1)}, f32[2,128,128]{2,1,0:T(8,128)S(1)}, u32[]{:S(2)}, u32[]{:S(2)}) %collective-permute-start.8) | collective-permute-done | bytes 131104 | tf_op jit(solution)/shard_map/ppermute | solution.py:389
  33.2 0.8 %collective-permute-start.10 = (f32[2,2,128,128]{3,2,1,0:T(8,128)S(1)}, f32[2,2,128,128]{3,2,1,0:T(8,128)S(1)}, u32[]{:S(2)}, u32[]{:S(2)}) collective-permute-start(f32[2,2,128,128]{3,2,1,0:T(8,128)S(1)} %get-tuple-element.80), channel_id=1, source_target_pairs={{0,2},{1,3},{2,0},{3,1},{4,6},{5,7},{6,4},{7,5},{8,10},{9,11},{10,... | collective-permute-start | bytes 786440 | tf_op jit(solution)/shard_map/ppermute | solution.py:379
  34.1 3.8 %collective-permute-start.9 = (f32[2,128,128]{2,1,0:T(8,128)S(1)}, f32[2,128,128]{2,1,0:T(8,128)S(1)}, u32[]{:S(2)}, u32[]{:S(2)}) collective-permute-start(f32[2,128,128]{2,1,0:T(8,128)S(1)} %bitcast_add_fusion.3), channel_id=1, source_target_pairs={{0,4},{1,5},{2,6},{3,7},{4,0},{5,1},{6,2},{7,3},{8,12},{9,13},{10,... | collective-permute-start | bytes 393224 | tf_op jit(solution)/shard_map/ppermute | solution.py:389
  37.9 2.8 %collective-permute-done.10.refs_1_ = f32[2,2,128,128]{3,2,1,0:T(8,128)S(1)} collective-permute-done((f32[2,2,128,128]{3,2,1,0:T(8,128)S(1)}, f32[2,2,128,128]{3,2,1,0:T(8,128)S(1)}, u32[]{:S(2)}, u32[]{:S(2)}) %collective-permute-start.10) | collective-permute-done | bytes 262176 | tf_op jit(solution)/shard_map/ppermute | solution.py:379
  41.1 0.8 %collective-permute-start.11 = (f32[2,2,128,128]{3,2,1,0:T(8,128)S(1)}, f32[2,2,128,128]{3,2,1,0:T(8,128)S(1)}, u32[]{:S(2)}, u32[]{:S(2)}) collective-permute-start(f32[2,2,128,128]{3,2,1,0:T(8,128)S(1)} %get-tuple-element.81), channel_id=1, source_target_pairs={{0,2},{1,3},{2,0},{3,1},{4,6},{5,7},{6,4},{7,5},{8,10},{9,11},{10,... | collective-permute-start | bytes 786440 | tf_op jit(solution)/shard_map/ppermute | solution.py:379
  42.4 0.7 shard_map.88
  43.6 4.2 %shard_map.89 = (bf16[128,2048]{1,0:T(8,128)(2,1)}, bf16[128,2048]{1,0:T(8,128)(2,1)}, bf16[128,2048]{1,0:T(8,128)(2,1)}) custom-call(f32[2,2,128,128]{3,2,1,0:T(8,128)S(1)} %get-tuple-element.77.refs_0_, f32[2,2,128,128]{3,2,1,0:T(8,128)S(1)} %collective-permute-done.10.refs_1_, f32[2,2,128,128]{3,2,1,0:T(8,128)S(1)} %collective-permute-done.13.refs_2_, ...), custom_call_target="tpu_custom_call" | custom-call | flops 4026531 | bytes 57671 | tf_op jit(solution)/shard_map/pallas_call | solution.py:59
  47.8 2.1 %collective-permute-done.11.refs_1_ = f32[2,2,128,128]{3,2,1,0:T(8,128)S(1)} collective-permute-done((f32[2,2,128,128]{3,2,1,0:T(8,128)S(1)}, f32[2,2,128,128]{3,2,1,0:T(8,128)S(1)}, u32[]{:S(2)}, u32[]{:S(2)}) %collective-permute-start.11) | collective-permute-done | bytes 262176 | tf_op jit(solution)/shard_map/ppermute | solution.py:379
  50.1 1.5 %collective-permute-done.15.refs_3_ = f32[2,2,128,128]{3,2,1,0:T(8,128)S(1)} collective-permute-done((f32[2,2,128,128]{3,2,1,0:T(8,128)S(1)}, f32[2,2,128,128]{3,2,1,0:T(8,128)S(1)}, u32[]{:S(2)}, u32[]{:S(2)}) %collective-permute-start.15) | collective-permute-done | bytes 262176 | tf_op jit(solution)/shard_map/ppermute | solution.py:375
  51.6 0.7 shard_map.90
  52.5 1.5 %collective-permute-done.17 = f32[8,64,128]{2,1,0:T(8,128)} collective-permute-done((f32[8,64,128]{2,1,0:T(8,128)S(1)}, f32[8,64,128]{2,1,0:T(8,128)}, u32[]{:S(2)}, u32[]{:S(2)}) %collective-permute-start.17) | collective-permute-done | bytes 262176 | tf_op jit(solution)/shard_map/ppermute | solution.py:375
  54.1 1.0 %add.217 = f32[8,64,128]{2,1,0:T(8,128)S(1)} add(f32[8,64,128]{2,1,0:T(8,128)S(1)} %get-tuple-element.74, f32[8,64,128]{2,1,0:T(8,128)} %collective-permute-done.17) | non-fusion elementwise | flops 65536 | bytes 786432 | tf_op jit(solution)/shard_map/add | solution.py:535
  55.1 1.7 %collective-permute-start.20 = (f32[4,64,128]{2,1,0:T(8,128)S(1)}, f32[4,64,128]{2,1,0:T(8,128)S(1)}, u32[]{:S(2)}, u32[]{:S(2)}) collective-permute-start(f32[4,64,128]{2,1,0:T(8,128)S(1)} %pad_maximum_fusion.4), channel_id=1, source_target_pairs={{0,18},{1,19},{2,16},{3,17},{4,22},{5,23},{6,20},{7,21},{8,26},{9,... | collective-permute-start | bytes 393224 | tf_op jit(solution)/shard_map/ppermute | solution.py:423
  57.4 0.7 pad_maximum_fusion.2
  58.1 1.3 %collective-permute-start.18 = (f32[4,64,128]{2,1,0:T(8,128)}, f32[4,64,128]{2,1,0:T(8,128)S(1)}, u32[]{:S(2)}, u32[]{:S(2)}) collective-permute-start(f32[4,64,128]{2,1,0:T(8,128)} %pad_maximum_fusion.2), channel_id=1, source_target_pairs={{0,2},{1,3},{2,0},{3,1},{4,6},{5,7},{6,4},{7,5},{8,10},{9,11},{10,... | collective-permute-start | bytes 393224 | tf_op jit(solution)/shard_map/ppermute | solution.py:423
  59.4 4.2 %shard_map.91 = (bf16[128,2048]{1,0:T(8,128)(2,1)}, bf16[128,2048]{1,0:T(8,128)(2,1)}, bf16[128,2048]{1,0:T(8,128)(2,1)}) custom-call(f32[2,2,128,128]{3,2,1,0:T(8,128)S(1)} %get-tuple-element.79.refs_0_, f32[2,2,128,128]{3,2,1,0:T(8,128)S(1)} %collective-permute-done.11.refs_1_, ...), custom_call_target="tpu_custom_call", output_to_operand_aliasing={{0}: (10, {}), {1}: (11, {}), {2}: (12, {})} | custom-call | flops 4026531 | bytes 73400 | tf_op jit(solution)/shard_map/pallas_call | solution.py:59
  63.7 0.7 collective-permute-done.18
  64.5 2.5 %collective-permute-start.23 = (f32[64,128]{1,0:T(8,128)S(1)}, f32[64,128]{1,0:T(8,128)S(1)}, u32[]{:S(2)}, u32[]{:S(2)}) collective-permute-start(f32[64,128]{1,0:T(8,128)S(1)} %get-tuple-element.95), channel_id=1, source_target_pairs={{0,12},{1,13},{2,14},{3,15},{4,8},{5,9},{6,10},{7,11},{8,4},{9,5},... | collective-permute-start | bytes 98312 | tf_op jit(solution)/shard_map/ppermute | solution.py:438
  67.0 1.9 %collective-permute-start.21 = (f32[64,128]{1,0:T(8,128)S(1)}, f32[64,128]{1,0:T(8,128)S(1)}, u32[]{:S(2)}, u32[]{:S(2)}) collective-permute-start(f32[64,128]{1,0:T(8,128)S(1)} %get-tuple-element.94), channel_id=1, source_target_pairs={{0,4},{1,5},{2,6},{3,7},{4,0},{5,1},{6,2},{7,3},{8,12},{9,13},{10,... | collective-permute-start | bytes 98312 | tf_op jit(solution)/shard_map/ppermute | solution.py:438
  68.9 1.4 %collective-permute-done.23 = f32[64,128]{1,0:T(8,128)S(1)} collective-permute-done((f32[64,128]{1,0:T(8,128)S(1)}, f32[64,128]{1,0:T(8,128)S(1)}, u32[]{:S(2)}, u32[]{:S(2)}) %collective-permute-start.23) | collective-permute-done | bytes 32800 | tf_op jit(solution)/shard_map/ppermute | solution.py:438
  70.3 1.5 %collective-permute-done.22 = f32[64,128]{1,0:T(8,128)S(1)} collective-permute-done((f32[64,128]{1,0:T(8,128)S(1)}, f32[64,128]{1,0:T(8,128)S(1)}, u32[]{:S(2)}, u32[]{:S(2)}) %collective-permute-start.22) | collective-permute-done | bytes 32800 | tf_op jit(solution)/shard_map/ppermute | solution.py:438
  (68 shorter events, 4.9 us)
Async XLA Ops:
  3.6 2.0 %collective-permute-start = (f32[2,2,2,128,128]{4,3,2,1,0:T(8,128)S(1)}, f32[2,2,2,128,128]{4,3,2,1,0:T(8,128)S(1)}, u32[]{:S(2)}, u32[]{:S(2)}) collective-permute-start(f32[2,2,2,128,128]{4,3,2,1,0:T(8,128)S(1)} %get-tuple-element.41), channel_id=1, source_target_pairs={{0,1},{1,0},{2,3},{3,2},{4,5},{5,4},{6,7},{7,6},{8,9},{9,8},{10,11... | collective-permute-start | bytes 1572872 | tf_op jit(solution)/shard_map/ppermute | solution.py:375
  5.7 9.7 %collective-permute-start.3 = (f32[2,2,128,128]{3,2,1,0:T(8,128)S(1)}, f32[2,2,128,128]{3,2,1,0:T(8,128)S(1)}, u32[]{:S(2)}, u32[]{:S(2)}) collective-permute-start(f32[2,2,128,128]{3,2,1,0:T(8,128)S(1)} %fusion.3), channel_id=1, source_target_pairs={{0,2},{1,3},{2,0},{3,1},{4,6},{5,7},{6,4},{7,5},{8,10},{9,11},{10,... | collective-permute-start | bytes 786440 | tf_op jit(solution)/shard_map/ppermute | solution.py:379
  11.6 3.8 %collective-permute-start.1 = (f32[2,2,2,128,128]{4,3,2,1,0:T(8,128)S(1)}, f32[2,2,2,128,128]{4,3,2,1,0:T(8,128)S(1)}, u32[]{:S(2)}, u32[]{:S(2)}) collective-permute-start(f32[2,2,2,128,128]{4,3,2,1,0:T(8,128)S(1)} %get-tuple-element.44), channel_id=1, source_target_pairs={{0,1},{1,0},{2,3},{3,2},{4,5},{5,4},{6,7},{7,6},{8,9},{9,8},{10,11... | collective-permute-start | bytes 1572872 | tf_op jit(solution)/shard_map/ppermute | solution.py:375
  11.8 3.6 %copy-start.7 = (f32[2,2,2,128,128]{4,3,2,1,0:T(8,128)S(1)}, f32[2,2,2,128,128]{4,3,2,1,0:T(8,128)}, u32[]{:S(2)}) copy-start(f32[2,2,2,128,128]{4,3,2,1,0:T(8,128)} %get-tuple-element.46) | copy-start | bytes 1572868
  15.5 6.8 %collective-permute-start.4 = (f32[2,128,128]{2,1,0:T(8,128)S(1)}, f32[2,128,128]{2,1,0:T(8,128)S(1)}, u32[]{:S(2)}, u32[]{:S(2)}) collective-permute-start(f32[2,128,128]{2,1,0:T(8,128)S(1)} %select_bitcast_fusion.4), channel_id=1, source_target_pairs={{0,4},{1,5},{2,6},{3,7},{4,0},{5,1},{6,2},{7,3},{8,12},{9,13},{10,... | collective-permute-start | bytes 393224 | tf_op jit(solution)/shard_map/ppermute | solution.py:389
  17.3 8.3 %collective-permute-start.2 = (f32[2,2,128,128]{3,2,1,0:T(8,128)S(1)}, f32[2,2,128,128]{3,2,1,0:T(8,128)S(1)}, u32[]{:S(2)}, u32[]{:S(2)}) collective-permute-start(f32[2,2,128,128]{3,2,1,0:T(8,128)S(1)} %fusion.1), channel_id=1, source_target_pairs={{0,2},{1,3},{2,0},{3,1},{4,6},{5,7},{6,4},{7,5},{8,10},{9,11},{10,... | collective-permute-start | bytes 786440 | tf_op jit(solution)/shard_map/ppermute | solution.py:379
  22.3 3.3 %copy-start.6 = (f32[2,2,2,128,128]{4,3,2,1,0:T(8,128)S(1)}, f32[2,2,2,128,128]{4,3,2,1,0:T(8,128)}, u32[]{:S(2)}) copy-start(f32[2,2,2,128,128]{4,3,2,1,0:T(8,128)} %get-tuple-element.43) | copy-start | bytes 1572868
  22.3 3.8 %collective-permute-start.6 = (f32[2,128,128]{2,1,0:T(8,128)S(1)}, f32[2,128,128]{2,1,0:T(8,128)S(1)}, u32[]{:S(2)}, u32[]{:S(2)}) collective-permute-start(f32[2,128,128]{2,1,0:T(8,128)S(1)} %bitcast_add_fusion.1), channel_id=1, source_target_pairs={{0,1},{1,0},{2,3},{3,2},{4,8},{5,9},{6,10},{7,11},{8,4},{9,5},{10,... | collective-permute-start | bytes 393224 | tf_op jit(solution)/shard_map/ppermute | solution.py:389
  25.6 6.1 %collective-permute-start.5 = (f32[2,128,128]{2,1,0:T(8,128)S(1)}, f32[2,128,128]{2,1,0:T(8,128)S(1)}, u32[]{:S(2)}, u32[]{:S(2)}) collective-permute-start(f32[2,128,128]{2,1,0:T(8,128)S(1)} %select_bitcast_fusion.5), channel_id=1, source_target_pairs={{0,4},{1,5},{2,6},{3,7},{4,0},{5,1},{6,2},{7,3},{8,12},{9,13},{10,... | collective-permute-start | bytes 393224 | tf_op jit(solution)/shard_map/ppermute | solution.py:389
  26.1 6.9 %collective-permute-start.8 = (f32[2,128,128]{2,1,0:T(8,128)S(1)}, f32[2,128,128]{2,1,0:T(8,128)S(1)}, u32[]{:S(2)}, u32[]{:S(2)}) collective-permute-start(f32[2,128,128]{2,1,0:T(8,128)S(1)} %bitcast_add_fusion), channel_id=1, source_target_pairs={{0,4},{1,5},{2,6},{3,7},{4,0},{5,1},{6,2},{7,3},{8,12},{9,13},{10,... | collective-permute-start | bytes 393224 | tf_op jit(solution)/shard_map/ppermute | solution.py:389
  31.7 2.4 %collective-permute-start.7 = (f32[2,128,128]{2,1,0:T(8,128)S(1)}, f32[2,128,128]{2,1,0:T(8,128)S(1)}, u32[]{:S(2)}, u32[]{:S(2)}) collective-permute-start(f32[2,128,128]{2,1,0:T(8,128)S(1)} %bitcast_add_fusion.2), channel_id=1, source_target_pairs={{0,1},{1,0},{2,3},{3,2},{4,8},{5,9},{6,10},{7,11},{8,4},{9,5},{10,... | collective-permute-start | bytes 393224 | tf_op jit(solution)/shard_map/ppermute | solution.py:389
  33.2 7.5 %collective-permute-start.10 = (f32[2,2,128,128]{3,2,1,0:T(8,128)S(1)}, f32[2,2,128,128]{3,2,1,0:T(8,128)S(1)}, u32[]{:S(2)}, u32[]{:S(2)}) collective-permute-start(f32[2,2,128,128]{3,2,1,0:T(8,128)S(1)} %get-tuple-element.80), channel_id=1, source_target_pairs={{0,2},{1,3},{2,0},{3,1},{4,6},{5,7},{6,4},{7,5},{8,10},{9,11},{10,... | collective-permute-start | bytes 786440 | tf_op jit(solution)/shard_map/ppermute | solution.py:379
  34.1 8.1 %collective-permute-start.13 = (f32[2,2,128,128]{3,2,1,0:T(8,128)S(1)}, f32[2,2,128,128]{3,2,1,0:T(8,128)S(1)}, u32[]{:S(2)}, u32[]{:S(2)}) collective-permute-start(f32[2,2,128,128]{3,2,1,0:T(8,128)S(1)} %get-tuple-element.76), channel_id=1, source_target_pairs={{0,1},{1,0},{2,3},{3,2},{4,5},{5,4},{6,7},{7,6},{8,9},{9,8},{10,11... | collective-permute-start | bytes 786440 | tf_op jit(solution)/shard_map/ppermute | solution.py:375
  34.1 6.8 %collective-permute-start.9 = (f32[2,128,128]{2,1,0:T(8,128)S(1)}, f32[2,128,128]{2,1,0:T(8,128)S(1)}, u32[]{:S(2)}, u32[]{:S(2)}) collective-permute-start(f32[2,128,128]{2,1,0:T(8,128)S(1)} %bitcast_add_fusion.3), channel_id=1, source_target_pairs={{0,4},{1,5},{2,6},{3,7},{4,0},{5,1},{6,2},{7,3},{8,12},{9,13},{10,... | collective-permute-start | bytes 393224 | tf_op jit(solution)/shard_map/ppermute | solution.py:389
  40.8 1.6 %collective-permute-start.14 = (f32[2,2,128,128]{3,2,1,0:T(8,128)S(1)}, f32[2,2,128,128]{3,2,1,0:T(8,128)S(1)}, u32[]{:S(2)}, u32[]{:S(2)}) collective-permute-start(f32[2,2,128,128]{3,2,1,0:T(8,128)S(1)} %fusion.5), channel_id=1, source_target_pairs={{0,1},{1,0},{2,3},{3,2},{4,5},{5,4},{6,7},{7,6},{8,9},{9,8},{10,11... | collective-permute-start | bytes 786440 | tf_op jit(solution)/shard_map/ppermute | solution.py:375
  41.0 1.5 %copy-start.4 = (f32[8,128,128]{2,1,0:T(8,128)S(1)}, f32[8,128,128]{2,1,0:T(8,128)}, u32[]{:S(2)}) copy-start(f32[8,128,128]{2,1,0:T(8,128)} %get-tuple-element.53.refs_5_) | copy-start | bytes 1572868
  41.0 1.5 %copy-start.5 = (bf16[2,8,128,128]{3,2,1,0:T(8,128)(2,1)S(1)}, bf16[2,8,128,128]{3,2,1,0:T(8,128)(2,1)}, u32[]{:S(2)}) copy-start(bf16[2,8,128,128]{3,2,1,0:T(8,128)(2,1)} %get-tuple-element.54.refs_6_) | copy-start | bytes 1572868
  41.1 8.8 %collective-permute-start.11 = (f32[2,2,128,128]{3,2,1,0:T(8,128)S(1)}, f32[2,2,128,128]{3,2,1,0:T(8,128)S(1)}, u32[]{:S(2)}, u32[]{:S(2)}) collective-permute-start(f32[2,2,128,128]{3,2,1,0:T(8,128)S(1)} %get-tuple-element.81), channel_id=1, source_target_pairs={{0,2},{1,3},{2,0},{3,1},{4,6},{5,7},{6,4},{7,5},{8,10},{9,11},{10,... | collective-permute-start | bytes 786440 | tf_op jit(solution)/shard_map/ppermute | solution.py:379
  42.0 7.9 %collective-permute-start.12 = (f32[2,2,128,128]{3,2,1,0:T(8,128)S(1)}, f32[2,2,128,128]{3,2,1,0:T(8,128)S(1)}, u32[]{:S(2)}, u32[]{:S(2)}) collective-permute-start(f32[2,2,128,128]{3,2,1,0:T(8,128)S(1)} %get-tuple-element.78), channel_id=1, source_target_pairs={{0,1},{1,0},{2,3},{3,2},{4,5},{5,4},{6,7},{7,6},{8,9},{9,8},{10,11... | collective-permute-start | bytes 786440 | tf_op jit(solution)/shard_map/ppermute | solution.py:375
  42.4 1.0 %copy-start = (bf16[1,128,2048]{2,1,0:T(8,128)(2,1)S(1)}, bf16[1,128,2048]{2,1,0:T(8,128)(2,1)}, u32[]{:S(2)}) copy-start(bf16[1,128,2048]{2,1,0:T(8,128)(2,1)} %param.5) | copy-start | bytes 1572868
  42.4 1.2 %copy-start.1 = (bf16[1,128,2048]{2,1,0:T(8,128)(2,1)S(1)}, bf16[1,128,2048]{2,1,0:T(8,128)(2,1)}, u32[]{:S(2)}) copy-start(bf16[1,128,2048]{2,1,0:T(8,128)(2,1)} %param.6) | copy-start | bytes 1572868
  43.2 6.9 %collective-permute-start.16 = (f32[8,64,128]{2,1,0:T(8,128)S(1)}, f32[8,64,128]{2,1,0:T(8,128)S(1)}, u32[]{:S(2)}, u32[]{:S(2)}) collective-permute-start(f32[8,64,128]{2,1,0:T(8,128)S(1)} %get-tuple-element.61), channel_id=1, source_target_pairs={{0,1},{1,0},{2,3},{3,2},{4,5},{5,4},{6,7},{7,6},{8,9},{9,8},{10,11... | collective-permute-start | bytes 786440 | tf_op jit(solution)/shard_map/ppermute | solution.py:375
  49.9 1.7 %copy-start.3 = (bf16[2,8,128,128]{3,2,1,0:T(8,128)(2,1)S(1)}, bf16[2,8,128,128]{3,2,1,0:T(8,128)(2,1)}, u32[]{:S(2)}) copy-start(bf16[2,8,128,128]{3,2,1,0:T(8,128)(2,1)} %get-tuple-element.49.refs_6_) | copy-start | bytes 1572868
  50.0 1.6 %copy-start.2 = (f32[8,128,128]{2,1,0:T(8,128)S(1)}, f32[8,128,128]{2,1,0:T(8,128)}, u32[]{:S(2)}) copy-start(f32[8,128,128]{2,1,0:T(8,128)} %get-tuple-element.48.refs_5_) | copy-start | bytes 1572868
  50.0 1.6 %collective-permute-start.15 = (f32[2,2,128,128]{3,2,1,0:T(8,128)S(1)}, f32[2,2,128,128]{3,2,1,0:T(8,128)S(1)}, u32[]{:S(2)}, u32[]{:S(2)}) collective-permute-start(f32[2,2,128,128]{3,2,1,0:T(8,128)S(1)} %fusion.4), channel_id=1, source_target_pairs={{0,1},{1,0},{2,3},{3,2},{4,5},{5,4},{6,7},{7,6},{8,9},{9,8},{10,11... | collective-permute-start | bytes 786440 | tf_op jit(solution)/shard_map/ppermute | solution.py:375
  52.3 1.7 %collective-permute-start.17 = (f32[8,64,128]{2,1,0:T(8,128)S(1)}, f32[8,64,128]{2,1,0:T(8,128)}, u32[]{:S(2)}, u32[]{:S(2)}) collective-permute-start(f32[8,64,128]{2,1,0:T(8,128)S(1)} %get-tuple-element.69), channel_id=1, source_target_pairs={{0,1},{1,0},{2,3},{3,2},{4,5},{5,4},{6,7},{7,6},{8,9},{9,8},{10,11... | collective-permute-start | bytes 786440 | tf_op jit(solution)/shard_map/ppermute | solution.py:375
  55.1 8.5 %collective-permute-start.20 = (f32[4,64,128]{2,1,0:T(8,128)S(1)}, f32[4,64,128]{2,1,0:T(8,128)S(1)}, u32[]{:S(2)}, u32[]{:S(2)}) collective-permute-start(f32[4,64,128]{2,1,0:T(8,128)S(1)} %pad_maximum_fusion.4), channel_id=1, source_target_pairs={{0,18},{1,19},{2,16},{3,17},{4,22},{5,23},{6,20},{7,21},{8,26},{9,... | collective-permute-start | bytes 393224 | tf_op jit(solution)/shard_map/ppermute | solution.py:423
  56.8 6.9 %collective-permute-start.19 = (f32[4,64,128]{2,1,0:T(8,128)S(1)}, f32[4,64,128]{2,1,0:T(8,128)S(1)}, u32[]{:S(2)}, u32[]{:S(2)}) collective-permute-start(f32[4,64,128]{2,1,0:T(8,128)S(1)} %pad_maximum_fusion.3), channel_id=1, source_target_pairs={{0,16},{1,17},{2,18},{3,19},{4,20},{5,21},{6,22},{7,23},{8,24},{9,... | collective-permute-start | bytes 393224 | tf_op jit(solution)/shard_map/ppermute | solution.py:423
  58.1 6.3 %collective-permute-start.18 = (f32[4,64,128]{2,1,0:T(8,128)}, f32[4,64,128]{2,1,0:T(8,128)S(1)}, u32[]{:S(2)}, u32[]{:S(2)}) collective-permute-start(f32[4,64,128]{2,1,0:T(8,128)} %pad_maximum_fusion.2), channel_id=1, source_target_pairs={{0,2},{1,3},{2,0},{3,1},{4,6},{5,7},{6,4},{7,5},{8,10},{9,11},{10,... | collective-permute-start | bytes 393224 | tf_op jit(solution)/shard_map/ppermute | solution.py:423
  64.5 5.9 %collective-permute-start.23 = (f32[64,128]{1,0:T(8,128)S(1)}, f32[64,128]{1,0:T(8,128)S(1)}, u32[]{:S(2)}, u32[]{:S(2)}) collective-permute-start(f32[64,128]{1,0:T(8,128)S(1)} %get-tuple-element.95), channel_id=1, source_target_pairs={{0,12},{1,13},{2,14},{3,15},{4,8},{5,9},{6,10},{7,11},{8,4},{9,5},... | collective-permute-start | bytes 98312 | tf_op jit(solution)/shard_map/ppermute | solution.py:438
  67.0 4.8 %collective-permute-start.22 = (f32[64,128]{1,0:T(8,128)S(1)}, f32[64,128]{1,0:T(8,128)S(1)}, u32[]{:S(2)}, u32[]{:S(2)}) collective-permute-start(f32[64,128]{1,0:T(8,128)S(1)} %get-tuple-element.96), channel_id=1, source_target_pairs={{0,8},{1,9},{2,10},{3,11},{4,12},{5,13},{6,14},{7,15},{8,0},{9,1},... | collective-permute-start | bytes 98312 | tf_op jit(solution)/shard_map/ppermute | solution.py:438
  67.0 4.8 %collective-permute-start.21 = (f32[64,128]{1,0:T(8,128)S(1)}, f32[64,128]{1,0:T(8,128)S(1)}, u32[]{:S(2)}, u32[]{:S(2)}) collective-permute-start(f32[64,128]{1,0:T(8,128)S(1)} %get-tuple-element.94), channel_id=1, source_target_pairs={{0,4},{1,5},{2,6},{3,7},{4,0},{5,1},{6,2},{7,3},{8,12},{9,13},{10,... | collective-permute-start | bytes 98312 | tf_op jit(solution)/shard_map/ppermute | solution.py:438

commit v5 on v4

--- a/solution.py
+++ b/solution.py
@@ -11,7 +11,7 @@
 F32 = jnp.float32
 BF16 = jnp.bfloat16
 VMEM_LIMIT = 57 * 1024 * 1024
-MIDDLE_LIMIT = 51 * 1024 * 1024
+MIDDLE_LIMIT = 52 * 1024 * 1024
 STATES_LIMIT = 53 * 1024 * 1024
 SMALL_LIMIT = 16 * 1024 * 1024
 LIGHT = 0.01

time: 72.8 us -> 71.6 us (0.984)
  other arithmetic: 3.16 us -> 1.56 us
    add x2, other arithmetic: 1.01 us -> 0.06 us  [per_device(): halves.append(own + swap_core(plan, for_mate))]
  transfers between devices with their start and end apart: 24 -> 24, of which waited for: 13 -> 13; matrix products, arithmetic and copies ran while one was open for 2% -> 1% of each run, Pallas kernels for 26% -> 27%
where the time goes in v5:
time: 71.6 us; the launch traced here: 71.4 us
  starting transfers between devices  24.3 us (34%)
  Pallas kernels  23 us (32%)
  waiting for transfers between devices  21.3 us (30%)
  other arithmetic  1.56 us (2%)
  between operations  1.03 us (1%)
    pallas_call x8, Pallas kernels, call(): pl.pallas_call(body, out_shape=shapes, in_specs=specs(len(operands), near...  23 us
    ppermute x6, starting transfers between devices, chain_swap(): return lax.ppermute(state, 'context', steps)  8.7 us
    ppermute x4, waiting for transfers between devices, swap_chip(): lax.ppermute(state, 'context', [(i, i ^ 2) for i in range(plan.ranks)])  8.06 us
    ppermute x4, starting transfers between devices, swap_chip(): lax.ppermute(state, 'context', [(i, i ^ 2) for i in range(plan.ranks)])  6.13 us
    ppermute x8, waiting for transfers between devices, swap_core(): lax.ppermute(state, 'context', [(i, i ^ 1) for i in range(plan.ranks)])  4.68 us
    ppermute x3, starting transfers between devices, group_sum(): result = result + lax.ppermute(sent, 'context', steps)  4.45 us
    ppermute x6, waiting for transfers between devices, chain_swap(): return lax.ppermute(state, 'context', steps)  4.39 us
    ppermute x3, starting transfers between devices, plane_sums(): plane = plane + lax.ppermute(sent, ('dp', 'context'), steps)  3.68 us
  transfers between devices with their start and end apart: 24, of which 13 were waited for; matrix products, arithmetic and copies ran while one was open for 1% of the time, Pallas kernels for 27%

profile of v5, /device:TPU:0, one launch (start us, length us, event | category | flops | bytes accessed | tf_op | source)
XLA Modules:
  0.0 71.4 jit_solution(1084785472825515930)
XLA Ops:
  0.6 3.0 %shard_map.84 = (f32[2,2,2,128,128]{4,3,2,1,0:T(8,128)S(1)}, f32[2,2,2,128,128]{4,3,2,1,0:T(8,128)}, f32[2,2,128,128]{3,2,1,0:T(8,128)S(1)}) custom-call(bf16[128,2048]{1,0:T(8,128)(2,1)} %bitcast.109, bf16[128,2048]{1,0:T(8,128)(2,1)} %bitcast.115, bf16[128,2048]{1,0:T(8,128)(2,1)} %bitcast.121, bf16[128,2048]{1,0:T(8,128)(2,1)} %bitcast.127, ...), custom_call_target="tpu_custom_call" | custom-call | flops 134217728 | bytes 3932160 | tf_op jit(solution)/shard_map/pallas_call | solution.py:59
  4.1 1.5 %collective-permute-done.refs_4_ = f32[2,2,2,128,128]{4,3,2,1,0:T(8,128)S(1)} collective-permute-done((f32[2,2,2,128,128]{4,3,2,1,0:T(8,128)S(1)}, f32[2,2,2,128,128]{4,3,2,1,0:T(8,128)S(1)}, u32[]{:S(2)}, u32[]{:S(2)}) %collective-permute-start) | collective-permute-done | bytes 524320 | tf_op jit(solution)/shard_map/ppermute | solution.py:375
  5.7 3.0 %collective-permute-start.3 = (f32[2,2,128,128]{3,2,1,0:T(8,128)S(1)}, f32[2,2,128,128]{3,2,1,0:T(8,128)S(1)}, u32[]{:S(2)}, u32[]{:S(2)}) collective-permute-start(f32[2,2,128,128]{3,2,1,0:T(8,128)S(1)} %fusion.3), channel_id=1, source_target_pairs={{0,2},{1,3},{2,0},{3,1},{4,6},{5,7},{6,4},{7,5},{8,10},{9,11},{10,... | collective-permute-start | bytes 786440 | tf_op jit(solution)/shard_map/ppermute | solution.py:379
  8.7 3.0 %shard_map.85 = (f32[2,2,2,128,128]{4,3,2,1,0:T(8,128)S(1)}, f32[2,2,2,128,128]{4,3,2,1,0:T(8,128)}, f32[2,2,128,128]{3,2,1,0:T(8,128)S(1)}) custom-call(bf16[128,2048]{1,0:T(8,128)(2,1)} %bitcast.110, bf16[128,2048]{1,0:T(8,128)(2,1)} %bitcast.116, bf16[128,2048]{1,0:T(8,128)(2,1)} %bitcast.122, bf16[128,2048]{1,0:T(8,128)(2,1)} %bitcast.128, ...), custom_call_target="tpu_custom_call" | custom-call | flops 134217728 | bytes 3932160 | tf_op jit(solution)/shard_map/pallas_call | solution.py:59
  11.8 3.6 %shard_map.86 = (f32[8,128,128]{2,1,0:T(8,128)}, bf16[2,8,128,128]{3,2,1,0:T(8,128)(2,1)}) custom-call(bf16[128,2048]{1,0:T(8,128)(2,1)} %bitcast.111, bf16[128,2048]{1,0:T(8,128)(2,1)} %bitcast.117, bf16[128,2048]{1,0:T(8,128)(2,1)} %bitcast.123, bf16[128,2048]{1,0:T(8,128)(2,1)} %bitcast.129, bf16[16,128,128]{2,1,0:T(8,128)(2,1)} %refs_9_.1), custom_call_target="tpu_custom_call" | custom-call | flops 301989888 | bytes 3670016 | tf_op jit(solution)/shard_map/pallas_call | solution.py:59
  15.5 1.8 %collective-permute-start.4 = (f32[2,128,128]{2,1,0:T(8,128)S(1)}, f32[2,128,128]{2,1,0:T(8,128)S(1)}, u32[]{:S(2)}, u32[]{:S(2)}) collective-permute-start(f32[2,128,128]{2,1,0:T(8,128)S(1)} %select_bitcast_fusion.4), channel_id=1, source_target_pairs={{0,4},{1,5},{2,6},{3,7},{4,0},{5,1},{6,2},{7,3},{8,12},{9,13},{10,... | collective-permute-start | bytes 393224 | tf_op jit(solution)/shard_map/ppermute | solution.py:389
  17.3 1.5 %collective-permute-start.2 = (f32[2,2,128,128]{3,2,1,0:T(8,128)S(1)}, f32[2,2,128,128]{3,2,1,0:T(8,128)S(1)}, u32[]{:S(2)}, u32[]{:S(2)}) collective-permute-start(f32[2,2,128,128]{3,2,1,0:T(8,128)S(1)} %fusion.1), channel_id=1, source_target_pairs={{0,2},{1,3},{2,0},{3,1},{4,6},{5,7},{6,4},{7,5},{8,10},{9,11},{10,... | collective-permute-start | bytes 786440 | tf_op jit(solution)/shard_map/ppermute | solution.py:379
  18.8 3.5 %shard_map.87 = (f32[8,128,128]{2,1,0:T(8,128)}, bf16[2,8,128,128]{3,2,1,0:T(8,128)(2,1)}) custom-call(bf16[128,2048]{1,0:T(8,128)(2,1)} %bitcast.112, bf16[128,2048]{1,0:T(8,128)(2,1)} %bitcast.118, bf16[128,2048]{1,0:T(8,128)(2,1)} %bitcast.124, bf16[128,2048]{1,0:T(8,128)(2,1)} %bitcast.130, bf16[16,128,128]{2,1,0:T(8,128)(2,1)} %refs_9_.1), custom_call_target="tpu_custom_call" | custom-call | flops 301989888 | bytes 3670016 | tf_op jit(solution)/shard_map/pallas_call | solution.py:59
  22.4 3.1 %collective-permute-done.2 = f32[2,2,128,128]{3,2,1,0:T(8,128)S(1)} collective-permute-done((f32[2,2,128,128]{3,2,1,0:T(8,128)S(1)}, f32[2,2,128,128]{3,2,1,0:T(8,128)S(1)}, u32[]{:S(2)}, u32[]{:S(2)}) %collective-permute-start.2) | collective-permute-done | bytes 262176 | tf_op jit(solution)/shard_map/ppermute | solution.py:379
  26.1 2.4 %collective-permute-start.8 = (f32[2,128,128]{2,1,0:T(8,128)S(1)}, f32[2,128,128]{2,1,0:T(8,128)S(1)}, u32[]{:S(2)}, u32[]{:S(2)}) collective-permute-start(f32[2,128,128]{2,1,0:T(8,128)S(1)} %bitcast_add_fusion), channel_id=1, source_target_pairs={{0,4},{1,5},{2,6},{3,7},{4,0},{5,1},{6,2},{7,3},{8,12},{9,13},{10,... | collective-permute-start | bytes 393224 | tf_op jit(solution)/shard_map/ppermute | solution.py:389
  28.6 3.1 %collective-permute-done.5 = f32[2,128,128]{2,1,0:T(8,128)S(1)} collective-permute-done((f32[2,128,128]{2,1,0:T(8,128)S(1)}, f32[2,128,128]{2,1,0:T(8,128)S(1)}, u32[]{:S(2)}, u32[]{:S(2)}) %collective-permute-start.5) | collective-permute-done | bytes 131104 | tf_op jit(solution)/shard_map/ppermute | solution.py:389
  31.8 1.3 %collective-permute-done.8 = f32[2,128,128]{2,1,0:T(8,128)S(1)} collective-permute-done((f32[2,128,128]{2,1,0:T(8,128)S(1)}, f32[2,128,128]{2,1,0:T(8,128)S(1)}, u32[]{:S(2)}, u32[]{:S(2)}) %collective-permute-start.8) | collective-permute-done | bytes 131104 | tf_op jit(solution)/shard_map/ppermute | solution.py:389
  33.2 0.8 %collective-permute-start.10 = (f32[2,2,128,128]{3,2,1,0:T(8,128)S(1)}, f32[2,2,128,128]{3,2,1,0:T(8,128)S(1)}, u32[]{:S(2)}, u32[]{:S(2)}) collective-permute-start(f32[2,2,128,128]{3,2,1,0:T(8,128)S(1)} %get-tuple-element.80), channel_id=1, source_target_pairs={{0,2},{1,3},{2,0},{3,1},{4,6},{5,7},{6,4},{7,5},{8,10},{9,11},{10,... | collective-permute-start | bytes 786440 | tf_op jit(solution)/shard_map/ppermute | solution.py:379
  34.1 3.8 %collective-permute-start.9 = (f32[2,128,128]{2,1,0:T(8,128)S(1)}, f32[2,128,128]{2,1,0:T(8,128)S(1)}, u32[]{:S(2)}, u32[]{:S(2)}) collective-permute-start(f32[2,128,128]{2,1,0:T(8,128)S(1)} %bitcast_add_fusion.3), channel_id=1, source_target_pairs={{0,4},{1,5},{2,6},{3,7},{4,0},{5,1},{6,2},{7,3},{8,12},{9,13},{10,... | collective-permute-start | bytes 393224 | tf_op jit(solution)/shard_map/ppermute | solution.py:389
  37.9 2.8 %collective-permute-done.10.refs_1_ = f32[2,2,128,128]{3,2,1,0:T(8,128)S(1)} collective-permute-done((f32[2,2,128,128]{3,2,1,0:T(8,128)S(1)}, f32[2,2,128,128]{3,2,1,0:T(8,128)S(1)}, u32[]{:S(2)}, u32[]{:S(2)}) %collective-permute-start.10) | collective-permute-done | bytes 262176 | tf_op jit(solution)/shard_map/ppermute | solution.py:379
  41.1 0.8 %collective-permute-start.11 = (f32[2,2,128,128]{3,2,1,0:T(8,128)S(1)}, f32[2,2,128,128]{3,2,1,0:T(8,128)S(1)}, u32[]{:S(2)}, u32[]{:S(2)}) collective-permute-start(f32[2,2,128,128]{3,2,1,0:T(8,128)S(1)} %get-tuple-element.81), channel_id=1, source_target_pairs={{0,2},{1,3},{2,0},{3,1},{4,6},{5,7},{6,4},{7,5},{8,10},{9,11},{10,... | collective-permute-start | bytes 786440 | tf_op jit(solution)/shard_map/ppermute | solution.py:379
  42.4 0.7 shard_map.88
  43.4 4.3 %shard_map.89 = (bf16[128,2048]{1,0:T(8,128)(2,1)}, bf16[128,2048]{1,0:T(8,128)(2,1)}, bf16[128,2048]{1,0:T(8,128)(2,1)}) custom-call(f32[2,2,128,128]{3,2,1,0:T(8,128)S(1)} %get-tuple-element.77.refs_0_, f32[2,2,128,128]{3,2,1,0:T(8,128)S(1)} %collective-permute-done.10.refs_1_, f32[2,2,128,128]{3,2,1,0:T(8,128)S(1)} %collective-permute-done.13.refs_2_, ...), custom_call_target="tpu_custom_call" | custom-call | flops 4026531 | bytes 57671 | tf_op jit(solution)/shard_map/pallas_call | solution.py:59
  47.7 2.2 %collective-permute-done.11.refs_1_ = f32[2,2,128,128]{3,2,1,0:T(8,128)S(1)} collective-permute-done((f32[2,2,128,128]{3,2,1,0:T(8,128)S(1)}, f32[2,2,128,128]{3,2,1,0:T(8,128)S(1)}, u32[]{:S(2)}, u32[]{:S(2)}) %collective-permute-start.11) | collective-permute-done | bytes 262176 | tf_op jit(solution)/shard_map/ppermute | solution.py:379
  50.1 1.5 %collective-permute-done.15.refs_3_ = f32[2,2,128,128]{3,2,1,0:T(8,128)S(1)} collective-permute-done((f32[2,2,128,128]{3,2,1,0:T(8,128)S(1)}, f32[2,2,128,128]{3,2,1,0:T(8,128)S(1)}, u32[]{:S(2)}, u32[]{:S(2)}) %collective-permute-start.15) | collective-permute-done | bytes 262176 | tf_op jit(solution)/shard_map/ppermute | solution.py:375
  51.6 0.7 shard_map.90
  52.5 1.4 %collective-permute-done.17 = f32[8,64,128]{2,1,0:T(8,128)S(1)} collective-permute-done((f32[8,64,128]{2,1,0:T(8,128)S(1)}, f32[8,64,128]{2,1,0:T(8,128)S(1)}, u32[]{:S(2)}, u32[]{:S(2)}) %collective-permute-start.17) | collective-permute-done | bytes 262176 | tf_op jit(solution)/shard_map/ppermute | solution.py:375
  54.0 1.7 %collective-permute-start.20 = (f32[4,64,128]{2,1,0:T(8,128)S(1)}, f32[4,64,128]{2,1,0:T(8,128)S(1)}, u32[]{:S(2)}, u32[]{:S(2)}) collective-permute-start(f32[4,64,128]{2,1,0:T(8,128)S(1)} %pad_maximum_fusion.4), channel_id=1, source_target_pairs={{0,18},{1,19},{2,16},{3,17},{4,22},{5,23},{6,20},{7,21},{8,26},{9,... | collective-permute-start | bytes 393224 | tf_op jit(solution)/shard_map/ppermute | solution.py:423
  55.8 0.6 collective-permute-start.19
  56.4 1.3 %collective-permute-start.18 = (f32[4,64,128]{2,1,0:T(8,128)S(1)}, f32[4,64,128]{2,1,0:T(8,128)S(1)}, u32[]{:S(2)}, u32[]{:S(2)}) collective-permute-start(f32[4,64,128]{2,1,0:T(8,128)S(1)} %pad_maximum_fusion.2), channel_id=1, source_target_pairs={{0,2},{1,3},{2,0},{3,1},{4,6},{5,7},{6,4},{7,5},{8,10},{9,11},{10,... | collective-permute-start | bytes 393224 | tf_op jit(solution)/shard_map/ppermute | solution.py:423
  57.7 4.3 %shard_map.91 = (bf16[128,2048]{1,0:T(8,128)(2,1)}, bf16[128,2048]{1,0:T(8,128)(2,1)}, bf16[128,2048]{1,0:T(8,128)(2,1)}) custom-call(f32[2,2,128,128]{3,2,1,0:T(8,128)S(1)} %get-tuple-element.79.refs_0_, f32[2,2,128,128]{3,2,1,0:T(8,128)S(1)} %collective-permute-done.11.refs_1_, ...), custom_call_target="tpu_custom_call", output_to_operand_aliasing={{0}: (10, {}), {1}: (11, {}), {2}: (12, {})} | custom-call | flops 4026531 | bytes 73400 | tf_op jit(solution)/shard_map/pallas_call | solution.py:59
  62.6 0.7 collective-permute-done.18
  63.4 2.5 %collective-permute-start.23 = (f32[64,128]{1,0:T(8,128)S(1)}, f32[64,128]{1,0:T(8,128)S(1)}, u32[]{:S(2)}, u32[]{:S(2)}) collective-permute-start(f32[64,128]{1,0:T(8,128)S(1)} %get-tuple-element.95), channel_id=1, source_target_pairs={{0,12},{1,13},{2,14},{3,15},{4,8},{5,9},{6,10},{7,11},{8,4},{9,5},... | collective-permute-start | bytes 98312 | tf_op jit(solution)/shard_map/ppermute | solution.py:438
  65.9 1.9 %collective-permute-start.21 = (f32[64,128]{1,0:T(8,128)S(1)}, f32[64,128]{1,0:T(8,128)S(1)}, u32[]{:S(2)}, u32[]{:S(2)}) collective-permute-start(f32[64,128]{1,0:T(8,128)S(1)} %get-tuple-element.94), channel_id=1, source_target_pairs={{0,4},{1,5},{2,6},{3,7},{4,0},{5,1},{6,2},{7,3},{8,12},{9,13},{10,... | collective-permute-start | bytes 98312 | tf_op jit(solution)/shard_map/ppermute | solution.py:438
  67.8 1.3 %collective-permute-done.23 = f32[64,128]{1,0:T(8,128)S(1)} collective-permute-done((f32[64,128]{1,0:T(8,128)S(1)}, f32[64,128]{1,0:T(8,128)S(1)}, u32[]{:S(2)}, u32[]{:S(2)}) %collective-permute-start.23) | collective-permute-done | bytes 32800 | tf_op jit(solution)/shard_map/ppermute | solution.py:438
  69.2 1.6 %collective-permute-done.22 = f32[64,128]{1,0:T(8,128)S(1)} collective-permute-done((f32[64,128]{1,0:T(8,128)S(1)}, f32[64,128]{1,0:T(8,128)S(1)}, u32[]{:S(2)}, u32[]{:S(2)}) %collective-permute-start.22) | collective-permute-done | bytes 32800 | tf_op jit(solution)/shard_map/ppermute | solution.py:438
  70.7 0.6 fusion.14
  (64 shorter events, 3.9 us)
Async XLA Ops:
  3.6 2.0 %collective-permute-start = (f32[2,2,2,128,128]{4,3,2,1,0:T(8,128)S(1)}, f32[2,2,2,128,128]{4,3,2,1,0:T(8,128)S(1)}, u32[]{:S(2)}, u32[]{:S(2)}) collective-permute-start(f32[2,2,2,128,128]{4,3,2,1,0:T(8,128)S(1)} %get-tuple-element.41), channel_id=1, source_target_pairs={{0,1},{1,0},{2,3},{3,2},{4,5},{5,4},{6,7},{7,6},{8,9},{9,8},{10,11... | collective-permute-start | bytes 1572872 | tf_op jit(solution)/shard_map/ppermute | solution.py:375
  5.7 9.7 %collective-permute-start.3 = (f32[2,2,128,128]{3,2,1,0:T(8,128)S(1)}, f32[2,2,128,128]{3,2,1,0:T(8,128)S(1)}, u32[]{:S(2)}, u32[]{:S(2)}) collective-permute-start(f32[2,2,128,128]{3,2,1,0:T(8,128)S(1)} %fusion.3), channel_id=1, source_target_pairs={{0,2},{1,3},{2,0},{3,1},{4,6},{5,7},{6,4},{7,5},{8,10},{9,11},{10,... | collective-permute-start | bytes 786440 | tf_op jit(solution)/shard_map/ppermute | solution.py:379
  11.6 3.8 %collective-permute-start.1 = (f32[2,2,2,128,128]{4,3,2,1,0:T(8,128)S(1)}, f32[2,2,2,128,128]{4,3,2,1,0:T(8,128)S(1)}, u32[]{:S(2)}, u32[]{:S(2)}) collective-permute-start(f32[2,2,2,128,128]{4,3,2,1,0:T(8,128)S(1)} %get-tuple-element.44), channel_id=1, source_target_pairs={{0,1},{1,0},{2,3},{3,2},{4,5},{5,4},{6,7},{7,6},{8,9},{9,8},{10,11... | collective-permute-start | bytes 1572872 | tf_op jit(solution)/shard_map/ppermute | solution.py:375
  11.8 3.6 %copy-start.5 = (f32[2,2,2,128,128]{4,3,2,1,0:T(8,128)S(1)}, f32[2,2,2,128,128]{4,3,2,1,0:T(8,128)}, u32[]{:S(2)}) copy-start(f32[2,2,2,128,128]{4,3,2,1,0:T(8,128)} %get-tuple-element.46) | copy-start | bytes 1572868
  15.5 6.8 %collective-permute-start.4 = (f32[2,128,128]{2,1,0:T(8,128)S(1)}, f32[2,128,128]{2,1,0:T(8,128)S(1)}, u32[]{:S(2)}, u32[]{:S(2)}) collective-permute-start(f32[2,128,128]{2,1,0:T(8,128)S(1)} %select_bitcast_fusion.4), channel_id=1, source_target_pairs={{0,4},{1,5},{2,6},{3,7},{4,0},{5,1},{6,2},{7,3},{8,12},{9,13},{10,... | collective-permute-start | bytes 393224 | tf_op jit(solution)/shard_map/ppermute | solution.py:389
  17.3 8.3 %collective-permute-start.2 = (f32[2,2,128,128]{3,2,1,0:T(8,128)S(1)}, f32[2,2,128,128]{3,2,1,0:T(8,128)S(1)}, u32[]{:S(2)}, u32[]{:S(2)}) collective-permute-start(f32[2,2,128,128]{3,2,1,0:T(8,128)S(1)} %fusion.1), channel_id=1, source_target_pairs={{0,2},{1,3},{2,0},{3,1},{4,6},{5,7},{6,4},{7,5},{8,10},{9,11},{10,... | collective-permute-start | bytes 786440 | tf_op jit(solution)/shard_map/ppermute | solution.py:379
  22.3 3.3 %copy-start.4 = (f32[2,2,2,128,128]{4,3,2,1,0:T(8,128)S(1)}, f32[2,2,2,128,128]{4,3,2,1,0:T(8,128)}, u32[]{:S(2)}) copy-start(f32[2,2,2,128,128]{4,3,2,1,0:T(8,128)} %get-tuple-element.43) | copy-start | bytes 1572868
  22.3 3.8 %collective-permute-start.6 = (f32[2,128,128]{2,1,0:T(8,128)S(1)}, f32[2,128,128]{2,1,0:T(8,128)S(1)}, u32[]{:S(2)}, u32[]{:S(2)}) collective-permute-start(f32[2,128,128]{2,1,0:T(8,128)S(1)} %bitcast_add_fusion.1), channel_id=1, source_target_pairs={{0,1},{1,0},{2,3},{3,2},{4,8},{5,9},{6,10},{7,11},{8,4},{9,5},{10,... | collective-permute-start | bytes 393224 | tf_op jit(solution)/shard_map/ppermute | solution.py:389
  25.6 6.1 %collective-permute-start.5 = (f32[2,128,128]{2,1,0:T(8,128)S(1)}, f32[2,128,128]{2,1,0:T(8,128)S(1)}, u32[]{:S(2)}, u32[]{:S(2)}) collective-permute-start(f32[2,128,128]{2,1,0:T(8,128)S(1)} %select_bitcast_fusion.5), channel_id=1, source_target_pairs={{0,4},{1,5},{2,6},{3,7},{4,0},{5,1},{6,2},{7,3},{8,12},{9,13},{10,... | collective-permute-start | bytes 393224 | tf_op jit(solution)/shard_map/ppermute | solution.py:389
  26.1 6.9 %collective-permute-start.8 = (f32[2,128,128]{2,1,0:T(8,128)S(1)}, f32[2,128,128]{2,1,0:T(8,128)S(1)}, u32[]{:S(2)}, u32[]{:S(2)}) collective-permute-start(f32[2,128,128]{2,1,0:T(8,128)S(1)} %bitcast_add_fusion), channel_id=1, source_target_pairs={{0,4},{1,5},{2,6},{3,7},{4,0},{5,1},{6,2},{7,3},{8,12},{9,13},{10,... | collective-permute-start | bytes 393224 | tf_op jit(solution)/shard_map/ppermute | solution.py:389
  31.7 2.4 %collective-permute-start.7 = (f32[2,128,128]{2,1,0:T(8,128)S(1)}, f32[2,128,128]{2,1,0:T(8,128)S(1)}, u32[]{:S(2)}, u32[]{:S(2)}) collective-permute-start(f32[2,128,128]{2,1,0:T(8,128)S(1)} %bitcast_add_fusion.2), channel_id=1, source_target_pairs={{0,1},{1,0},{2,3},{3,2},{4,8},{5,9},{6,10},{7,11},{8,4},{9,5},{10,... | collective-permute-start | bytes 393224 | tf_op jit(solution)/shard_map/ppermute | solution.py:389
  33.2 7.5 %collective-permute-start.10 = (f32[2,2,128,128]{3,2,1,0:T(8,128)S(1)}, f32[2,2,128,128]{3,2,1,0:T(8,128)S(1)}, u32[]{:S(2)}, u32[]{:S(2)}) collective-permute-start(f32[2,2,128,128]{3,2,1,0:T(8,128)S(1)} %get-tuple-element.80), channel_id=1, source_target_pairs={{0,2},{1,3},{2,0},{3,1},{4,6},{5,7},{6,4},{7,5},{8,10},{9,11},{10,... | collective-permute-start | bytes 786440 | tf_op jit(solution)/shard_map/ppermute | solution.py:379
  34.1 8.1 %collective-permute-start.13 = (f32[2,2,128,128]{3,2,1,0:T(8,128)S(1)}, f32[2,2,128,128]{3,2,1,0:T(8,128)S(1)}, u32[]{:S(2)}, u32[]{:S(2)}) collective-permute-start(f32[2,2,128,128]{3,2,1,0:T(8,128)S(1)} %get-tuple-element.76), channel_id=1, source_target_pairs={{0,1},{1,0},{2,3},{3,2},{4,5},{5,4},{6,7},{7,6},{8,9},{9,8},{10,11... | collective-permute-start | bytes 786440 | tf_op jit(solution)/shard_map/ppermute | solution.py:375
  34.1 6.8 %collective-permute-start.9 = (f32[2,128,128]{2,1,0:T(8,128)S(1)}, f32[2,128,128]{2,1,0:T(8,128)S(1)}, u32[]{:S(2)}, u32[]{:S(2)}) collective-permute-start(f32[2,128,128]{2,1,0:T(8,128)S(1)} %bitcast_add_fusion.3), channel_id=1, source_target_pairs={{0,4},{1,5},{2,6},{3,7},{4,0},{5,1},{6,2},{7,3},{8,12},{9,13},{10,... | collective-permute-start | bytes 393224 | tf_op jit(solution)/shard_map/ppermute | solution.py:389
  40.8 1.6 %collective-permute-start.14 = (f32[2,2,128,128]{3,2,1,0:T(8,128)S(1)}, f32[2,2,128,128]{3,2,1,0:T(8,128)S(1)}, u32[]{:S(2)}, u32[]{:S(2)}) collective-permute-start(f32[2,2,128,128]{3,2,1,0:T(8,128)S(1)} %fusion.5), channel_id=1, source_target_pairs={{0,1},{1,0},{2,3},{3,2},{4,5},{5,4},{6,7},{7,6},{8,9},{9,8},{10,11... | collective-permute-start | bytes 786440 | tf_op jit(solution)/shard_map/ppermute | solution.py:375
  40.9 1.5 %copy-start.2 = (f32[8,128,128]{2,1,0:T(8,128)S(1)}, f32[8,128,128]{2,1,0:T(8,128)}, u32[]{:S(2)}) copy-start(f32[8,128,128]{2,1,0:T(8,128)} %get-tuple-element.53.refs_5_) | copy-start | bytes 1572868
  41.0 1.5 %copy-start.3 = (bf16[2,8,128,128]{3,2,1,0:T(8,128)(2,1)S(1)}, bf16[2,8,128,128]{3,2,1,0:T(8,128)(2,1)}, u32[]{:S(2)}) copy-start(bf16[2,8,128,128]{3,2,1,0:T(8,128)(2,1)} %get-tuple-element.54.refs_6_) | copy-start | bytes 1572868
  41.1 8.8 %collective-permute-start.11 = (f32[2,2,128,128]{3,2,1,0:T(8,128)S(1)}, f32[2,2,128,128]{3,2,1,0:T(8,128)S(1)}, u32[]{:S(2)}, u32[]{:S(2)}) collective-permute-start(f32[2,2,128,128]{3,2,1,0:T(8,128)S(1)} %get-tuple-element.81), channel_id=1, source_target_pairs={{0,2},{1,3},{2,0},{3,1},{4,6},{5,7},{6,4},{7,5},{8,10},{9,11},{10,... | collective-permute-start | bytes 786440 | tf_op jit(solution)/shard_map/ppermute | solution.py:379
  41.9 7.9 %collective-permute-start.12 = (f32[2,2,128,128]{3,2,1,0:T(8,128)S(1)}, f32[2,2,128,128]{3,2,1,0:T(8,128)S(1)}, u32[]{:S(2)}, u32[]{:S(2)}) collective-permute-start(f32[2,2,128,128]{3,2,1,0:T(8,128)S(1)} %get-tuple-element.78), channel_id=1, source_target_pairs={{0,1},{1,0},{2,3},{3,2},{4,5},{5,4},{6,7},{7,6},{8,9},{9,8},{10,11... | collective-permute-start | bytes 786440 | tf_op jit(solution)/shard_map/ppermute | solution.py:375
  43.1 6.9 %collective-permute-start.16 = (f32[8,64,128]{2,1,0:T(8,128)S(1)}, f32[8,64,128]{2,1,0:T(8,128)S(1)}, u32[]{:S(2)}, u32[]{:S(2)}) collective-permute-start(f32[8,64,128]{2,1,0:T(8,128)S(1)} %get-tuple-element.61), channel_id=1, source_target_pairs={{0,1},{1,0},{2,3},{3,2},{4,5},{5,4},{6,7},{7,6},{8,9},{9,8},{10,11... | collective-permute-start | bytes 786440 | tf_op jit(solution)/shard_map/ppermute | solution.py:375
  49.9 1.7 %copy-start.1 = (bf16[2,8,128,128]{3,2,1,0:T(8,128)(2,1)S(1)}, bf16[2,8,128,128]{3,2,1,0:T(8,128)(2,1)}, u32[]{:S(2)}) copy-start(bf16[2,8,128,128]{3,2,1,0:T(8,128)(2,1)} %get-tuple-element.49.refs_6_) | copy-start | bytes 1572868
  50.0 1.6 %copy-start = (f32[8,128,128]{2,1,0:T(8,128)S(1)}, f32[8,128,128]{2,1,0:T(8,128)}, u32[]{:S(2)}) copy-start(f32[8,128,128]{2,1,0:T(8,128)} %get-tuple-element.48.refs_5_) | copy-start | bytes 1572868
  50.0 1.6 %collective-permute-start.15 = (f32[2,2,128,128]{3,2,1,0:T(8,128)S(1)}, f32[2,2,128,128]{3,2,1,0:T(8,128)S(1)}, u32[]{:S(2)}, u32[]{:S(2)}) collective-permute-start(f32[2,2,128,128]{3,2,1,0:T(8,128)S(1)} %fusion.4), channel_id=1, source_target_pairs={{0,1},{1,0},{2,3},{3,2},{4,5},{5,4},{6,7},{7,6},{8,9},{9,8},{10,11... | collective-permute-start | bytes 786440 | tf_op jit(solution)/shard_map/ppermute | solution.py:375
  52.3 1.6 %collective-permute-start.17 = (f32[8,64,128]{2,1,0:T(8,128)S(1)}, f32[8,64,128]{2,1,0:T(8,128)S(1)}, u32[]{:S(2)}, u32[]{:S(2)}) collective-permute-start(f32[8,64,128]{2,1,0:T(8,128)S(1)} %get-tuple-element.69), channel_id=1, source_target_pairs={{0,1},{1,0},{2,3},{3,2},{4,5},{5,4},{6,7},{7,6},{8,9},{9,8},{10,11... | collective-permute-start | bytes 786440 | tf_op jit(solution)/shard_map/ppermute | solution.py:375
  54.0 8.0 %collective-permute-start.20 = (f32[4,64,128]{2,1,0:T(8,128)S(1)}, f32[4,64,128]{2,1,0:T(8,128)S(1)}, u32[]{:S(2)}, u32[]{:S(2)}) collective-permute-start(f32[4,64,128]{2,1,0:T(8,128)S(1)} %pad_maximum_fusion.4), channel_id=1, source_target_pairs={{0,18},{1,19},{2,16},{3,17},{4,22},{5,23},{6,20},{7,21},{8,26},{9,... | collective-permute-start | bytes 393224 | tf_op jit(solution)/shard_map/ppermute | solution.py:423
  55.8 6.9 %collective-permute-start.19 = (f32[4,64,128]{2,1,0:T(8,128)S(1)}, f32[4,64,128]{2,1,0:T(8,128)S(1)}, u32[]{:S(2)}, u32[]{:S(2)}) collective-permute-start(f32[4,64,128]{2,1,0:T(8,128)S(1)} %pad_maximum_fusion.3), channel_id=1, source_target_pairs={{0,16},{1,17},{2,18},{3,19},{4,20},{5,21},{6,22},{7,23},{8,24},{9,... | collective-permute-start | bytes 393224 | tf_op jit(solution)/shard_map/ppermute | solution.py:423
  56.4 6.9 %collective-permute-start.18 = (f32[4,64,128]{2,1,0:T(8,128)S(1)}, f32[4,64,128]{2,1,0:T(8,128)S(1)}, u32[]{:S(2)}, u32[]{:S(2)}) collective-permute-start(f32[4,64,128]{2,1,0:T(8,128)S(1)} %pad_maximum_fusion.2), channel_id=1, source_target_pairs={{0,2},{1,3},{2,0},{3,1},{4,6},{5,7},{6,4},{7,5},{8,10},{9,11},{10,... | collective-permute-start | bytes 393224 | tf_op jit(solution)/shard_map/ppermute | solution.py:423
  63.4 5.8 %collective-permute-start.23 = (f32[64,128]{1,0:T(8,128)S(1)}, f32[64,128]{1,0:T(8,128)S(1)}, u32[]{:S(2)}, u32[]{:S(2)}) collective-permute-start(f32[64,128]{1,0:T(8,128)S(1)} %get-tuple-element.95), channel_id=1, source_target_pairs={{0,12},{1,13},{2,14},{3,15},{4,8},{5,9},{6,10},{7,11},{8,4},{9,5},... | collective-permute-start | bytes 98312 | tf_op jit(solution)/shard_map/ppermute | solution.py:438
  65.9 4.8 %collective-permute-start.22 = (f32[64,128]{1,0:T(8,128)S(1)}, f32[64,128]{1,0:T(8,128)S(1)}, u32[]{:S(2)}, u32[]{:S(2)}) collective-permute-start(f32[64,128]{1,0:T(8,128)S(1)} %get-tuple-element.96), channel_id=1, source_target_pairs={{0,8},{1,9},{2,10},{3,11},{4,12},{5,13},{6,14},{7,15},{8,0},{9,1},... | collective-permute-start | bytes 98312 | tf_op jit(solution)/shard_map/ppermute | solution.py:438
  65.9 4.8 %collective-permute-start.21 = (f32[64,128]{1,0:T(8,128)S(1)}, f32[64,128]{1,0:T(8,128)S(1)}, u32[]{:S(2)}, u32[]{:S(2)}) collective-permute-start(f32[64,128]{1,0:T(8,128)S(1)} %get-tuple-element.94), channel_id=1, source_target_pairs={{0,4},{1,5},{2,6},{3,7},{4,0},{5,1},{6,2},{7,3},{8,12},{9,13},{10,... | collective-permute-start | bytes 98312 | tf_op jit(solution)/shard_map/ppermute | solution.py:438

commit v6 on v5

--- a/solution.py
+++ b/solution.py
@@ -29,6 +29,9 @@
         self.run = per_copy // self.chunks if self.chunks > 1 else self.in_chunk
         self.stride = per_copy if self.chunks > 1 else 0
         self.height = heads * width // (copies * ranks)
+        self.pieces = 2 if tokens % 32 == 0 else 1
+        self.piece = tokens // self.pieces
+        self.loads = 4 * self.pieces + 1
         self.factor = 1.0 / math.sqrt(width * tokens * ranks)
         self.norm = 1.0 / math.sqrt(copies * tokens * ranks)
 
@@ -99,12 +102,14 @@
         source = pl.ds(head * width, plan.run * width)
         target = pl.ds((offset + first) * width, plan.run * width)
         for ref, buf in zip(row_refs, row_bufs):
-            started.append(copies.start(ref.at[:, source], buf.at[:, target]))
+            for part in range(plan.pieces):
+                rows = pl.ds(part * plan.piece, plan.piece)
+                started.append(copies.start(ref.at[rows, source], buf.at[rows, target]))
     return started
 
 
 def chunk_copies(plan):
-    return 5 * (plan.in_chunk // plan.run)
+    return plan.loads * (plan.in_chunk // plan.run)
 
 
 def row_scratch(plan, count):
@@ -130,7 +135,7 @@
     copies, width = Copies(sems), plan.width
     started = load_chunk(plan, copies, chunk, 0, row_refs, maps_ref, row_bufs, maps_buf)
     q_buf, k_buf, v_buf, g_buf = row_bufs
-    size = 5 * max(1, 4 // plan.run)
+    size = plan.loads * max(1, 4 // plan.run)
     for first in range(0, plan.in_chunk, 4):
         places = range(first, first + 4)
         wait(started[:size])
@@ -186,7 +191,7 @@
     started = load_chunk(plan, copies, chunk, 0, row_refs, maps_ref, row_bufs, maps_buf)
     causal = causal_mask(plan.tokens)
     written = []
-    size = 5 * max(1, 4 // plan.run)
+    size = plan.loads * max(1, 4 // plan.run)
     for first in range(0, plan.in_chunk, 4):
         places = range(first, first + 4)
         wait(started[:size])
@@ -309,7 +314,7 @@
     extra_copy.wait()
     finish_states(plan, state_refs, extra_buf, state_buf)
     written = []
-    size = 5 * max(1, 4 // plan.run)
+    size = plan.loads * max(1, 4 // plan.run)
     for first in range(0, plan.in_chunk, 4):
         places = range(first, first + 4)
         wait(started[:size])

time: 71.6 us -> 71.7 us (level)
  no operation moved by 1% of the time
where the time goes in v6:
time: 71.7 us; the launch traced here: 71.5 us
  starting transfers between devices  24.3 us (34%)
  Pallas kernels  23.2 us (32%)
  waiting for transfers between devices  21.4 us (30%)
  other arithmetic  1.56 us (2%)
  between operations  1.03 us (1%)
    pallas_call x8, Pallas kernels, call(): pl.pallas_call(body, out_shape=shapes, in_specs=specs(len(operands), near...  23.2 us
    ppermute x6, starting transfers between devices, chain_swap(): return lax.ppermute(state, 'context', steps)  8.6 us
    ppermute x4, waiting for transfers between devices, swap_chip(): lax.ppermute(state, 'context', [(i, i ^ 2) for i in range(plan.ranks)])  8.08 us
    ppermute x4, starting transfers between devices, swap_chip(): lax.ppermute(state, 'context', [(i, i ^ 2) for i in range(plan.ranks)])  6.15 us
    ppermute x8, waiting for transfers between devices, swap_core(): lax.ppermute(state, 'context', [(i, i ^ 1) for i in range(plan.ranks)])  4.65 us
    ppermute x6, waiting for transfers between devices, chain_swap(): return lax.ppermute(state, 'context', steps)  4.48 us
    ppermute x3, starting transfers between devices, group_sum(): result = result + lax.ppermute(sent, 'context', steps)  4.45 us
    ppermute x3, starting transfers between devices, plane_sums(): plane = plane + lax.ppermute(sent, ('dp', 'context'), steps)  3.68 us
  transfers between devices with their start and end apart: 24, of which 13 were waited for; matrix products, arithmetic and copies ran while one was open for 1% of the time, Pallas kernels for 27%

profile of v6, /device:TPU:0, one launch (start us, length us, event | category | flops | bytes accessed | tf_op | source)
XLA Modules:
  0.0 71.5 jit_solution(12657176938660159050)
XLA Ops:
  0.6 3.0 %shard_map.84 = (f32[2,2,2,128,128]{4,3,2,1,0:T(8,128)S(1)}, f32[2,2,2,128,128]{4,3,2,1,0:T(8,128)}, f32[2,2,128,128]{3,2,1,0:T(8,128)S(1)}) custom-call(bf16[128,2048]{1,0:T(8,128)(2,1)} %bitcast.109, bf16[128,2048]{1,0:T(8,128)(2,1)} %bitcast.115, bf16[128,2048]{1,0:T(8,128)(2,1)} %bitcast.121, bf16[128,2048]{1,0:T(8,128)(2,1)} %bitcast.127, ...), custom_call_target="tpu_custom_call" | custom-call | flops 134217728 | bytes 3932160 | tf_op jit(solution)/shard_map/pallas_call | solution.py:62
  4.1 1.5 %collective-permute-done.refs_4_ = f32[2,2,2,128,128]{4,3,2,1,0:T(8,128)S(1)} collective-permute-done((f32[2,2,2,128,128]{4,3,2,1,0:T(8,128)S(1)}, f32[2,2,2,128,128]{4,3,2,1,0:T(8,128)S(1)}, u32[]{:S(2)}, u32[]{:S(2)}) %collective-permute-start) | collective-permute-done | bytes 524320 | tf_op jit(solution)/shard_map/ppermute | solution.py:380
  5.7 3.0 %collective-permute-start.3 = (f32[2,2,128,128]{3,2,1,0:T(8,128)S(1)}, f32[2,2,128,128]{3,2,1,0:T(8,128)S(1)}, u32[]{:S(2)}, u32[]{:S(2)}) collective-permute-start(f32[2,2,128,128]{3,2,1,0:T(8,128)S(1)} %fusion.3), channel_id=1, source_target_pairs={{0,2},{1,3},{2,0},{3,1},{4,6},{5,7},{6,4},{7,5},{8,10},{9,11},{10,... | collective-permute-start | bytes 786440 | tf_op jit(solution)/shard_map/ppermute | solution.py:384
  8.7 3.0 %shard_map.85 = (f32[2,2,2,128,128]{4,3,2,1,0:T(8,128)S(1)}, f32[2,2,2,128,128]{4,3,2,1,0:T(8,128)}, f32[2,2,128,128]{3,2,1,0:T(8,128)S(1)}) custom-call(bf16[128,2048]{1,0:T(8,128)(2,1)} %bitcast.110, bf16[128,2048]{1,0:T(8,128)(2,1)} %bitcast.116, bf16[128,2048]{1,0:T(8,128)(2,1)} %bitcast.122, bf16[128,2048]{1,0:T(8,128)(2,1)} %bitcast.128, ...), custom_call_target="tpu_custom_call" | custom-call | flops 134217728 | bytes 3932160 | tf_op jit(solution)/shard_map/pallas_call | solution.py:62
  11.8 3.6 %shard_map.86 = (f32[8,128,128]{2,1,0:T(8,128)}, bf16[2,8,128,128]{3,2,1,0:T(8,128)(2,1)}) custom-call(bf16[128,2048]{1,0:T(8,128)(2,1)} %bitcast.111, bf16[128,2048]{1,0:T(8,128)(2,1)} %bitcast.117, bf16[128,2048]{1,0:T(8,128)(2,1)} %bitcast.123, bf16[128,2048]{1,0:T(8,128)(2,1)} %bitcast.129, bf16[16,128,128]{2,1,0:T(8,128)(2,1)} %refs_9_.1), custom_call_target="tpu_custom_call" | custom-call | flops 301989888 | bytes 3670016 | tf_op jit(solution)/shard_map/pallas_call | solution.py:62
  15.6 1.7 %collective-permute-start.4 = (f32[2,128,128]{2,1,0:T(8,128)S(1)}, f32[2,128,128]{2,1,0:T(8,128)S(1)}, u32[]{:S(2)}, u32[]{:S(2)}) collective-permute-start(f32[2,128,128]{2,1,0:T(8,128)S(1)} %select_bitcast_fusion.4), channel_id=1, source_target_pairs={{0,4},{1,5},{2,6},{3,7},{4,0},{5,1},{6,2},{7,3},{8,12},{9,13},{10,... | collective-permute-start | bytes 393224 | tf_op jit(solution)/shard_map/ppermute | solution.py:394
  17.3 1.5 %collective-permute-start.2 = (f32[2,2,128,128]{3,2,1,0:T(8,128)S(1)}, f32[2,2,128,128]{3,2,1,0:T(8,128)S(1)}, u32[]{:S(2)}, u32[]{:S(2)}) collective-permute-start(f32[2,2,128,128]{3,2,1,0:T(8,128)S(1)} %fusion.1), channel_id=1, source_target_pairs={{0,2},{1,3},{2,0},{3,1},{4,6},{5,7},{6,4},{7,5},{8,10},{9,11},{10,... | collective-permute-start | bytes 786440 | tf_op jit(solution)/shard_map/ppermute | solution.py:384
  18.8 3.5 %shard_map.87 = (f32[8,128,128]{2,1,0:T(8,128)}, bf16[2,8,128,128]{3,2,1,0:T(8,128)(2,1)}) custom-call(bf16[128,2048]{1,0:T(8,128)(2,1)} %bitcast.112, bf16[128,2048]{1,0:T(8,128)(2,1)} %bitcast.118, bf16[128,2048]{1,0:T(8,128)(2,1)} %bitcast.124, bf16[128,2048]{1,0:T(8,128)(2,1)} %bitcast.130, bf16[16,128,128]{2,1,0:T(8,128)(2,1)} %refs_9_.1), custom_call_target="tpu_custom_call" | custom-call | flops 301989888 | bytes 3670016 | tf_op jit(solution)/shard_map/pallas_call | solution.py:62
  22.4 3.2 %collective-permute-done.2 = f32[2,2,128,128]{3,2,1,0:T(8,128)S(1)} collective-permute-done((f32[2,2,128,128]{3,2,1,0:T(8,128)S(1)}, f32[2,2,128,128]{3,2,1,0:T(8,128)S(1)}, u32[]{:S(2)}, u32[]{:S(2)}) %collective-permute-start.2) | collective-permute-done | bytes 262176 | tf_op jit(solution)/shard_map/ppermute | solution.py:384
  26.2 2.4 %collective-permute-start.8 = (f32[2,128,128]{2,1,0:T(8,128)S(1)}, f32[2,128,128]{2,1,0:T(8,128)S(1)}, u32[]{:S(2)}, u32[]{:S(2)}) collective-permute-start(f32[2,128,128]{2,1,0:T(8,128)S(1)} %bitcast_add_fusion), channel_id=1, source_target_pairs={{0,4},{1,5},{2,6},{3,7},{4,0},{5,1},{6,2},{7,3},{8,12},{9,13},{10,... | collective-permute-start | bytes 393224 | tf_op jit(solution)/shard_map/ppermute | solution.py:394
  28.6 3.2 %collective-permute-done.5 = f32[2,128,128]{2,1,0:T(8,128)S(1)} collective-permute-done((f32[2,128,128]{2,1,0:T(8,128)S(1)}, f32[2,128,128]{2,1,0:T(8,128)S(1)}, u32[]{:S(2)}, u32[]{:S(2)}) %collective-permute-start.5) | collective-permute-done | bytes 131104 | tf_op jit(solution)/shard_map/ppermute | solution.py:394
  31.9 1.3 %collective-permute-done.8 = f32[2,128,128]{2,1,0:T(8,128)S(1)} collective-permute-done((f32[2,128,128]{2,1,0:T(8,128)S(1)}, f32[2,128,128]{2,1,0:T(8,128)S(1)}, u32[]{:S(2)}, u32[]{:S(2)}) %collective-permute-start.8) | collective-permute-done | bytes 131104 | tf_op jit(solution)/shard_map/ppermute | solution.py:394
  33.4 0.8 %collective-permute-start.10 = (f32[2,2,128,128]{3,2,1,0:T(8,128)S(1)}, f32[2,2,128,128]{3,2,1,0:T(8,128)S(1)}, u32[]{:S(2)}, u32[]{:S(2)}) collective-permute-start(f32[2,2,128,128]{3,2,1,0:T(8,128)S(1)} %get-tuple-element.80), channel_id=1, source_target_pairs={{0,2},{1,3},{2,0},{3,1},{4,6},{5,7},{6,4},{7,5},{8,10},{9,11},{10,... | collective-permute-start | bytes 786440 | tf_op jit(solution)/shard_map/ppermute | solution.py:384
  34.2 3.8 %collective-permute-start.9 = (f32[2,128,128]{2,1,0:T(8,128)S(1)}, f32[2,128,128]{2,1,0:T(8,128)S(1)}, u32[]{:S(2)}, u32[]{:S(2)}) collective-permute-start(f32[2,128,128]{2,1,0:T(8,128)S(1)} %bitcast_add_fusion.3), channel_id=1, source_target_pairs={{0,4},{1,5},{2,6},{3,7},{4,0},{5,1},{6,2},{7,3},{8,12},{9,13},{10,... | collective-permute-start | bytes 393224 | tf_op jit(solution)/shard_map/ppermute | solution.py:394
  38.1 2.8 %collective-permute-done.10.refs_1_ = f32[2,2,128,128]{3,2,1,0:T(8,128)S(1)} collective-permute-done((f32[2,2,128,128]{3,2,1,0:T(8,128)S(1)}, f32[2,2,128,128]{3,2,1,0:T(8,128)S(1)}, u32[]{:S(2)}, u32[]{:S(2)}) %collective-permute-start.10) | collective-permute-done | bytes 262176 | tf_op jit(solution)/shard_map/ppermute | solution.py:384
  41.3 0.8 %collective-permute-start.11 = (f32[2,2,128,128]{3,2,1,0:T(8,128)S(1)}, f32[2,2,128,128]{3,2,1,0:T(8,128)S(1)}, u32[]{:S(2)}, u32[]{:S(2)}) collective-permute-start(f32[2,2,128,128]{3,2,1,0:T(8,128)S(1)} %get-tuple-element.81), channel_id=1, source_target_pairs={{0,2},{1,3},{2,0},{3,1},{4,6},{5,7},{6,4},{7,5},{8,10},{9,11},{10,... | collective-permute-start | bytes 786440 | tf_op jit(solution)/shard_map/ppermute | solution.py:384
  42.6 0.7 shard_map.88
  43.5 4.3 %shard_map.89 = (bf16[128,2048]{1,0:T(8,128)(2,1)}, bf16[128,2048]{1,0:T(8,128)(2,1)}, bf16[128,2048]{1,0:T(8,128)(2,1)}) custom-call(f32[2,2,128,128]{3,2,1,0:T(8,128)S(1)} %get-tuple-element.77.refs_0_, f32[2,2,128,128]{3,2,1,0:T(8,128)S(1)} %collective-permute-done.10.refs_1_, f32[2,2,128,128]{3,2,1,0:T(8,128)S(1)} %collective-permute-done.13.refs_2_, ...), custom_call_target="tpu_custom_call" | custom-call | flops 4026531 | bytes 57671 | tf_op jit(solution)/shard_map/pallas_call | solution.py:62
  47.9 2.1 %collective-permute-done.11.refs_1_ = f32[2,2,128,128]{3,2,1,0:T(8,128)S(1)} collective-permute-done((f32[2,2,128,128]{3,2,1,0:T(8,128)S(1)}, f32[2,2,128,128]{3,2,1,0:T(8,128)S(1)}, u32[]{:S(2)}, u32[]{:S(2)}) %collective-permute-start.11) | collective-permute-done | bytes 262176 | tf_op jit(solution)/shard_map/ppermute | solution.py:384
  50.3 1.5 %collective-permute-done.15.refs_3_ = f32[2,2,128,128]{3,2,1,0:T(8,128)S(1)} collective-permute-done((f32[2,2,128,128]{3,2,1,0:T(8,128)S(1)}, f32[2,2,128,128]{3,2,1,0:T(8,128)S(1)}, u32[]{:S(2)}, u32[]{:S(2)}) %collective-permute-start.15) | collective-permute-done | bytes 262176 | tf_op jit(solution)/shard_map/ppermute | solution.py:380
  51.7 0.7 shard_map.90
  52.7 1.4 %collective-permute-done.17 = f32[8,64,128]{2,1,0:T(8,128)S(1)} collective-permute-done((f32[8,64,128]{2,1,0:T(8,128)S(1)}, f32[8,64,128]{2,1,0:T(8,128)S(1)}, u32[]{:S(2)}, u32[]{:S(2)}) %collective-permute-start.17) | collective-permute-done | bytes 262176 | tf_op jit(solution)/shard_map/ppermute | solution.py:380
  54.1 1.8 %collective-permute-start.20 = (f32[4,64,128]{2,1,0:T(8,128)S(1)}, f32[4,64,128]{2,1,0:T(8,128)S(1)}, u32[]{:S(2)}, u32[]{:S(2)}) collective-permute-start(f32[4,64,128]{2,1,0:T(8,128)S(1)} %pad_maximum_fusion.4), channel_id=1, source_target_pairs={{0,18},{1,19},{2,16},{3,17},{4,22},{5,23},{6,20},{7,21},{8,26},{9,... | collective-permute-start | bytes 393224 | tf_op jit(solution)/shard_map/ppermute | solution.py:428
  55.9 0.6 collective-permute-start.19
  56.5 1.3 %collective-permute-start.18 = (f32[4,64,128]{2,1,0:T(8,128)S(1)}, f32[4,64,128]{2,1,0:T(8,128)S(1)}, u32[]{:S(2)}, u32[]{:S(2)}) collective-permute-start(f32[4,64,128]{2,1,0:T(8,128)S(1)} %pad_maximum_fusion.2), channel_id=1, source_target_pairs={{0,2},{1,3},{2,0},{3,1},{4,6},{5,7},{6,4},{7,5},{8,10},{9,11},{10,... | collective-permute-start | bytes 393224 | tf_op jit(solution)/shard_map/ppermute | solution.py:428
  57.8 4.3 %shard_map.91 = (bf16[128,2048]{1,0:T(8,128)(2,1)}, bf16[128,2048]{1,0:T(8,128)(2,1)}, bf16[128,2048]{1,0:T(8,128)(2,1)}) custom-call(f32[2,2,128,128]{3,2,1,0:T(8,128)S(1)} %get-tuple-element.79.refs_0_, f32[2,2,128,128]{3,2,1,0:T(8,128)S(1)} %collective-permute-done.11.refs_1_, ...), custom_call_target="tpu_custom_call", output_to_operand_aliasing={{0}: (10, {}), {1}: (11, {}), {2}: (12, {})} | custom-call | flops 4026531 | bytes 73400 | tf_op jit(solution)/shard_map/pallas_call | solution.py:62
  62.8 0.7 collective-permute-done.18
  63.5 2.5 %collective-permute-start.23 = (f32[64,128]{1,0:T(8,128)S(1)}, f32[64,128]{1,0:T(8,128)S(1)}, u32[]{:S(2)}, u32[]{:S(2)}) collective-permute-start(f32[64,128]{1,0:T(8,128)S(1)} %get-tuple-element.95), channel_id=1, source_target_pairs={{0,12},{1,13},{2,14},{3,15},{4,8},{5,9},{6,10},{7,11},{8,4},{9,5},... | collective-permute-start | bytes 98312 | tf_op jit(solution)/shard_map/ppermute | solution.py:443
  66.1 1.9 %collective-permute-start.21 = (f32[64,128]{1,0:T(8,128)S(1)}, f32[64,128]{1,0:T(8,128)S(1)}, u32[]{:S(2)}, u32[]{:S(2)}) collective-permute-start(f32[64,128]{1,0:T(8,128)S(1)} %get-tuple-element.94), channel_id=1, source_target_pairs={{0,4},{1,5},{2,6},{3,7},{4,0},{5,1},{6,2},{7,3},{8,12},{9,13},{10,... | collective-permute-start | bytes 98312 | tf_op jit(solution)/shard_map/ppermute | solution.py:443
  68.0 1.3 %collective-permute-done.23 = f32[64,128]{1,0:T(8,128)S(1)} collective-permute-done((f32[64,128]{1,0:T(8,128)S(1)}, f32[64,128]{1,0:T(8,128)S(1)}, u32[]{:S(2)}, u32[]{:S(2)}) %collective-permute-start.23) | collective-permute-done | bytes 32800 | tf_op jit(solution)/shard_map/ppermute | solution.py:443
  69.3 1.6 %collective-permute-done.22 = f32[64,128]{1,0:T(8,128)S(1)} collective-permute-done((f32[64,128]{1,0:T(8,128)S(1)}, f32[64,128]{1,0:T(8,128)S(1)}, u32[]{:S(2)}, u32[]{:S(2)}) %collective-permute-start.22) | collective-permute-done | bytes 32800 | tf_op jit(solution)/shard_map/ppermute | solution.py:443
  70.9 0.6 fusion.14
  (64 shorter events, 3.9 us)
Async XLA Ops:
  3.6 2.0 %collective-permute-start = (f32[2,2,2,128,128]{4,3,2,1,0:T(8,128)S(1)}, f32[2,2,2,128,128]{4,3,2,1,0:T(8,128)S(1)}, u32[]{:S(2)}, u32[]{:S(2)}) collective-permute-start(f32[2,2,2,128,128]{4,3,2,1,0:T(8,128)S(1)} %get-tuple-element.41), channel_id=1, source_target_pairs={{0,1},{1,0},{2,3},{3,2},{4,5},{5,4},{6,7},{7,6},{8,9},{9,8},{10,11... | collective-permute-start | bytes 1572872 | tf_op jit(solution)/shard_map/ppermute | solution.py:380
  5.7 9.7 %collective-permute-start.3 = (f32[2,2,128,128]{3,2,1,0:T(8,128)S(1)}, f32[2,2,128,128]{3,2,1,0:T(8,128)S(1)}, u32[]{:S(2)}, u32[]{:S(2)}) collective-permute-start(f32[2,2,128,128]{3,2,1,0:T(8,128)S(1)} %fusion.3), channel_id=1, source_target_pairs={{0,2},{1,3},{2,0},{3,1},{4,6},{5,7},{6,4},{7,5},{8,10},{9,11},{10,... | collective-permute-start | bytes 786440 | tf_op jit(solution)/shard_map/ppermute | solution.py:384
  11.7 3.8 %collective-permute-start.1 = (f32[2,2,2,128,128]{4,3,2,1,0:T(8,128)S(1)}, f32[2,2,2,128,128]{4,3,2,1,0:T(8,128)S(1)}, u32[]{:S(2)}, u32[]{:S(2)}) collective-permute-start(f32[2,2,2,128,128]{4,3,2,1,0:T(8,128)S(1)} %get-tuple-element.44), channel_id=1, source_target_pairs={{0,1},{1,0},{2,3},{3,2},{4,5},{5,4},{6,7},{7,6},{8,9},{9,8},{10,11... | collective-permute-start | bytes 1572872 | tf_op jit(solution)/shard_map/ppermute | solution.py:380
  11.8 3.6 %copy-start.5 = (f32[2,2,2,128,128]{4,3,2,1,0:T(8,128)S(1)}, f32[2,2,2,128,128]{4,3,2,1,0:T(8,128)}, u32[]{:S(2)}) copy-start(f32[2,2,2,128,128]{4,3,2,1,0:T(8,128)} %get-tuple-element.46) | copy-start | bytes 1572868
  15.6 6.8 %collective-permute-start.4 = (f32[2,128,128]{2,1,0:T(8,128)S(1)}, f32[2,128,128]{2,1,0:T(8,128)S(1)}, u32[]{:S(2)}, u32[]{:S(2)}) collective-permute-start(f32[2,128,128]{2,1,0:T(8,128)S(1)} %select_bitcast_fusion.4), channel_id=1, source_target_pairs={{0,4},{1,5},{2,6},{3,7},{4,0},{5,1},{6,2},{7,3},{8,12},{9,13},{10,... | collective-permute-start | bytes 393224 | tf_op jit(solution)/shard_map/ppermute | solution.py:394
  17.3 8.3 %collective-permute-start.2 = (f32[2,2,128,128]{3,2,1,0:T(8,128)S(1)}, f32[2,2,128,128]{3,2,1,0:T(8,128)S(1)}, u32[]{:S(2)}, u32[]{:S(2)}) collective-permute-start(f32[2,2,128,128]{3,2,1,0:T(8,128)S(1)} %fusion.1), channel_id=1, source_target_pairs={{0,2},{1,3},{2,0},{3,1},{4,6},{5,7},{6,4},{7,5},{8,10},{9,11},{10,... | collective-permute-start | bytes 786440 | tf_op jit(solution)/shard_map/ppermute | solution.py:384
  22.3 3.3 %copy-start.4 = (f32[2,2,2,128,128]{4,3,2,1,0:T(8,128)S(1)}, f32[2,2,2,128,128]{4,3,2,1,0:T(8,128)}, u32[]{:S(2)}) copy-start(f32[2,2,2,128,128]{4,3,2,1,0:T(8,128)} %get-tuple-element.43) | copy-start | bytes 1572868
  22.4 3.8 %collective-permute-start.6 = (f32[2,128,128]{2,1,0:T(8,128)S(1)}, f32[2,128,128]{2,1,0:T(8,128)S(1)}, u32[]{:S(2)}, u32[]{:S(2)}) collective-permute-start(f32[2,128,128]{2,1,0:T(8,128)S(1)} %bitcast_add_fusion.1), channel_id=1, source_target_pairs={{0,1},{1,0},{2,3},{3,2},{4,8},{5,9},{6,10},{7,11},{8,4},{9,5},{10,... | collective-permute-start | bytes 393224 | tf_op jit(solution)/shard_map/ppermute | solution.py:394
  25.7 6.1 %collective-permute-start.5 = (f32[2,128,128]{2,1,0:T(8,128)S(1)}, f32[2,128,128]{2,1,0:T(8,128)S(1)}, u32[]{:S(2)}, u32[]{:S(2)}) collective-permute-start(f32[2,128,128]{2,1,0:T(8,128)S(1)} %select_bitcast_fusion.5), channel_id=1, source_target_pairs={{0,4},{1,5},{2,6},{3,7},{4,0},{5,1},{6,2},{7,3},{8,12},{9,13},{10,... | collective-permute-start | bytes 393224 | tf_op jit(solution)/shard_map/ppermute | solution.py:394
  26.2 7.0 %collective-permute-start.8 = (f32[2,128,128]{2,1,0:T(8,128)S(1)}, f32[2,128,128]{2,1,0:T(8,128)S(1)}, u32[]{:S(2)}, u32[]{:S(2)}) collective-permute-start(f32[2,128,128]{2,1,0:T(8,128)S(1)} %bitcast_add_fusion), channel_id=1, source_target_pairs={{0,4},{1,5},{2,6},{3,7},{4,0},{5,1},{6,2},{7,3},{8,12},{9,13},{10,... | collective-permute-start | bytes 393224 | tf_op jit(solution)/shard_map/ppermute | solution.py:394
  31.8 2.4 %collective-permute-start.7 = (f32[2,128,128]{2,1,0:T(8,128)S(1)}, f32[2,128,128]{2,1,0:T(8,128)S(1)}, u32[]{:S(2)}, u32[]{:S(2)}) collective-permute-start(f32[2,128,128]{2,1,0:T(8,128)S(1)} %bitcast_add_fusion.2), channel_id=1, source_target_pairs={{0,1},{1,0},{2,3},{3,2},{4,8},{5,9},{6,10},{7,11},{8,4},{9,5},{10,... | collective-permute-start | bytes 393224 | tf_op jit(solution)/shard_map/ppermute | solution.py:394
  33.4 7.5 %collective-permute-start.10 = (f32[2,2,128,128]{3,2,1,0:T(8,128)S(1)}, f32[2,2,128,128]{3,2,1,0:T(8,128)S(1)}, u32[]{:S(2)}, u32[]{:S(2)}) collective-permute-start(f32[2,2,128,128]{3,2,1,0:T(8,128)S(1)} %get-tuple-element.80), channel_id=1, source_target_pairs={{0,2},{1,3},{2,0},{3,1},{4,6},{5,7},{6,4},{7,5},{8,10},{9,11},{10,... | collective-permute-start | bytes 786440 | tf_op jit(solution)/shard_map/ppermute | solution.py:384
  34.2 8.1 %collective-permute-start.13 = (f32[2,2,128,128]{3,2,1,0:T(8,128)S(1)}, f32[2,2,128,128]{3,2,1,0:T(8,128)S(1)}, u32[]{:S(2)}, u32[]{:S(2)}) collective-permute-start(f32[2,2,128,128]{3,2,1,0:T(8,128)S(1)} %get-tuple-element.76), channel_id=1, source_target_pairs={{0,1},{1,0},{2,3},{3,2},{4,5},{5,4},{6,7},{7,6},{8,9},{9,8},{10,11... | collective-permute-start | bytes 786440 | tf_op jit(solution)/shard_map/ppermute | solution.py:380
  34.2 6.8 %collective-permute-start.9 = (f32[2,128,128]{2,1,0:T(8,128)S(1)}, f32[2,128,128]{2,1,0:T(8,128)S(1)}, u32[]{:S(2)}, u32[]{:S(2)}) collective-permute-start(f32[2,128,128]{2,1,0:T(8,128)S(1)} %bitcast_add_fusion.3), channel_id=1, source_target_pairs={{0,4},{1,5},{2,6},{3,7},{4,0},{5,1},{6,2},{7,3},{8,12},{9,13},{10,... | collective-permute-start | bytes 393224 | tf_op jit(solution)/shard_map/ppermute | solution.py:394
  40.9 1.6 %collective-permute-start.14 = (f32[2,2,128,128]{3,2,1,0:T(8,128)S(1)}, f32[2,2,128,128]{3,2,1,0:T(8,128)S(1)}, u32[]{:S(2)}, u32[]{:S(2)}) collective-permute-start(f32[2,2,128,128]{3,2,1,0:T(8,128)S(1)} %fusion.5), channel_id=1, source_target_pairs={{0,1},{1,0},{2,3},{3,2},{4,5},{5,4},{6,7},{7,6},{8,9},{9,8},{10,11... | collective-permute-start | bytes 786440 | tf_op jit(solution)/shard_map/ppermute | solution.py:380
  41.1 1.5 %copy-start.2 = (f32[8,128,128]{2,1,0:T(8,128)S(1)}, f32[8,128,128]{2,1,0:T(8,128)}, u32[]{:S(2)}) copy-start(f32[8,128,128]{2,1,0:T(8,128)} %get-tuple-element.53.refs_5_) | copy-start | bytes 1572868
  41.1 1.5 %copy-start.3 = (bf16[2,8,128,128]{3,2,1,0:T(8,128)(2,1)S(1)}, bf16[2,8,128,128]{3,2,1,0:T(8,128)(2,1)}, u32[]{:S(2)}) copy-start(bf16[2,8,128,128]{3,2,1,0:T(8,128)(2,1)} %get-tuple-element.54.refs_6_) | copy-start | bytes 1572868
  41.3 8.8 %collective-permute-start.11 = (f32[2,2,128,128]{3,2,1,0:T(8,128)S(1)}, f32[2,2,128,128]{3,2,1,0:T(8,128)S(1)}, u32[]{:S(2)}, u32[]{:S(2)}) collective-permute-start(f32[2,2,128,128]{3,2,1,0:T(8,128)S(1)} %get-tuple-element.81), channel_id=1, source_target_pairs={{0,2},{1,3},{2,0},{3,1},{4,6},{5,7},{6,4},{7,5},{8,10},{9,11},{10,... | collective-permute-start | bytes 786440 | tf_op jit(solution)/shard_map/ppermute | solution.py:384
  42.1 7.9 %collective-permute-start.12 = (f32[2,2,128,128]{3,2,1,0:T(8,128)S(1)}, f32[2,2,128,128]{3,2,1,0:T(8,128)S(1)}, u32[]{:S(2)}, u32[]{:S(2)}) collective-permute-start(f32[2,2,128,128]{3,2,1,0:T(8,128)S(1)} %get-tuple-element.78), channel_id=1, source_target_pairs={{0,1},{1,0},{2,3},{3,2},{4,5},{5,4},{6,7},{7,6},{8,9},{9,8},{10,11... | collective-permute-start | bytes 786440 | tf_op jit(solution)/shard_map/ppermute | solution.py:380
  43.3 6.9 %collective-permute-start.16 = (f32[8,64,128]{2,1,0:T(8,128)S(1)}, f32[8,64,128]{2,1,0:T(8,128)S(1)}, u32[]{:S(2)}, u32[]{:S(2)}) collective-permute-start(f32[8,64,128]{2,1,0:T(8,128)S(1)} %get-tuple-element.61), channel_id=1, source_target_pairs={{0,1},{1,0},{2,3},{3,2},{4,5},{5,4},{6,7},{7,6},{8,9},{9,8},{10,11... | collective-permute-start | bytes 786440 | tf_op jit(solution)/shard_map/ppermute | solution.py:380
  50.0 1.7 %copy-start.1 = (bf16[2,8,128,128]{3,2,1,0:T(8,128)(2,1)S(1)}, bf16[2,8,128,128]{3,2,1,0:T(8,128)(2,1)}, u32[]{:S(2)}) copy-start(bf16[2,8,128,128]{3,2,1,0:T(8,128)(2,1)} %get-tuple-element.49.refs_6_) | copy-start | bytes 1572868
  50.1 1.6 %copy-start = (f32[8,128,128]{2,1,0:T(8,128)S(1)}, f32[8,128,128]{2,1,0:T(8,128)}, u32[]{:S(2)}) copy-start(f32[8,128,128]{2,1,0:T(8,128)} %get-tuple-element.48.refs_5_) | copy-start | bytes 1572868
  50.1 1.6 %collective-permute-start.15 = (f32[2,2,128,128]{3,2,1,0:T(8,128)S(1)}, f32[2,2,128,128]{3,2,1,0:T(8,128)S(1)}, u32[]{:S(2)}, u32[]{:S(2)}) collective-permute-start(f32[2,2,128,128]{3,2,1,0:T(8,128)S(1)} %fusion.4), channel_id=1, source_target_pairs={{0,1},{1,0},{2,3},{3,2},{4,5},{5,4},{6,7},{7,6},{8,9},{9,8},{10,11... | collective-permute-start | bytes 786440 | tf_op jit(solution)/shard_map/ppermute | solution.py:380
  52.4 1.6 %collective-permute-start.17 = (f32[8,64,128]{2,1,0:T(8,128)S(1)}, f32[8,64,128]{2,1,0:T(8,128)S(1)}, u32[]{:S(2)}, u32[]{:S(2)}) collective-permute-start(f32[8,64,128]{2,1,0:T(8,128)S(1)} %get-tuple-element.69), channel_id=1, source_target_pairs={{0,1},{1,0},{2,3},{3,2},{4,5},{5,4},{6,7},{7,6},{8,9},{9,8},{10,11... | collective-permute-start | bytes 786440 | tf_op jit(solution)/shard_map/ppermute | solution.py:380
  54.1 8.1 %collective-permute-start.20 = (f32[4,64,128]{2,1,0:T(8,128)S(1)}, f32[4,64,128]{2,1,0:T(8,128)S(1)}, u32[]{:S(2)}, u32[]{:S(2)}) collective-permute-start(f32[4,64,128]{2,1,0:T(8,128)S(1)} %pad_maximum_fusion.4), channel_id=1, source_target_pairs={{0,18},{1,19},{2,16},{3,17},{4,22},{5,23},{6,20},{7,21},{8,26},{9,... | collective-permute-start | bytes 393224 | tf_op jit(solution)/shard_map/ppermute | solution.py:428
  55.9 6.8 %collective-permute-start.19 = (f32[4,64,128]{2,1,0:T(8,128)S(1)}, f32[4,64,128]{2,1,0:T(8,128)S(1)}, u32[]{:S(2)}, u32[]{:S(2)}) collective-permute-start(f32[4,64,128]{2,1,0:T(8,128)S(1)} %pad_maximum_fusion.3), channel_id=1, source_target_pairs={{0,16},{1,17},{2,18},{3,19},{4,20},{5,21},{6,22},{7,23},{8,24},{9,... | collective-permute-start | bytes 393224 | tf_op jit(solution)/shard_map/ppermute | solution.py:428
  56.5 6.9 %collective-permute-start.18 = (f32[4,64,128]{2,1,0:T(8,128)S(1)}, f32[4,64,128]{2,1,0:T(8,128)S(1)}, u32[]{:S(2)}, u32[]{:S(2)}) collective-permute-start(f32[4,64,128]{2,1,0:T(8,128)S(1)} %pad_maximum_fusion.2), channel_id=1, source_target_pairs={{0,2},{1,3},{2,0},{3,1},{4,6},{5,7},{6,4},{7,5},{8,10},{9,11},{10,... | collective-permute-start | bytes 393224 | tf_op jit(solution)/shard_map/ppermute | solution.py:428
  63.5 5.8 %collective-permute-start.23 = (f32[64,128]{1,0:T(8,128)S(1)}, f32[64,128]{1,0:T(8,128)S(1)}, u32[]{:S(2)}, u32[]{:S(2)}) collective-permute-start(f32[64,128]{1,0:T(8,128)S(1)} %get-tuple-element.95), channel_id=1, source_target_pairs={{0,12},{1,13},{2,14},{3,15},{4,8},{5,9},{6,10},{7,11},{8,4},{9,5},... | collective-permute-start | bytes 98312 | tf_op jit(solution)/shard_map/ppermute | solution.py:443
  66.1 4.8 %collective-permute-start.22 = (f32[64,128]{1,0:T(8,128)S(1)}, f32[64,128]{1,0:T(8,128)S(1)}, u32[]{:S(2)}, u32[]{:S(2)}) collective-permute-start(f32[64,128]{1,0:T(8,128)S(1)} %get-tuple-element.96), channel_id=1, source_target_pairs={{0,8},{1,9},{2,10},{3,11},{4,12},{5,13},{6,14},{7,15},{8,0},{9,1},... | collective-permute-start | bytes 98312 | tf_op jit(solution)/shard_map/ppermute | solution.py:443
  66.1 4.8 %collective-permute-start.21 = (f32[64,128]{1,0:T(8,128)S(1)}, f32[64,128]{1,0:T(8,128)S(1)}, u32[]{:S(2)}, u32[]{:S(2)}) collective-permute-start(f32[64,128]{1,0:T(8,128)S(1)} %get-tuple-element.94), channel_id=1, source_target_pairs={{0,4},{1,5},{2,6},{3,7},{4,0},{5,1},{6,2},{7,3},{8,12},{9,13},{10,... | collective-permute-start | bytes 98312 | tf_op jit(solution)/shard_map/ppermute | solution.py:443

commit v7 on v5

--- a/solution.py
+++ b/solution.py
@@ -126,7 +126,7 @@
 
 def states_kernel(plan, chunk, *refs):
     row_refs, maps_ref, sent_ref, kept_ref, given_ref = refs[:4], refs[4], refs[5], refs[6], refs[7]
-    row_bufs, maps_buf, sems = refs[8:12], refs[12], refs[13]
+    row_bufs, maps_buf, out_buf, sems = refs[8:12], refs[12], refs[13], refs[14]
     copies, width = Copies(sems), plan.width
     started = load_chunk(plan, copies, chunk, 0, row_refs, maps_ref, row_bufs, maps_buf)
     q_buf, k_buf, v_buf, g_buf = row_bufs
@@ -145,17 +145,11 @@
         ]
         for place, key_state, query_state in zip(places, key_states, query_states):
             core_turn, chip_turn, i = quarter_of(plan, place)
-
-            @pl.when(core_turn == 1)
-            def _():
-                sent_ref[chip_turn, 0, i] = key_state
-                sent_ref[chip_turn, 1, i] = query_state
-
-            @pl.when(core_turn == 0)
-            def _():
-                kept_ref[chip_turn, 0, i] = key_state
-                kept_ref[chip_turn, 1, i] = query_state
-    given_ref[...] = kept_ref[1]
+            out_buf[core_turn, chip_turn, 0, i] = key_state
+            out_buf[core_turn, chip_turn, 1, i] = query_state
+    sent_ref[...] = out_buf[1]
+    kept_ref[...] = out_buf[0]
+    given_ref[...] = out_buf[0, 1]
 
 
 def block_states(plan, chunk, rows, maps):
@@ -166,7 +160,7 @@
         (*rows, maps),
         [state, state, jax.ShapeDtypeStruct(shape[1:], F32)],
         matmuls(plan, 4 * plan.in_chunk),
-        row_scratch(plan, plan.in_chunk),
+        row_scratch(plan, plan.in_chunk) + [pltpu.VMEM((2,) + shape, F32)],
         chunk_copies(plan),
         near_out=(0, 1, 2),
         limit=STATES_LIMIT,

time: 71.6 us -> 71.6 us (level)
  no operation moved by 1% of the time
where the time goes in v7:
time: 71.6 us; the launch traced here: 71.3 us
  starting transfers between devices  24.4 us (34%)
  Pallas kernels  23 us (32%)
  waiting for transfers between devices  21.3 us (30%)
  other arithmetic  1.56 us (2%)
  between operations  1.03 us (1%)
    pallas_call x8, Pallas kernels, call(): pl.pallas_call(body, out_shape=shapes, in_specs=specs(len(operands), near...  23 us
    ppermute x6, starting transfers between devices, chain_swap(): return lax.ppermute(state, 'context', steps)  8.71 us
    ppermute x4, waiting for transfers between devices, swap_chip(): lax.ppermute(state, 'context', [(i, i ^ 2) for i in range(plan.ranks)])  8.06 us
    ppermute x4, starting transfers between devices, swap_chip(): lax.ppermute(state, 'context', [(i, i ^ 2) for i in range(plan.ranks)])  6.11 us
    ppermute x8, waiting for transfers between devices, swap_core(): lax.ppermute(state, 'context', [(i, i ^ 1) for i in range(plan.ranks)])  4.68 us
    ppermute x3, starting transfers between devices, group_sum(): result = result + lax.ppermute(sent, 'context', steps)  4.45 us
    ppermute x6, waiting for transfers between devices, chain_swap(): return lax.ppermute(state, 'context', steps)  4.38 us
    ppermute x3, starting transfers between devices, plane_sums(): plane = plane + lax.ppermute(sent, ('dp', 'context'), steps)  3.68 us
  transfers between devices with their start and end apart: 24, of which 13 were waited for; matrix products, arithmetic and copies ran while one was open for 1% of the time, Pallas kernels for 27%

profile of v7, /device:TPU:0, one launch (start us, length us, event | category | flops | bytes accessed | tf_op | source)
XLA Modules:
  0.0 71.3 jit_solution(17376847365866532057)
XLA Ops:
  0.6 3.0 %shard_map.84 = (f32[2,2,2,128,128]{4,3,2,1,0:T(8,128)S(1)}, f32[2,2,2,128,128]{4,3,2,1,0:T(8,128)}, f32[2,2,128,128]{3,2,1,0:T(8,128)S(1)}) custom-call(bf16[128,2048]{1,0:T(8,128)(2,1)} %bitcast.109, bf16[128,2048]{1,0:T(8,128)(2,1)} %bitcast.115, bf16[128,2048]{1,0:T(8,128)(2,1)} %bitcast.121, bf16[128,2048]{1,0:T(8,128)(2,1)} %bitcast.127, ...), custom_call_target="tpu_custom_call" | custom-call | flops 134217728 | bytes 3932160 | tf_op jit(solution)/shard_map/pallas_call | solution.py:59
  4.1 1.5 %collective-permute-done.refs_4_ = f32[2,2,2,128,128]{4,3,2,1,0:T(8,128)S(1)} collective-permute-done((f32[2,2,2,128,128]{4,3,2,1,0:T(8,128)S(1)}, f32[2,2,2,128,128]{4,3,2,1,0:T(8,128)S(1)}, u32[]{:S(2)}, u32[]{:S(2)}) %collective-permute-start) | collective-permute-done | bytes 524320 | tf_op jit(solution)/shard_map/ppermute | solution.py:369
  5.7 3.0 %collective-permute-start.3 = (f32[2,2,128,128]{3,2,1,0:T(8,128)S(1)}, f32[2,2,128,128]{3,2,1,0:T(8,128)S(1)}, u32[]{:S(2)}, u32[]{:S(2)}) collective-permute-start(f32[2,2,128,128]{3,2,1,0:T(8,128)S(1)} %fusion.3), channel_id=1, source_target_pairs={{0,2},{1,3},{2,0},{3,1},{4,6},{5,7},{6,4},{7,5},{8,10},{9,11},{10,... | collective-permute-start | bytes 786440 | tf_op jit(solution)/shard_map/ppermute | solution.py:373
  8.7 3.0 %shard_map.85 = (f32[2,2,2,128,128]{4,3,2,1,0:T(8,128)S(1)}, f32[2,2,2,128,128]{4,3,2,1,0:T(8,128)}, f32[2,2,128,128]{3,2,1,0:T(8,128)S(1)}) custom-call(bf16[128,2048]{1,0:T(8,128)(2,1)} %bitcast.110, bf16[128,2048]{1,0:T(8,128)(2,1)} %bitcast.116, bf16[128,2048]{1,0:T(8,128)(2,1)} %bitcast.122, bf16[128,2048]{1,0:T(8,128)(2,1)} %bitcast.128, ...), custom_call_target="tpu_custom_call" | custom-call | flops 134217728 | bytes 3932160 | tf_op jit(solution)/shard_map/pallas_call | solution.py:59
  11.8 3.6 %shard_map.86 = (f32[8,128,128]{2,1,0:T(8,128)}, bf16[2,8,128,128]{3,2,1,0:T(8,128)(2,1)}) custom-call(bf16[128,2048]{1,0:T(8,128)(2,1)} %bitcast.111, bf16[128,2048]{1,0:T(8,128)(2,1)} %bitcast.117, bf16[128,2048]{1,0:T(8,128)(2,1)} %bitcast.123, bf16[128,2048]{1,0:T(8,128)(2,1)} %bitcast.129, bf16[16,128,128]{2,1,0:T(8,128)(2,1)} %refs_9_.1), custom_call_target="tpu_custom_call" | custom-call | flops 301989888 | bytes 3670016 | tf_op jit(solution)/shard_map/pallas_call | solution.py:59
  15.5 1.8 %collective-permute-start.4 = (f32[2,128,128]{2,1,0:T(8,128)S(1)}, f32[2,128,128]{2,1,0:T(8,128)S(1)}, u32[]{:S(2)}, u32[]{:S(2)}) collective-permute-start(f32[2,128,128]{2,1,0:T(8,128)S(1)} %select_bitcast_fusion.4), channel_id=1, source_target_pairs={{0,4},{1,5},{2,6},{3,7},{4,0},{5,1},{6,2},{7,3},{8,12},{9,13},{10,... | collective-permute-start | bytes 393224 | tf_op jit(solution)/shard_map/ppermute | solution.py:383
  17.3 1.5 %collective-permute-start.2 = (f32[2,2,128,128]{3,2,1,0:T(8,128)S(1)}, f32[2,2,128,128]{3,2,1,0:T(8,128)S(1)}, u32[]{:S(2)}, u32[]{:S(2)}) collective-permute-start(f32[2,2,128,128]{3,2,1,0:T(8,128)S(1)} %fusion.1), channel_id=1, source_target_pairs={{0,2},{1,3},{2,0},{3,1},{4,6},{5,7},{6,4},{7,5},{8,10},{9,11},{10,... | collective-permute-start | bytes 786440 | tf_op jit(solution)/shard_map/ppermute | solution.py:373
  18.8 3.5 %shard_map.87 = (f32[8,128,128]{2,1,0:T(8,128)}, bf16[2,8,128,128]{3,2,1,0:T(8,128)(2,1)}) custom-call(bf16[128,2048]{1,0:T(8,128)(2,1)} %bitcast.112, bf16[128,2048]{1,0:T(8,128)(2,1)} %bitcast.118, bf16[128,2048]{1,0:T(8,128)(2,1)} %bitcast.124, bf16[128,2048]{1,0:T(8,128)(2,1)} %bitcast.130, bf16[16,128,128]{2,1,0:T(8,128)(2,1)} %refs_9_.1), custom_call_target="tpu_custom_call" | custom-call | flops 301989888 | bytes 3670016 | tf_op jit(solution)/shard_map/pallas_call | solution.py:59
  22.4 3.1 %collective-permute-done.2 = f32[2,2,128,128]{3,2,1,0:T(8,128)S(1)} collective-permute-done((f32[2,2,128,128]{3,2,1,0:T(8,128)S(1)}, f32[2,2,128,128]{3,2,1,0:T(8,128)S(1)}, u32[]{:S(2)}, u32[]{:S(2)}) %collective-permute-start.2) | collective-permute-done | bytes 262176 | tf_op jit(solution)/shard_map/ppermute | solution.py:373
  26.1 2.4 %collective-permute-start.8 = (f32[2,128,128]{2,1,0:T(8,128)S(1)}, f32[2,128,128]{2,1,0:T(8,128)S(1)}, u32[]{:S(2)}, u32[]{:S(2)}) collective-permute-start(f32[2,128,128]{2,1,0:T(8,128)S(1)} %bitcast_add_fusion), channel_id=1, source_target_pairs={{0,4},{1,5},{2,6},{3,7},{4,0},{5,1},{6,2},{7,3},{8,12},{9,13},{10,... | collective-permute-start | bytes 393224 | tf_op jit(solution)/shard_map/ppermute | solution.py:383
  28.6 3.1 %collective-permute-done.5 = f32[2,128,128]{2,1,0:T(8,128)S(1)} collective-permute-done((f32[2,128,128]{2,1,0:T(8,128)S(1)}, f32[2,128,128]{2,1,0:T(8,128)S(1)}, u32[]{:S(2)}, u32[]{:S(2)}) %collective-permute-start.5) | collective-permute-done | bytes 131104 | tf_op jit(solution)/shard_map/ppermute | solution.py:383
  31.7 1.3 %collective-permute-done.8 = f32[2,128,128]{2,1,0:T(8,128)S(1)} collective-permute-done((f32[2,128,128]{2,1,0:T(8,128)S(1)}, f32[2,128,128]{2,1,0:T(8,128)S(1)}, u32[]{:S(2)}, u32[]{:S(2)}) %collective-permute-start.8) | collective-permute-done | bytes 131104 | tf_op jit(solution)/shard_map/ppermute | solution.py:383
  33.2 0.8 %collective-permute-start.10 = (f32[2,2,128,128]{3,2,1,0:T(8,128)S(1)}, f32[2,2,128,128]{3,2,1,0:T(8,128)S(1)}, u32[]{:S(2)}, u32[]{:S(2)}) collective-permute-start(f32[2,2,128,128]{3,2,1,0:T(8,128)S(1)} %get-tuple-element.80), channel_id=1, source_target_pairs={{0,2},{1,3},{2,0},{3,1},{4,6},{5,7},{6,4},{7,5},{8,10},{9,11},{10,... | collective-permute-start | bytes 786440 | tf_op jit(solution)/shard_map/ppermute | solution.py:373
  34.1 3.8 %collective-permute-start.9 = (f32[2,128,128]{2,1,0:T(8,128)S(1)}, f32[2,128,128]{2,1,0:T(8,128)S(1)}, u32[]{:S(2)}, u32[]{:S(2)}) collective-permute-start(f32[2,128,128]{2,1,0:T(8,128)S(1)} %bitcast_add_fusion.3), channel_id=1, source_target_pairs={{0,4},{1,5},{2,6},{3,7},{4,0},{5,1},{6,2},{7,3},{8,12},{9,13},{10,... | collective-permute-start | bytes 393224 | tf_op jit(solution)/shard_map/ppermute | solution.py:383
  37.9 2.8 %collective-permute-done.10.refs_1_ = f32[2,2,128,128]{3,2,1,0:T(8,128)S(1)} collective-permute-done((f32[2,2,128,128]{3,2,1,0:T(8,128)S(1)}, f32[2,2,128,128]{3,2,1,0:T(8,128)S(1)}, u32[]{:S(2)}, u32[]{:S(2)}) %collective-permute-start.10) | collective-permute-done | bytes 262176 | tf_op jit(solution)/shard_map/ppermute | solution.py:373
  41.1 0.8 %collective-permute-start.11 = (f32[2,2,128,128]{3,2,1,0:T(8,128)S(1)}, f32[2,2,128,128]{3,2,1,0:T(8,128)S(1)}, u32[]{:S(2)}, u32[]{:S(2)}) collective-permute-start(f32[2,2,128,128]{3,2,1,0:T(8,128)S(1)} %get-tuple-element.81), channel_id=1, source_target_pairs={{0,2},{1,3},{2,0},{3,1},{4,6},{5,7},{6,4},{7,5},{8,10},{9,11},{10,... | collective-permute-start | bytes 786440 | tf_op jit(solution)/shard_map/ppermute | solution.py:373
  42.4 0.7 shard_map.88
  43.4 4.3 %shard_map.89 = (bf16[128,2048]{1,0:T(8,128)(2,1)}, bf16[128,2048]{1,0:T(8,128)(2,1)}, bf16[128,2048]{1,0:T(8,128)(2,1)}) custom-call(f32[2,2,128,128]{3,2,1,0:T(8,128)S(1)} %get-tuple-element.77.refs_0_, f32[2,2,128,128]{3,2,1,0:T(8,128)S(1)} %collective-permute-done.10.refs_1_, f32[2,2,128,128]{3,2,1,0:T(8,128)S(1)} %collective-permute-done.13.refs_2_, ...), custom_call_target="tpu_custom_call" | custom-call | flops 4026531 | bytes 57671 | tf_op jit(solution)/shard_map/pallas_call | solution.py:59
  47.7 2.2 %collective-permute-done.11.refs_1_ = f32[2,2,128,128]{3,2,1,0:T(8,128)S(1)} collective-permute-done((f32[2,2,128,128]{3,2,1,0:T(8,128)S(1)}, f32[2,2,128,128]{3,2,1,0:T(8,128)S(1)}, u32[]{:S(2)}, u32[]{:S(2)}) %collective-permute-start.11) | collective-permute-done | bytes 262176 | tf_op jit(solution)/shard_map/ppermute | solution.py:373
  50.1 1.5 %collective-permute-done.15.refs_3_ = f32[2,2,128,128]{3,2,1,0:T(8,128)S(1)} collective-permute-done((f32[2,2,128,128]{3,2,1,0:T(8,128)S(1)}, f32[2,2,128,128]{3,2,1,0:T(8,128)S(1)}, u32[]{:S(2)}, u32[]{:S(2)}) %collective-permute-start.15) | collective-permute-done | bytes 262176 | tf_op jit(solution)/shard_map/ppermute | solution.py:369
  51.6 0.7 shard_map.90
  52.5 1.4 %collective-permute-done.17 = f32[8,64,128]{2,1,0:T(8,128)S(1)} collective-permute-done((f32[8,64,128]{2,1,0:T(8,128)S(1)}, f32[8,64,128]{2,1,0:T(8,128)S(1)}, u32[]{:S(2)}, u32[]{:S(2)}) %collective-permute-start.17) | collective-permute-done | bytes 262176 | tf_op jit(solution)/shard_map/ppermute | solution.py:369
  54.0 1.7 %collective-permute-start.20 = (f32[4,64,128]{2,1,0:T(8,128)S(1)}, f32[4,64,128]{2,1,0:T(8,128)S(1)}, u32[]{:S(2)}, u32[]{:S(2)}) collective-permute-start(f32[4,64,128]{2,1,0:T(8,128)S(1)} %pad_maximum_fusion.4), channel_id=1, source_target_pairs={{0,18},{1,19},{2,16},{3,17},{4,22},{5,23},{6,20},{7,21},{8,26},{9,... | collective-permute-start | bytes 393224 | tf_op jit(solution)/shard_map/ppermute | solution.py:417
  55.7 0.6 collective-permute-start.19
  56.4 1.3 %collective-permute-start.18 = (f32[4,64,128]{2,1,0:T(8,128)S(1)}, f32[4,64,128]{2,1,0:T(8,128)S(1)}, u32[]{:S(2)}, u32[]{:S(2)}) collective-permute-start(f32[4,64,128]{2,1,0:T(8,128)S(1)} %pad_maximum_fusion.2), channel_id=1, source_target_pairs={{0,2},{1,3},{2,0},{3,1},{4,6},{5,7},{6,4},{7,5},{8,10},{9,11},{10,... | collective-permute-start | bytes 393224 | tf_op jit(solution)/shard_map/ppermute | solution.py:417
  57.7 4.3 %shard_map.91 = (bf16[128,2048]{1,0:T(8,128)(2,1)}, bf16[128,2048]{1,0:T(8,128)(2,1)}, bf16[128,2048]{1,0:T(8,128)(2,1)}) custom-call(f32[2,2,128,128]{3,2,1,0:T(8,128)S(1)} %get-tuple-element.79.refs_0_, f32[2,2,128,128]{3,2,1,0:T(8,128)S(1)} %collective-permute-done.11.refs_1_, ...), custom_call_target="tpu_custom_call", output_to_operand_aliasing={{0}: (10, {}), {1}: (11, {}), {2}: (12, {})} | custom-call | flops 4026531 | bytes 73400 | tf_op jit(solution)/shard_map/pallas_call | solution.py:59
  62.6 0.7 %collective-permute-done.18 = f32[4,64,128]{2,1,0:T(8,128)S(1)} collective-permute-done((f32[4,64,128]{2,1,0:T(8,128)S(1)}, f32[4,64,128]{2,1,0:T(8,128)S(1)}, u32[]{:S(2)}, u32[]{:S(2)}) %collective-permute-start.18) | collective-permute-done | bytes 131104 | tf_op jit(solution)/shard_map/ppermute | solution.py:417
  63.4 2.5 %collective-permute-start.23 = (f32[64,128]{1,0:T(8,128)S(1)}, f32[64,128]{1,0:T(8,128)S(1)}, u32[]{:S(2)}, u32[]{:S(2)}) collective-permute-start(f32[64,128]{1,0:T(8,128)S(1)} %get-tuple-element.95), channel_id=1, source_target_pairs={{0,12},{1,13},{2,14},{3,15},{4,8},{5,9},{6,10},{7,11},{8,4},{9,5},... | collective-permute-start | bytes 98312 | tf_op jit(solution)/shard_map/ppermute | solution.py:432
  65.9 1.9 %collective-permute-start.21 = (f32[64,128]{1,0:T(8,128)S(1)}, f32[64,128]{1,0:T(8,128)S(1)}, u32[]{:S(2)}, u32[]{:S(2)}) collective-permute-start(f32[64,128]{1,0:T(8,128)S(1)} %get-tuple-element.94), channel_id=1, source_target_pairs={{0,4},{1,5},{2,6},{3,7},{4,0},{5,1},{6,2},{7,3},{8,12},{9,13},{10,... | collective-permute-start | bytes 98312 | tf_op jit(solution)/shard_map/ppermute | solution.py:432
  67.8 1.3 %collective-permute-done.23 = f32[64,128]{1,0:T(8,128)S(1)} collective-permute-done((f32[64,128]{1,0:T(8,128)S(1)}, f32[64,128]{1,0:T(8,128)S(1)}, u32[]{:S(2)}, u32[]{:S(2)}) %collective-permute-start.23) | collective-permute-done | bytes 32800 | tf_op jit(solution)/shard_map/ppermute | solution.py:432
  69.1 1.6 %collective-permute-done.22 = f32[64,128]{1,0:T(8,128)S(1)} collective-permute-done((f32[64,128]{1,0:T(8,128)S(1)}, f32[64,128]{1,0:T(8,128)S(1)}, u32[]{:S(2)}, u32[]{:S(2)}) %collective-permute-start.22) | collective-permute-done | bytes 32800 | tf_op jit(solution)/shard_map/ppermute | solution.py:432
  70.7 0.6 fusion.14
  (64 shorter events, 3.9 us)
Async XLA Ops:
  3.6 2.1 %collective-permute-start = (f32[2,2,2,128,128]{4,3,2,1,0:T(8,128)S(1)}, f32[2,2,2,128,128]{4,3,2,1,0:T(8,128)S(1)}, u32[]{:S(2)}, u32[]{:S(2)}) collective-permute-start(f32[2,2,2,128,128]{4,3,2,1,0:T(8,128)S(1)} %get-tuple-element.41), channel_id=1, source_target_pairs={{0,1},{1,0},{2,3},{3,2},{4,5},{5,4},{6,7},{7,6},{8,9},{9,8},{10,11... | collective-permute-start | bytes 1572872 | tf_op jit(solution)/shard_map/ppermute | solution.py:369
  5.7 9.6 %collective-permute-start.3 = (f32[2,2,128,128]{3,2,1,0:T(8,128)S(1)}, f32[2,2,128,128]{3,2,1,0:T(8,128)S(1)}, u32[]{:S(2)}, u32[]{:S(2)}) collective-permute-start(f32[2,2,128,128]{3,2,1,0:T(8,128)S(1)} %fusion.3), channel_id=1, source_target_pairs={{0,2},{1,3},{2,0},{3,1},{4,6},{5,7},{6,4},{7,5},{8,10},{9,11},{10,... | collective-permute-start | bytes 786440 | tf_op jit(solution)/shard_map/ppermute | solution.py:373
  11.6 3.8 %collective-permute-start.1 = (f32[2,2,2,128,128]{4,3,2,1,0:T(8,128)S(1)}, f32[2,2,2,128,128]{4,3,2,1,0:T(8,128)S(1)}, u32[]{:S(2)}, u32[]{:S(2)}) collective-permute-start(f32[2,2,2,128,128]{4,3,2,1,0:T(8,128)S(1)} %get-tuple-element.44), channel_id=1, source_target_pairs={{0,1},{1,0},{2,3},{3,2},{4,5},{5,4},{6,7},{7,6},{8,9},{9,8},{10,11... | collective-permute-start | bytes 1572872 | tf_op jit(solution)/shard_map/ppermute | solution.py:369
  11.8 3.6 %copy-start.5 = (f32[2,2,2,128,128]{4,3,2,1,0:T(8,128)S(1)}, f32[2,2,2,128,128]{4,3,2,1,0:T(8,128)}, u32[]{:S(2)}) copy-start(f32[2,2,2,128,128]{4,3,2,1,0:T(8,128)} %get-tuple-element.46) | copy-start | bytes 1572868
  15.5 6.8 %collective-permute-start.4 = (f32[2,128,128]{2,1,0:T(8,128)S(1)}, f32[2,128,128]{2,1,0:T(8,128)S(1)}, u32[]{:S(2)}, u32[]{:S(2)}) collective-permute-start(f32[2,128,128]{2,1,0:T(8,128)S(1)} %select_bitcast_fusion.4), channel_id=1, source_target_pairs={{0,4},{1,5},{2,6},{3,7},{4,0},{5,1},{6,2},{7,3},{8,12},{9,13},{10,... | collective-permute-start | bytes 393224 | tf_op jit(solution)/shard_map/ppermute | solution.py:383
  17.3 8.2 %collective-permute-start.2 = (f32[2,2,128,128]{3,2,1,0:T(8,128)S(1)}, f32[2,2,128,128]{3,2,1,0:T(8,128)S(1)}, u32[]{:S(2)}, u32[]{:S(2)}) collective-permute-start(f32[2,2,128,128]{3,2,1,0:T(8,128)S(1)} %fusion.1), channel_id=1, source_target_pairs={{0,2},{1,3},{2,0},{3,1},{4,6},{5,7},{6,4},{7,5},{8,10},{9,11},{10,... | collective-permute-start | bytes 786440 | tf_op jit(solution)/shard_map/ppermute | solution.py:373
  22.3 3.3 %copy-start.4 = (f32[2,2,2,128,128]{4,3,2,1,0:T(8,128)S(1)}, f32[2,2,2,128,128]{4,3,2,1,0:T(8,128)}, u32[]{:S(2)}) copy-start(f32[2,2,2,128,128]{4,3,2,1,0:T(8,128)} %get-tuple-element.43) | copy-start | bytes 1572868
  22.3 3.8 %collective-permute-start.6 = (f32[2,128,128]{2,1,0:T(8,128)S(1)}, f32[2,128,128]{2,1,0:T(8,128)S(1)}, u32[]{:S(2)}, u32[]{:S(2)}) collective-permute-start(f32[2,128,128]{2,1,0:T(8,128)S(1)} %bitcast_add_fusion.1), channel_id=1, source_target_pairs={{0,1},{1,0},{2,3},{3,2},{4,8},{5,9},{6,10},{7,11},{8,4},{9,5},{10,... | collective-permute-start | bytes 393224 | tf_op jit(solution)/shard_map/ppermute | solution.py:383
  25.6 6.1 %collective-permute-start.5 = (f32[2,128,128]{2,1,0:T(8,128)S(1)}, f32[2,128,128]{2,1,0:T(8,128)S(1)}, u32[]{:S(2)}, u32[]{:S(2)}) collective-permute-start(f32[2,128,128]{2,1,0:T(8,128)S(1)} %select_bitcast_fusion.5), channel_id=1, source_target_pairs={{0,4},{1,5},{2,6},{3,7},{4,0},{5,1},{6,2},{7,3},{8,12},{9,13},{10,... | collective-permute-start | bytes 393224 | tf_op jit(solution)/shard_map/ppermute | solution.py:383
  26.1 6.9 %collective-permute-start.8 = (f32[2,128,128]{2,1,0:T(8,128)S(1)}, f32[2,128,128]{2,1,0:T(8,128)S(1)}, u32[]{:S(2)}, u32[]{:S(2)}) collective-permute-start(f32[2,128,128]{2,1,0:T(8,128)S(1)} %bitcast_add_fusion), channel_id=1, source_target_pairs={{0,4},{1,5},{2,6},{3,7},{4,0},{5,1},{6,2},{7,3},{8,12},{9,13},{10,... | collective-permute-start | bytes 393224 | tf_op jit(solution)/shard_map/ppermute | solution.py:383
  31.7 2.4 %collective-permute-start.7 = (f32[2,128,128]{2,1,0:T(8,128)S(1)}, f32[2,128,128]{2,1,0:T(8,128)S(1)}, u32[]{:S(2)}, u32[]{:S(2)}) collective-permute-start(f32[2,128,128]{2,1,0:T(8,128)S(1)} %bitcast_add_fusion.2), channel_id=1, source_target_pairs={{0,1},{1,0},{2,3},{3,2},{4,8},{5,9},{6,10},{7,11},{8,4},{9,5},{10,... | collective-permute-start | bytes 393224 | tf_op jit(solution)/shard_map/ppermute | solution.py:383
  33.2 7.5 %collective-permute-start.10 = (f32[2,2,128,128]{3,2,1,0:T(8,128)S(1)}, f32[2,2,128,128]{3,2,1,0:T(8,128)S(1)}, u32[]{:S(2)}, u32[]{:S(2)}) collective-permute-start(f32[2,2,128,128]{3,2,1,0:T(8,128)S(1)} %get-tuple-element.80), channel_id=1, source_target_pairs={{0,2},{1,3},{2,0},{3,1},{4,6},{5,7},{6,4},{7,5},{8,10},{9,11},{10,... | collective-permute-start | bytes 786440 | tf_op jit(solution)/shard_map/ppermute | solution.py:373
  34.0 8.1 %collective-permute-start.13 = (f32[2,2,128,128]{3,2,1,0:T(8,128)S(1)}, f32[2,2,128,128]{3,2,1,0:T(8,128)S(1)}, u32[]{:S(2)}, u32[]{:S(2)}) collective-permute-start(f32[2,2,128,128]{3,2,1,0:T(8,128)S(1)} %get-tuple-element.76), channel_id=1, source_target_pairs={{0,1},{1,0},{2,3},{3,2},{4,5},{5,4},{6,7},{7,6},{8,9},{9,8},{10,11... | collective-permute-start | bytes 786440 | tf_op jit(solution)/shard_map/ppermute | solution.py:369
  34.1 6.8 %collective-permute-start.9 = (f32[2,128,128]{2,1,0:T(8,128)S(1)}, f32[2,128,128]{2,1,0:T(8,128)S(1)}, u32[]{:S(2)}, u32[]{:S(2)}) collective-permute-start(f32[2,128,128]{2,1,0:T(8,128)S(1)} %bitcast_add_fusion.3), channel_id=1, source_target_pairs={{0,4},{1,5},{2,6},{3,7},{4,0},{5,1},{6,2},{7,3},{8,12},{9,13},{10,... | collective-permute-start | bytes 393224 | tf_op jit(solution)/shard_map/ppermute | solution.py:383
  40.8 1.6 %collective-permute-start.14 = (f32[2,2,128,128]{3,2,1,0:T(8,128)S(1)}, f32[2,2,128,128]{3,2,1,0:T(8,128)S(1)}, u32[]{:S(2)}, u32[]{:S(2)}) collective-permute-start(f32[2,2,128,128]{3,2,1,0:T(8,128)S(1)} %fusion.5), channel_id=1, source_target_pairs={{0,1},{1,0},{2,3},{3,2},{4,5},{5,4},{6,7},{7,6},{8,9},{9,8},{10,11... | collective-permute-start | bytes 786440 | tf_op jit(solution)/shard_map/ppermute | solution.py:369
  40.9 1.5 %copy-start.2 = (f32[8,128,128]{2,1,0:T(8,128)S(1)}, f32[8,128,128]{2,1,0:T(8,128)}, u32[]{:S(2)}) copy-start(f32[8,128,128]{2,1,0:T(8,128)} %get-tuple-element.53.refs_5_) | copy-start | bytes 1572868
  40.9 1.5 %copy-start.3 = (bf16[2,8,128,128]{3,2,1,0:T(8,128)(2,1)S(1)}, bf16[2,8,128,128]{3,2,1,0:T(8,128)(2,1)}, u32[]{:S(2)}) copy-start(bf16[2,8,128,128]{3,2,1,0:T(8,128)(2,1)} %get-tuple-element.54.refs_6_) | copy-start | bytes 1572868
  41.1 8.8 %collective-permute-start.11 = (f32[2,2,128,128]{3,2,1,0:T(8,128)S(1)}, f32[2,2,128,128]{3,2,1,0:T(8,128)S(1)}, u32[]{:S(2)}, u32[]{:S(2)}) collective-permute-start(f32[2,2,128,128]{3,2,1,0:T(8,128)S(1)} %get-tuple-element.81), channel_id=1, source_target_pairs={{0,2},{1,3},{2,0},{3,1},{4,6},{5,7},{6,4},{7,5},{8,10},{9,11},{10,... | collective-permute-start | bytes 786440 | tf_op jit(solution)/shard_map/ppermute | solution.py:373
  41.9 7.9 %collective-permute-start.12 = (f32[2,2,128,128]{3,2,1,0:T(8,128)S(1)}, f32[2,2,128,128]{3,2,1,0:T(8,128)S(1)}, u32[]{:S(2)}, u32[]{:S(2)}) collective-permute-start(f32[2,2,128,128]{3,2,1,0:T(8,128)S(1)} %get-tuple-element.78), channel_id=1, source_target_pairs={{0,1},{1,0},{2,3},{3,2},{4,5},{5,4},{6,7},{7,6},{8,9},{9,8},{10,11... | collective-permute-start | bytes 786440 | tf_op jit(solution)/shard_map/ppermute | solution.py:369
  43.1 6.9 %collective-permute-start.16 = (f32[8,64,128]{2,1,0:T(8,128)S(1)}, f32[8,64,128]{2,1,0:T(8,128)S(1)}, u32[]{:S(2)}, u32[]{:S(2)}) collective-permute-start(f32[8,64,128]{2,1,0:T(8,128)S(1)} %get-tuple-element.61), channel_id=1, source_target_pairs={{0,1},{1,0},{2,3},{3,2},{4,5},{5,4},{6,7},{7,6},{8,9},{9,8},{10,11... | collective-permute-start | bytes 786440 | tf_op jit(solution)/shard_map/ppermute | solution.py:369
  49.9 1.7 %copy-start.1 = (bf16[2,8,128,128]{3,2,1,0:T(8,128)(2,1)S(1)}, bf16[2,8,128,128]{3,2,1,0:T(8,128)(2,1)}, u32[]{:S(2)}) copy-start(bf16[2,8,128,128]{3,2,1,0:T(8,128)(2,1)} %get-tuple-element.49.refs_6_) | copy-start | bytes 1572868
  50.0 1.6 %copy-start = (f32[8,128,128]{2,1,0:T(8,128)S(1)}, f32[8,128,128]{2,1,0:T(8,128)}, u32[]{:S(2)}) copy-start(f32[8,128,128]{2,1,0:T(8,128)} %get-tuple-element.48.refs_5_) | copy-start | bytes 1572868
  50.0 1.6 %collective-permute-start.15 = (f32[2,2,128,128]{3,2,1,0:T(8,128)S(1)}, f32[2,2,128,128]{3,2,1,0:T(8,128)S(1)}, u32[]{:S(2)}, u32[]{:S(2)}) collective-permute-start(f32[2,2,128,128]{3,2,1,0:T(8,128)S(1)} %fusion.4), channel_id=1, source_target_pairs={{0,1},{1,0},{2,3},{3,2},{4,5},{5,4},{6,7},{7,6},{8,9},{9,8},{10,11... | collective-permute-start | bytes 786440 | tf_op jit(solution)/shard_map/ppermute | solution.py:369
  52.3 1.6 %collective-permute-start.17 = (f32[8,64,128]{2,1,0:T(8,128)S(1)}, f32[8,64,128]{2,1,0:T(8,128)S(1)}, u32[]{:S(2)}, u32[]{:S(2)}) collective-permute-start(f32[8,64,128]{2,1,0:T(8,128)S(1)} %get-tuple-element.69), channel_id=1, source_target_pairs={{0,1},{1,0},{2,3},{3,2},{4,5},{5,4},{6,7},{7,6},{8,9},{9,8},{10,11... | collective-permute-start | bytes 786440 | tf_op jit(solution)/shard_map/ppermute | solution.py:369
  54.0 8.0 %collective-permute-start.20 = (f32[4,64,128]{2,1,0:T(8,128)S(1)}, f32[4,64,128]{2,1,0:T(8,128)S(1)}, u32[]{:S(2)}, u32[]{:S(2)}) collective-permute-start(f32[4,64,128]{2,1,0:T(8,128)S(1)} %pad_maximum_fusion.4), channel_id=1, source_target_pairs={{0,18},{1,19},{2,16},{3,17},{4,22},{5,23},{6,20},{7,21},{8,26},{9,... | collective-permute-start | bytes 393224 | tf_op jit(solution)/shard_map/ppermute | solution.py:417
  55.7 6.8 %collective-permute-start.19 = (f32[4,64,128]{2,1,0:T(8,128)S(1)}, f32[4,64,128]{2,1,0:T(8,128)S(1)}, u32[]{:S(2)}, u32[]{:S(2)}) collective-permute-start(f32[4,64,128]{2,1,0:T(8,128)S(1)} %pad_maximum_fusion.3), channel_id=1, source_target_pairs={{0,16},{1,17},{2,18},{3,19},{4,20},{5,21},{6,22},{7,23},{8,24},{9,... | collective-permute-start | bytes 393224 | tf_op jit(solution)/shard_map/ppermute | solution.py:417
  56.4 7.0 %collective-permute-start.18 = (f32[4,64,128]{2,1,0:T(8,128)S(1)}, f32[4,64,128]{2,1,0:T(8,128)S(1)}, u32[]{:S(2)}, u32[]{:S(2)}) collective-permute-start(f32[4,64,128]{2,1,0:T(8,128)S(1)} %pad_maximum_fusion.2), channel_id=1, source_target_pairs={{0,2},{1,3},{2,0},{3,1},{4,6},{5,7},{6,4},{7,5},{8,10},{9,11},{10,... | collective-permute-start | bytes 393224 | tf_op jit(solution)/shard_map/ppermute | solution.py:417
  63.4 5.8 %collective-permute-start.23 = (f32[64,128]{1,0:T(8,128)S(1)}, f32[64,128]{1,0:T(8,128)S(1)}, u32[]{:S(2)}, u32[]{:S(2)}) collective-permute-start(f32[64,128]{1,0:T(8,128)S(1)} %get-tuple-element.95), channel_id=1, source_target_pairs={{0,12},{1,13},{2,14},{3,15},{4,8},{5,9},{6,10},{7,11},{8,4},{9,5},... | collective-permute-start | bytes 98312 | tf_op jit(solution)/shard_map/ppermute | solution.py:432
  65.9 4.8 %collective-permute-start.22 = (f32[64,128]{1,0:T(8,128)S(1)}, f32[64,128]{1,0:T(8,128)S(1)}, u32[]{:S(2)}, u32[]{:S(2)}) collective-permute-start(f32[64,128]{1,0:T(8,128)S(1)} %get-tuple-element.96), channel_id=1, source_target_pairs={{0,8},{1,9},{2,10},{3,11},{4,12},{5,13},{6,14},{7,15},{8,0},{9,1},... | collective-permute-start | bytes 98312 | tf_op jit(solution)/shard_map/ppermute | solution.py:432
  65.9 4.8 %collective-permute-start.21 = (f32[64,128]{1,0:T(8,128)S(1)}, f32[64,128]{1,0:T(8,128)S(1)}, u32[]{:S(2)}, u32[]{:S(2)}) collective-permute-start(f32[64,128]{1,0:T(8,128)S(1)} %get-tuple-element.94), channel_id=1, source_target_pairs={{0,4},{1,5},{2,6},{3,7},{4,0},{5,1},{6,2},{7,3},{8,12},{9,13},{10,... | collective-permute-start | bytes 98312 | tf_op jit(solution)/shard_map/ppermute | solution.py:432
